TPU v7x, 32 devices: a whole 2x2x4 slice. The times are simulated.
32 devices in a mesh: grp: 2 (over core), seg: 16 (over z, y, x).
Axes of the slice: x: 2, y: 2, z: 4, core: 2. Of those that a mesh axis runs over, the one named last changes fastest.
Arguments:
- frames_in: bfloat16 [2048, 20, 512], P(('grp', 'seg')), may hold values from -6 to 6
- memory: bfloat16 [2048, 512], P(('grp', 'seg')), may hold values from -6 to 6
- counts: int32 [2, 48], P('grp'), may hold values from 1 to 32, 1024 in all within a row
- query_weight: bfloat16 [512, 512], replicated, may hold values from -0.25 to 0.25
- key_weight: bfloat16 [512, 512], replicated, may hold values from -0.25 to 0.25
- value_weight: bfloat16 [512, 512], replicated, may hold values from -0.25 to 0.25
- out_weight: bfloat16 [512, 512], replicated, may hold values from -1 to 1
- up_weight: bfloat16 [512, 2048], replicated, may hold values from -0.25 to 0.25
- down_weight: bfloat16 [2048, 512], replicated, may hold values from -0.125 to 0.125
- input_gain: float32 [512], replicated, may hold values from 0.1 to 1.9
- middle_gain: float32 [512], replicated, may hold values from 0.1 to 1.9
- output_gain: float32 [512], replicated, may hold values from 0.1 to 1.9
- out_grad: bfloat16 [2048, 20, 512], P(('grp', 'seg')), may hold values from -6 to 6
- memory_grad: bfloat16 [2048, 512], P(('grp', 'seg')), may hold values from -6 to 6
Outputs:
- result_frames: bfloat16 [2048, 20, 512], P(('grp', 'seg'))
- memory_out: bfloat16 [2048, 512], P(('grp', 'seg'))
- grad_frames: float32 [2048, 20, 512], P(('grp', 'seg'))
- grad_memory: bfloat16 [2048, 512], P(('grp', 'seg'))
- grad_query: float32 [512, 512], replicated
- grad_key: float32 [512, 512], replicated
- grad_value: float32 [512, 512], replicated
- grad_out: float32 [512, 512], replicated
- grad_up: float32 [512, 2048], replicated
- grad_down: float32 [2048, 512], replicated
- grad_input_gain: float32 [512], replicated
- grad_middle_gain: float32 [512], replicated
- grad_output_gain: float32 [512], replicated
Inputs may be any that keep to these rules, and one draw needn't show every extreme that they name: In each group the 48 counts sum to 1024, and the largest is exactly 32.
All inputs are finite; a program needn't handle non-finite values.
Results may differ from a plain program's by a relative error of at most 0.015.
Values may be sent and summed in bfloat16 or wider, within the bound.
No kernel may reach another device: no remote copies, remote signals or barrier semaphores. Data moves between devices by JAX's collectives and lax.ppermute only.
A program may use at most 320 MiB of HBM per device.

v0:
```python
import jax
import jax.numpy as jnp
from jax import lax
from jax.sharding import PartitionSpec as P

HEADS = 8
HDIM = 64
SEGLEN = 16
RIGHT = 4
LEFT = 30
MEMS = 4


EPSILON = 1e-05
MASKED_SCORE = -1e30


def from_behind(x, axis, by):
    size = lax.axis_size(axis)
    return lax.ppermute(x, axis, [(i, (i + by) % size) for i in range(size)])


def norm_rows(values, norm_gain):
    centered = values - jnp.mean(values, axis=-1, keepdims=True)
    spread = jnp.mean(centered * centered, axis=-1, keepdims=True)
    return centered * lax.rsqrt(spread + EPSILON) * norm_gain


def norm_pull(values, norm_gain, gradient):
    _, pullback = jax.vjp(norm_rows, values, norm_gain)
    return pullback(gradient)


def gelu_exact(values):
    return jax.nn.gelu(values, approximate=False)


def project(operand, weight):
    return jnp.einsum("...i,ij->...j", operand, weight, preferred_element_type=jnp.float32)


def project_back(gradient, weight):
    return jnp.einsum("...j,ij->...i", gradient, weight, preferred_element_type=jnp.float32)


def outer_sum(operand, gradient):
    return jnp.einsum("nri,nrj->ij", operand, gradient, preferred_element_type=jnp.float32)


def key_mask(position):
    columns = jnp.arange(MEMS + LEFT + SEGLEN + RIGHT, dtype=jnp.int32)
    needed = jnp.where(
        columns < MEMS,
        MEMS - columns,
        jnp.where(columns < MEMS + LEFT - SEGLEN, 2, jnp.where(columns < MEMS + LEFT, 1, 0)),
    )
    queries = jnp.arange(SEGLEN + RIGHT + 1, dtype=jnp.int32)
    summary_row = (queries[:, None] == SEGLEN + RIGHT) & (columns[None, :] < MEMS)
    return (position[:, None, None] >= needed[None, None, :]) & jnp.logical_not(summary_row)[None]


def segment_position(counts_row, segment):
    starts = jnp.cumsum(counts_row, dtype=jnp.int32) - counts_row
    first_segment = jnp.max(
        jnp.where(starts[None, :] <= segment[:, None], starts[None, :], 0), axis=1
    )
    return segment - first_segment


def slot_of(segment, slot_count, devices, capacity):
    return segment // slot_count * capacity + segment % slot_count // devices


def per_device(
    frames_in,
    memory,
    counts,
    query_weight,
    key_weight,
    value_weight,
    out_weight,
    up_weight,
    down_weight,
    input_gain,
    middle_gain,
    output_gain,
    out_grad,
    memory_grad,
):
    devices = lax.axis_size("seg")
    holder = lax.axis_index("seg")
    slot_count = frames_in.shape[0]
    frame_count = frames_in.shape[1]
    model_width = frames_in.shape[2]
    capacity = max(1, slot_count // devices)
    slot_total = devices * capacity
    group_total = devices * slot_count
    frames_wide = frames_in.astype(jnp.float32)
    normed = norm_rows(frames_wide, input_gain)
    summary = jnp.mean(normed[:, RIGHT:], axis=1)
    payload = jnp.concatenate(
        [normed, summary[:, None], memory.astype(jnp.float32)[:, None]], axis=1
    ).astype(jnp.bfloat16)
    pair_weight = jnp.concatenate([key_weight, value_weight], axis=1)
    slot_number = jnp.arange(slot_total, dtype=jnp.int32)
    partner = slot_number // capacity
    within = slot_number % capacity
    outgoing_slot = (partner - holder * slot_count) % devices + within * devices
    outgoing_live = outgoing_slot < slot_count
    outgoing_index = jnp.minimum(outgoing_slot, slot_count - 1)
    incoming_slot = (holder - partner * slot_count) % devices + within * devices
    segment = jnp.clip(partner * slot_count + incoming_slot, 0, group_total - 1)
    own_number = jnp.arange(slot_count, dtype=jnp.int32)
    home_slot = (holder * slot_count + own_number) % devices * capacity + own_number // devices

    def send_out(values):
        picked = jnp.take(values, outgoing_index, axis=0)
        return jnp.where(outgoing_live[:, None, None], picked, jnp.zeros_like(picked))

    def earlier_take(values, offset):
        return jnp.take(
            values,
            slot_of(jnp.clip(segment - offset, 0, group_total - 1), slot_count, devices, capacity),
            axis=0,
        )

    def later_take(values, offset):
        picked = jnp.take(
            values,
            slot_of(jnp.clip(segment + offset, 0, group_total - 1), slot_count, devices, capacity),
            axis=0,
        )
        inside = (segment + offset < group_total).reshape((-1,) + (1,) * (picked.ndim - 1))
        return jnp.where(inside, picked, jnp.zeros_like(picked))

    arrived = lax.all_to_all(send_out(payload), "seg", split_axis=0, concat_axis=0, tiled=True)
    position = segment_position(counts[0], segment)
    rows = arrived.shape[0]
    query_rows = arrived[:, : frame_count + 1]
    key_rows = jnp.concatenate([arrived[:, :frame_count], arrived[:, frame_count + 1 :]], axis=1)
    queries = (project(query_rows, query_weight) * 0.125).astype(jnp.bfloat16)
    key_value = project(key_rows, pair_weight).astype(jnp.bfloat16)
    recent = key_value[:, RIGHT:]
    by_offset = {}
    recent_taken = []
    for offset in (1, 2):
        shifted = from_behind(recent, "seg", offset)
        taken = earlier_take(shifted, offset)
        recent_taken.append(taken)
        by_offset[offset] = taken[:, SEGLEN]
    for offset in range(3, MEMS + 1):
        shifted = from_behind(key_value[:, frame_count], "seg", offset)
        by_offset[offset] = earlier_take(shifted, offset)
    memory_keys = jnp.stack([by_offset[MEMS - column] for column in range(MEMS)], axis=1)
    all_keys = jnp.concatenate(
        [
            memory_keys,
            recent_taken[1][:, 2 * SEGLEN - LEFT : SEGLEN],
            recent_taken[0][:, :SEGLEN],
            key_value[:, RIGHT:frame_count],
            key_value[:, :RIGHT],
        ],
        axis=1,
    )
    key_count = all_keys.shape[1]
    query_heads = queries.reshape(rows, frame_count + 1, HEADS, HDIM)
    key_heads = all_keys[..., :model_width].reshape(rows, key_count, HEADS, HDIM)
    value_heads = all_keys[..., model_width:].reshape(rows, key_count, HEADS, HDIM)
    scores = jnp.einsum(
        "nqhe,nkhe->nhqk", query_heads, key_heads, preferred_element_type=jnp.float32
    )
    allowed = key_mask(position)[:, None]
    scores = jnp.where(allowed, scores, MASKED_SCORE)
    soft_scores = jax.nn.softmax(scores, axis=-1)
    soft_low = soft_scores.astype(jnp.bfloat16)
    attended = jnp.einsum(
        "nhqk,nkhe->nqhe", soft_low, value_heads, preferred_element_type=jnp.float32
    )
    attended = attended.reshape(rows, frame_count + 1, model_width).astype(jnp.bfloat16)
    returned = lax.all_to_all(attended, "seg", split_axis=0, concat_axis=0, tiled=True)
    attended_home = jnp.take(returned, home_slot, axis=0)
    branch = project(attended_home, out_weight)
    residual = frames_wide + branch[:, :frame_count]
    memory_out = branch[:, frame_count].astype(jnp.bfloat16)
    middle = norm_rows(residual, middle_gain).astype(jnp.bfloat16)
    lifted = project(middle, up_weight)
    hidden = gelu_exact(lifted).astype(jnp.bfloat16)
    combined = residual + project(hidden, down_weight)
    result_frames = norm_rows(combined, output_gain).astype(jnp.bfloat16)
    grad_combined, grad_output_gain = norm_pull(combined, output_gain, out_grad.astype(jnp.float32))
    grad_ff = grad_combined.astype(jnp.bfloat16)
    grad_down = outer_sum(hidden, grad_ff)
    grad_hidden = project_back(grad_ff, down_weight)
    _, gelu_pull = jax.vjp(gelu_exact, lifted)
    grad_lifted = gelu_pull(grad_hidden)[0].astype(jnp.bfloat16)
    grad_up = outer_sum(middle, grad_lifted)
    grad_middle = project_back(grad_lifted, up_weight)
    grad_residual_norm, grad_middle_gain = norm_pull(residual, middle_gain, grad_middle)
    grad_residual = grad_combined + grad_residual_norm
    grad_branch = jnp.concatenate(
        [grad_residual, memory_grad.astype(jnp.float32)[:, None]], axis=1
    ).astype(jnp.bfloat16)
    grad_out = outer_sum(attended_home, grad_branch)
    grad_attended = project_back(grad_branch, out_weight).astype(jnp.bfloat16)
    grad_mixed = lax.all_to_all(
        send_out(grad_attended), "seg", split_axis=0, concat_axis=0, tiled=True
    )
    grad_heads = grad_mixed.reshape(rows, frame_count + 1, HEADS, HDIM)
    grad_soft = jnp.einsum(
        "nqhe,nkhe->nhqk", grad_heads, value_heads, preferred_element_type=jnp.float32
    )
    grad_values = jnp.einsum(
        "nhqk,nqhe->nkhe", soft_low, grad_heads, preferred_element_type=jnp.float32
    )
    grad_scores = (
        soft_scores * (grad_soft - jnp.sum(grad_soft * soft_scores, axis=-1, keepdims=True))
    ).astype(jnp.bfloat16)
    grad_queries = jnp.einsum(
        "nhqk,nkhe->nqhe", grad_scores, key_heads, preferred_element_type=jnp.float32
    )
    grad_queries = grad_queries.reshape(rows, frame_count + 1, model_width).astype(jnp.bfloat16)
    grad_keys = jnp.einsum(
        "nhqk,nqhe->nkhe", grad_scores, query_heads, preferred_element_type=jnp.float32
    )
    grad_pairs = jnp.concatenate(
        [
            grad_keys.reshape(rows, key_count, model_width),
            grad_values.reshape(rows, key_count, model_width),
        ],
        axis=-1,
    )
    split_one = MEMS + LEFT - SEGLEN
    split_own = MEMS + LEFT
    split_right = MEMS + LEFT + SEGLEN
    first_back = jnp.concatenate(
        [grad_pairs[:, split_one:split_own], grad_pairs[:, MEMS - 1 : MEMS]], axis=1
    )
    second_back = jnp.concatenate(
        [
            jnp.zeros((rows, 2 * SEGLEN - LEFT, 2 * model_width), jnp.float32),
            grad_pairs[:, MEMS:split_one],
            grad_pairs[:, MEMS - 2 : MEMS - 1],
        ],
        axis=1,
    )
    center_sum = grad_pairs[:, split_own:split_right]
    memory_sum = jnp.zeros((rows, 2 * model_width), jnp.float32)
    for offset, outgoing in ((1, first_back), (2, second_back)):
        returned_keys = from_behind(outgoing.astype(jnp.bfloat16), "seg", -offset).astype(
            outgoing.dtype
        )
        taken = later_take(returned_keys, offset)
        center_sum = center_sum + taken[:, :SEGLEN]
        memory_sum = memory_sum + taken[:, SEGLEN]
    for offset in range(3, MEMS + 1):
        returned_keys = from_behind(
            grad_pairs[:, MEMS - offset].astype(jnp.bfloat16), "seg", -offset
        ).astype(jnp.float32)
        memory_sum = memory_sum + later_take(returned_keys, offset)
    grad_pair = jnp.concatenate(
        [grad_pairs[:, split_right:], center_sum, memory_sum[:, None]], axis=1
    ).astype(jnp.bfloat16)
    grad_query = outer_sum(query_rows, grad_queries) * 0.125
    grad_key = outer_sum(key_rows, grad_pair[..., :model_width])
    grad_value = outer_sum(key_rows, grad_pair[..., model_width:])
    query_back = project_back(grad_queries, query_weight) * 0.125
    key_back = project_back(grad_pair, pair_weight)
    sent_home = jnp.concatenate(
        [
            query_back[:, :frame_count] + key_back[:, :frame_count],
            query_back[:, frame_count:],
            key_back[:, frame_count:],
        ],
        axis=1,
    ).astype(jnp.bfloat16)
    grad_payload = lax.all_to_all(sent_home, "seg", split_axis=0, concat_axis=0, tiled=True)
    grad_local = jnp.take(grad_payload, home_slot, axis=0)
    center_rows = (jnp.arange(frame_count) >= RIGHT)[None, :, None]
    grad_normed = grad_local[:, :frame_count].astype(jnp.float32)
    grad_normed = grad_normed + jnp.where(
        center_rows, grad_local[:, frame_count : frame_count + 1].astype(jnp.float32) / SEGLEN, 0.0
    )
    grad_frames_norm, grad_input_gain = norm_pull(frames_wide, input_gain, grad_normed)
    grad_frames = grad_residual + grad_frames_norm
    grad_memory = grad_local[:, frame_count + 1]
    summed = tuple(
        lax.psum(
            (
                grad_query,
                grad_key,
                grad_value,
                grad_input_gain,
                grad_up,
                grad_down,
                grad_out,
                grad_middle_gain,
                grad_output_gain,
            ),
            ("grp", "seg"),
        )
    )
    return (
        result_frames,
        memory_out,
        grad_frames,
        grad_memory,
        summed[0],
        summed[1],
        summed[2],
        summed[6],
        summed[4],
        summed[5],
        summed[3],
        summed[7],
        summed[8],
    )


def solution(mesh):
    return jax.shard_map(
        per_device,
        mesh=mesh,
        in_specs=(
            P(("grp", "seg"), None, None),
            P(("grp", "seg"), None),
            P("grp", None),
            P(),
            P(),
            P(),
            P(),
            P(),
            P(),
            P(),
            P(),
            P(),
            P(("grp", "seg"), None, None),
            P(("grp", "seg"), None),
        ),
        out_specs=(
            P(("grp", "seg"), None, None),
            P(("grp", "seg"), None),
            P(("grp", "seg"), None, None),
            P(("grp", "seg"), None),
            P(),
            P(),
            P(),
            P(),
            P(),
            P(),
            P(),
            P(),
            P(),
        ),
        check_vma=False,
    )
```

profile of v0, /device:TPU:0, one launch (start us, length us, event | category | flops | bytes accessed | tf_op | source)
XLA Modules:
  0.0 1033.8 jit_solution(722573117891519534)
XLA Ops:
  20.6 8.4 all-to-all-start
  31.7 31.5 %all-to-all-done = bf16[64,22,512]{2,1,0:T(8,128)(2,1)} async-done(((bf16[64,22,512]{2,1,0:T(8,128)(2,1)}), bf16[64,22,512]{2,1,0:T(8,128)(2,1)}, u32[]{:S(2)}, u32[]{:S(2)}) %all-to-all-start) | async-done | bytes 1441824 | tf_op jit(solution)/shard_map/all_to_all | solution.py:136
  89.5 30.0 %collective-permute-done.1 = bf16[64,1024]{1,0:T(8,128)(2,1)} collective-permute-done((bf16[64,1024]{1,0:T(8,128)(2,1)}, bf16[64,1024]{1,0:T(8,128)(2,1)}, u32[]{:S(2)}, u32[]{:S(2)}) %collective-permute-start.1) | collective-permute-done | bytes 131104 | tf_op jit(solution)/shard_map/ppermute | solution.py:20
  126.7 40.5 %collective-permute-done.3 = bf16[64,17,1024]{2,0,1:T(8,128)(2,1)} collective-permute-done((bf16[64,17,1024]{2,0,1:T(8,128)(2,1)}, bf16[64,17,1024]{2,0,1:T(8,128)(2,1)}, u32[]{:S(2)}, u32[]{:S(2)}) %collective-permute-start.3) | collective-permute-done | bytes 2228256 | tf_op jit(solution)/shard_map/ppermute | solution.py:20
  210.2 9.7 reshape.386
  219.8 9.8 reshape.384
  229.6 9.7 fusion.13
  239.3 12.9 %fusion.115 = (f32[64,8,21]{2,1,0:T(8,128)S(1)}, f32[64,8,21,54]{3,2,1,0:T(8,128)S(1)}) fusion(f32[64,8,21,54]{3,2,1,0:T(8,128)S(1)} %fusion.13, pred[64,21,54]{2,1,0:T(8,128)(4,1)S(1)} %copy-done.37), kind=kOutput, calls=%fused_computation.354 | output fusion | flops 2322485 | bytes 4760448 | tf_op jit(solution)/shard_map/sub | solution.py:174
  252.2 11.0 %convert_bitcast_fusion.1 = bf16[64,21,8,64]{3,1,2,0:T(8,128)(2,1)S(1)} fusion(bf16[64,54,8,64]{3,2,0,1:T(8,128)(2,1)} %reshape.384, f32[64,8,21,54]{3,2,1,0:T(8,128)S(1)} %get-tuple-element.54, f32[64,8,21]{2,1,0:T(8,128)S(1)} %get-tuple-element.53), kind=kOutput, calls=%fused_computation.71 | convolution fusion | flops 76167168 | bytes 7280640 | tf_op jit(solution)/shard_map/nhqk,nkhe->nqhe/dot_general | solution.py:176
  270.0 59.4 %all-to-all-start.1 = ((bf16[64,21,512]{2,1,0:T(8,128)(2,1)}), bf16[64,21,512]{2,1,0:T(8,128)(2,1)}, u32[]{:S(2)}, u32[]{:S(2)}) async-start(bf16[64,21,512]{2,1,0:T(8,128)(2,1)} %reshape.533), calls=%async_computation.1 | async-start | bytes 3145728 | tf_op jit(solution)/shard_map/all_to_all | solution.py:180
  329.6 30.5 %all-to-all-done.1 = bf16[64,21,512]{2,1,0:T(8,128)(2,1)} async-done(((bf16[64,21,512]{2,1,0:T(8,128)(2,1)}), bf16[64,21,512]{2,1,0:T(8,128)(2,1)}, u32[]{:S(2)}, u32[]{:S(2)}) %all-to-all-start.1) | async-done | bytes 1376288 | tf_op jit(solution)/shard_map/all_to_all | solution.py:180
  373.0 24.7 %multiply_convert_fusion = (bf16[64,20,2048]{2,0,1:T(8,128)(2,1)S(1)}, f32[64,20,2048]{2,0,1:T(8,128)}) fusion(f32[64,20,2048]{2,0,1:T(8,128)S(1)} %get-tuple-element.55, u32[64,2048]{1,0:T(8,128)S(1)} %get-tuple-element.20, u32[64,2048]{1,0:T(8,128)S(1)} %get-tuple-element.19), kind=kLoop, calls=%fused_computation.21 | loop fusion | flops 178257920 | bytes 27262976 | tf_op jit(solution)/shard_map/convert_element_type | solution.py:187
  406.1 11.3 %add_convert_fusion = bf16[64,20,2048]{2,0,1:T(8,128)(2,1)S(1)} fusion(f32[64,20,2048]{2,0,1:T(8,128)} %get-tuple-element.41, f32[64,20,2048]{2,0,1:T(8,128)} %copy-done.16, bf16[2048,512]{1,0:T(8,128)(2,1)} %param.34, f32[64,20,512]{2,0,1:T(8,128)S(1)} %get-tuple-element.39, f32[64,20]{0,1:T(8,128)S(1)} %negate_multiply_fusion.3), kind=kOutput, calls=%fused_computation.20 | convolution fusion | flops 2722365440 | bytes 30938112 | tf_op jit(solution)/shard_map/...j,ij->...i/dot_general | solution.py:43
  441.8 7.6 convolution_bitcast_fusion.3
  449.4 21.3 %all-to-all-done.2 = bf16[64,21,512]{2,1,0:T(8,128)(2,1)S(1)} async-done(((bf16[64,21,512]{2,1,0:T(8,128)(2,1)}), bf16[64,21,512]{2,1,0:T(8,128)(2,1)S(1)}, u32[]{:S(2)}, u32[]{:S(2)}) %all-to-all-start.2) | async-done | bytes 1376288 | tf_op jit(solution)/shard_map/all_to_all | solution.py:205
  473.7 13.0 %multiply_reduce_fusion = (f32[64,8,21]{2,1,0:T(8,128)S(1)}, f32[64,8,21,54]{3,2,1,0:T(8,128)}) fusion(f32[64,8,21,54]{3,2,1,0:T(8,128)} %copy-done.9, f32[64,8,21]{2,1,0:T(8,128)S(1)} %copy-done.31, bf16[64,54,8,64]{3,2,0,1:T(8,128)(2,1)} %reshape.384, bf16[64,21,8,64]{3,2,1,0:T(8,128)(2,1)} %reshape.534), kind=kOutput, calls=%fused_computation.45 | convolution fusion | flops 76048896 | bytes 9646080 | tf_op jit(solution)/shard_map/nqhe,nkhe->nhqk/dot_general | solution.py:209
  486.7 11.2 %convolution_bitcast_fusion = f32[64,54,8,64]{3,1,2,0:T(8,128)} fusion(bf16[64,21,8,64]{3,2,1,0:T(8,128)(2,1)S(1)} %copy-done.25, f32[64,8,21,54]{3,2,1,0:T(8,128)} %copy-done.9, f32[64,8,21]{2,1,0:T(8,128)S(1)} %copy-done.31), kind=kOutput, calls=%fused_computation.34 | convolution fusion | flops 75479040 | bytes 10819584 | tf_op jit(solution)/shard_map/nhqk,nqhe->nkhe/dot_general | solution.py:212
  497.9 12.9 %copy.144 = f32[64,54,8,64]{3,2,0,1:T(8,128)} copy(f32[64,54,8,64]{3,1,2,0:T(8,128)} %convolution_bitcast_fusion) | data formatting | bytes 14155776 | tf_op jit(solution)/shard_map/nhqk,nqhe->nkhe/transpose | solution.py:212
  510.8 12.3 %reshape.389 = f32[64,54,512]{2,0,1:T(8,128)} reshape(f32[64,54,8,64]{3,2,0,1:T(8,128)} %copy.144) | data formatting | bytes 14155776 | tf_op jit(solution)/shard_map/reshape | solution.py:228
  523.1 8.4 multiply_convert_fusion.1
  533.2 7.6 convolution_bitcast_fusion.1
  540.7 13.0 %copy.142 = f32[64,54,8,64]{3,2,0,1:T(8,128)} copy(f32[64,54,8,64]{3,1,2,0:T(8,128)} %convolution_bitcast_fusion.1) | data formatting | bytes 14155776 | tf_op jit(solution)/shard_map/nhqk,nqhe->nkhe/transpose | solution.py:222
  553.7 12.3 %reshape.388 = f32[64,54,512]{2,0,1:T(8,128)} reshape(f32[64,54,8,64]{3,2,0,1:T(8,128)} %copy.142) | data formatting | bytes 14155776 | tf_op jit(solution)/shard_map/reshape | solution.py:227
  566.0 7.4 constant_dynamic-update-slice_fusion.1
  573.4 7.5 constant_dynamic-update-slice_fusion
  580.9 9.0 convert.55
  602.2 8.3 convolution_bitcast_fusion.2
  610.5 9.6 convert_bitcast_fusion
  637.7 60.5 %collective-permute-done.7 = bf16[64,1024]{1,0:T(8,128)(2,1)S(1)} collective-permute-done((bf16[64,1024]{1,0:T(8,128)(2,1)S(1)}, bf16[64,1024]{1,0:T(8,128)(2,1)S(1)}, u32[]{:S(2)}, u32[]{:S(2)}) %collective-permute-start.7) | collective-permute-done | bytes 131104 | tf_op jit(solution)/shard_map/ppermute | solution.py:20
  759.0 46.9 %all-to-all-done.3 = bf16[64,22,512]{2,1,0:T(8,128)(2,1)} async-done(((bf16[64,22,512]{2,1,0:T(8,128)(2,1)}), bf16[64,22,512]{2,1,0:T(8,128)(2,1)}, u32[]{:S(2)}, u32[]{:S(2)}) %all-to-all-start.3) | async-done | bytes 1441824 | tf_op jit(solution)/shard_map/all_to_all | solution.py:276
  814.2 45.0 %all-reduce = (f32[512]{0:T(512)}, f32[512]{0:T(512)}, f32[512]{0:T(512)}) all-reduce(f32[512]{0:T(512)S(1)} %get-tuple-element.25, f32[512]{0:T(512)S(1)} %copy-done.63, f32[512]{0:T(512)S(1)} %copy-done.57), channel_id=1, replica_groups=mesh['grp'=2,'seg'=16] {'grp','seg'}, use_global_device_ids=true, to_apply=%region_25.32 | all-reduce | flops 1536 | bytes 12288 | tf_op jit(solution)/shard_map/psum | solution.py:287
  865.4 150.1 %all-reduce.4.cloned.1.call-done = (f32[512,512]{1,0:T(8,128)}, f32[512,512]{1,0:T(8,128)}, f32[512,512]{1,0:T(8,128)}, f32[512,512]{1,0:T(8,128)}, f32[512,2048]{1,0:T(8,128)}, /*index=5*/f32[2048,512]{1,0:T(8,128)}) async-done(((f32[512,512]{1,0:T(8,128)}, f32[512,512]{1,0:T(8,128)}, f32[512,512]{1,0:T(8,128)}, f32[512,512]{1,0:T(8,128)}, f32[512,2048]{1,0:T(8,128)}, /*index=5*/f32[2048,512]{1,0:T(8,128)}), ...) | async-done | bytes 12582928 | tf_op jit(solution)/shard_map/psum | solution.py:287
  (323 shorter events, 265.1 us)
Async XLA Ops:
  7.2 360.9 %copy-start = (bf16[512,2048]{1,0:T(8,128)(2,1)S(1)}, bf16[512,2048]{1,0:T(8,128)(2,1)}, u32[]{:S(2)}) copy-start(bf16[512,2048]{1,0:T(8,128)(2,1)} %param.33) | copy-start | bytes 6291460
  7.3 10.5 %copy-start.59 = (pred[64]{0:T(512)(128)(4,1)}, pred[64]{0:T(512)(128)(4,1)S(1)}, u32[]{:S(2)}) copy-start(pred[64]{0:T(512)(128)(4,1)S(1)} %get-tuple-element.71) | copy-start | bytes 196
  17.8 11.2 %copy-start.74 = (s32[1,48]{1,0:T(1,128)S(1)}, s32[1,48]{1,0:T(1,128)}, u32[]{:S(2)}) copy-start(s32[1,48]{1,0:T(1,128)} %param.28) | copy-start | bytes 580
  20.6 42.6 %all-to-all-start = ((bf16[64,22,512]{2,1,0:T(8,128)(2,1)}), bf16[64,22,512]{2,1,0:T(8,128)(2,1)}, u32[]{:S(2)}, u32[]{:S(2)}) async-start(bf16[64,22,512]{2,1,0:T(8,128)(2,1)} %select_select_fusion.1), calls=%async_computation | async-start | bytes 3145728 | tf_op jit(solution)/shard_map/all_to_all | solution.py:136
  69.1 12.2 %copy-start.39 = (bf16[512,512]{1,0:T(8,128)(2,1)S(1)}, bf16[512,512]{1,0:T(8,128)(2,1)}, u32[]{:S(2)}) copy-start(bf16[512,512]{1,0:T(8,128)(2,1)} %param.29) | copy-start | bytes 1572868
  70.7 96.5 %collective-permute-start.3 = (bf16[64,17,1024]{2,0,1:T(8,128)(2,1)}, bf16[64,17,1024]{2,0,1:T(8,128)(2,1)}, u32[]{:S(2)}, u32[]{:S(2)}) collective-permute-start(bf16[64,17,1024]{2,0,1:T(8,128)(2,1)} %slice.187), channel_id=1, source_target_pairs={{0,1},{1,2},{2,3},{3,4},{4,5},{5,6},{6,7},{7,8},{8,9},{9,10},{10,1... | collective-permute-start | bytes 6684680 | tf_op jit(solution)/shard_map/ppermute | solution.py:20
  71.7 110.3 %collective-permute-start.2 = (bf16[64,17,1024]{2,0,1:T(8,128)(2,1)}, bf16[64,17,1024]{2,0,1:T(8,128)(2,1)}, u32[]{:S(2)}, u32[]{:S(2)}) collective-permute-start(bf16[64,17,1024]{2,0,1:T(8,128)(2,1)} %slice.187), channel_id=1, source_target_pairs={{0,2},{1,3},{2,4},{3,5},{4,6},{5,7},{6,8},{7,9},{8,10},{9,11},{10,... | collective-permute-start | bytes 6684680 | tf_op jit(solution)/shard_map/ppermute | solution.py:20
  76.0 43.5 %collective-permute-start.1 = (bf16[64,1024]{1,0:T(8,128)(2,1)}, bf16[64,1024]{1,0:T(8,128)(2,1)}, u32[]{:S(2)}, u32[]{:S(2)}) collective-permute-start(bf16[64,1024]{1,0:T(8,128)(2,1)} %slice_bitcast_fusion.2), channel_id=1, source_target_pairs={{0,3},{1,4},{2,5},{3,6},{4,7},{5,8},{6,9},{7,10},{8,11},{9,12},{10... | collective-permute-start | bytes 393224 | tf_op jit(solution)/shard_map/ppermute | solution.py:20
  81.2 40.8 %collective-permute-start = (bf16[64,1024]{1,0:T(8,128)(2,1)}, bf16[64,1024]{1,0:T(8,128)(2,1)S(1)}, u32[]{:S(2)}, u32[]{:S(2)}) collective-permute-start(bf16[64,1024]{1,0:T(8,128)(2,1)} %slice_bitcast_fusion.2), channel_id=1, source_target_pairs={{0,4},{1,5},{2,6},{3,7},{4,8},{5,9},{6,10},{7,11},{8,12},{9,13},{1... | collective-permute-start | bytes 393224 | tf_op jit(solution)/shard_map/ppermute | solution.py:20
  252.2 11.1 %copy-start.9 = (f32[64,8,21,54]{3,2,1,0:T(8,128)}, f32[64,8,21,54]{3,2,1,0:T(8,128)S(1)}, u32[]{:S(2)}) copy-start(f32[64,8,21,54]{3,2,1,0:T(8,128)S(1)} %get-tuple-element.54) | copy-start | bytes 6967300
  252.2 11.1 %copy-start.30 = (f32[64,8,21]{2,1,0:T(8,128)}, f32[64,8,21]{2,1,0:T(8,128)S(1)}, u32[]{:S(2)}) copy-start(f32[64,8,21]{2,1,0:T(8,128)S(1)} %get-tuple-element.53) | copy-start | bytes 129028
  270.0 90.1 %all-to-all-start.1 = ((bf16[64,21,512]{2,1,0:T(8,128)(2,1)}), bf16[64,21,512]{2,1,0:T(8,128)(2,1)}, u32[]{:S(2)}, u32[]{:S(2)}) async-start(bf16[64,21,512]{2,1,0:T(8,128)(2,1)} %reshape.533), calls=%async_computation.1 | async-start | bytes 3145728 | tf_op jit(solution)/shard_map/all_to_all | solution.py:180
  329.4 35.6 %copy-start.64 = (pred[64]{0:T(512)(128)(4,1)}, pred[64]{0:T(512)(128)(4,1)S(1)}, u32[]{:S(2)}) copy-start(pred[64]{0:T(512)(128)(4,1)S(1)} %compare_and_fusion.4) | copy-start | bytes 196
  329.6 35.4 %copy-start.58 = (s32[1024]{0:T(1024)}, s32[1024]{0:T(1024)S(1)}, u32[]{:S(2)}) copy-start(s32[1024]{0:T(1024)S(1)} %pad_clamp_fusion.4) | copy-start | bytes 12292
  367.5 53.9 %copy-start.4 = (f32[64,20,512]{2,0,1:T(8,128)}, f32[64,20,512]{2,0,1:T(8,128)S(1)}, u32[]{:S(2)}) copy-start(f32[64,20,512]{2,0,1:T(8,128)S(1)} %get-tuple-element.43) | copy-start | bytes 7864324
  373.0 24.7 %copy-start.16 = (f32[64,20,2048]{2,0,1:T(8,128)}, f32[64,20,2048]{2,0,1:T(8,128)S(1)}, u32[]{:S(2)}) copy-start(f32[64,20,2048]{2,0,1:T(8,128)S(1)} %get-tuple-element.55) | copy-start | bytes 31457284
  373.0 24.7 %copy-start.68 = (bf16[2048,512]{1,0:T(8,128)(2,1)S(1)}, bf16[2048,512]{1,0:T(8,128)(2,1)}, u32[]{:S(2)}) copy-start(bf16[2048,512]{1,0:T(8,128)(2,1)} %param.34) | copy-start | bytes 6291460
  406.1 16.8 %copy-start.11 = (f32[64,20,512]{2,0,1:T(8,128)}, f32[64,20,512]{2,0,1:T(8,128)S(1)}, u32[]{:S(2)}) copy-start(f32[64,20,512]{2,0,1:T(8,128)S(1)} %get-tuple-element.39) | copy-start | bytes 7864324
  430.7 40.0 %all-to-all-start.2 = ((bf16[64,21,512]{2,1,0:T(8,128)(2,1)}), bf16[64,21,512]{2,1,0:T(8,128)(2,1)S(1)}, u32[]{:S(2)}, u32[]{:S(2)}) async-start(bf16[64,21,512]{2,1,0:T(8,128)(2,1)} %select_select_fusion), calls=%async_computation.2 | async-start | bytes 3145728 | tf_op jit(solution)/shard_map/all_to_all | solution.py:205
  438.0 577.5 %all-reduce.4.cloned.1.call-start = ((), (), s32[]{:S(2)}) async-start(), calls=%async_computation.4 | async-start | bytes 25165824 | tf_op jit(solution)/shard_map/psum | solution.py:287
  449.4 24.3 %copy-start.31 = (f32[64,8,21]{2,1,0:T(8,128)S(1)}, f32[64,8,21]{2,1,0:T(8,128)}, u32[]{:S(2)}) copy-start(f32[64,8,21]{2,1,0:T(8,128)} %copy-done.30) | copy-start | bytes 129028
  473.7 13.0 %copy-start.25 = (bf16[64,21,8,64]{3,2,1,0:T(8,128)(2,1)S(1)}, bf16[64,21,8,64]{3,2,1,0:T(8,128)(2,1)}, u32[]{:S(2)}) copy-start(bf16[64,21,8,64]{3,2,1,0:T(8,128)(2,1)} %reshape.534) | copy-start | bytes 4128772
  594.9 118.3 %collective-permute-start.5 = (bf16[64,17,1024]{2,0,1:T(8,128)(2,1)}, bf16[64,17,1024]{2,0,1:T(8,128)(2,1)}, u32[]{:S(2)}, u32[]{:S(2)}) collective-permute-start(bf16[64,17,1024]{2,0,1:T(8,128)(2,1)} %pad_maximum_fusion.2), channel_id=1, source_target_pairs={{0,14},{1,15},{2,0},{3,1},{4,2},{5,3},{6,4},{7,5},{8,6},{9,7},{10,... | collective-permute-start | bytes 6684680 | tf_op jit(solution)/shard_map/ppermute | solution.py:20
  602.2 98.8 %collective-permute-start.4 = (bf16[64,17,1024]{2,0,1:T(8,128)(2,1)}, bf16[64,17,1024]{2,0,1:T(8,128)(2,1)}, u32[]{:S(2)}, u32[]{:S(2)}) collective-permute-start(bf16[64,17,1024]{2,0,1:T(8,128)(2,1)} %pad_maximum_fusion.1), channel_id=1, source_target_pairs={{0,15},{1,0},{2,1},{3,2},{4,3},{5,4},{6,5},{7,6},{8,7},{9,8},{10,9... | collective-permute-start | bytes 6684680 | tf_op jit(solution)/shard_map/ppermute | solution.py:20
  628.0 70.2 %collective-permute-start.7 = (bf16[64,1024]{1,0:T(8,128)(2,1)S(1)}, bf16[64,1024]{1,0:T(8,128)(2,1)S(1)}, u32[]{:S(2)}, u32[]{:S(2)}) collective-permute-start(bf16[64,1024]{1,0:T(8,128)(2,1)S(1)} %copy-done.47), channel_id=1, source_target_pairs={{0,12},{1,13},{2,14},{3,15},{4,0},{5,1},{6,2},{7,3},{8,4},{9,5},{1... | collective-permute-start | bytes 393224 | tf_op jit(solution)/shard_map/ppermute | solution.py:20
  630.3 69.3 %collective-permute-start.6 = (bf16[64,1024]{1,0:T(8,128)(2,1)S(1)}, bf16[64,1024]{1,0:T(8,128)(2,1)S(1)}, u32[]{:S(2)}, u32[]{:S(2)}) collective-permute-start(bf16[64,1024]{1,0:T(8,128)(2,1)S(1)} %copy-done.46), channel_id=1, source_target_pairs={{0,13},{1,14},{2,15},{3,0},{4,1},{5,2},{6,3},{7,4},{8,5},{9,6},{10... | collective-permute-start | bytes 393224 | tf_op jit(solution)/shard_map/ppermute | solution.py:20
  750.7 58.6 %copy-start.65 = (pred[64]{0:T(512)(128)(4,1)S(1)}, pred[64]{0:T(512)(128)(4,1)}, u32[]{:S(2)}) copy-start(pred[64]{0:T(512)(128)(4,1)} %copy-done.64) | copy-start | bytes 196
  750.7 55.2 %all-to-all-start.3 = ((bf16[64,22,512]{2,1,0:T(8,128)(2,1)}), bf16[64,22,512]{2,1,0:T(8,128)(2,1)}, u32[]{:S(2)}, u32[]{:S(2)}) async-start(bf16[64,22,512]{2,1,0:T(8,128)(2,1)} %copy.149), calls=%async_computation.3 | async-start | bytes 3145728 | tf_op jit(solution)/shard_map/all_to_all | solution.py:276
  759.0 52.2 %copy-start.3 = (bf16[64,20,512]{2,0,1:T(8,128)(2,1)S(1)}, bf16[64,20,512]{2,0,1:T(8,128)(2,1)}, u32[]{:S(2)}) copy-start(bf16[64,20,512]{2,0,1:T(8,128)(2,1)} %param.26) | copy-start | bytes 3932164
  759.0 52.2 %copy-start.43 = (f32[64,20]{0,1:T(8,128)S(1)}, f32[64,20]{0,1:T(8,128)}, u32[]{:S(2)}) copy-start(f32[64,20]{0,1:T(8,128)} %copy-done.42) | copy-start | bytes 15364
  759.0 52.2 %copy-start.54 = (f32[512]{0:T(512)S(1)}, f32[512]{0:T(512)}, u32[]{:S(2)}) copy-start(f32[512]{0:T(512)} %param.35) | copy-start | bytes 6148
  811.3 48.5 %copy-start.51 = (f32[64,20]{0,1:T(8,128)S(1)}, f32[64,20]{0,1:T(8,128)}, u32[]{:S(2)}) copy-start(f32[64,20]{0,1:T(8,128)} %copy-done.50) | copy-start | bytes 15364
  (58 other events, 208.2 us)
Sparse Core Ops, SparseCore 0:
  744.1 271.3 all-reduce.3
where the time goes:
time: 1040 us; the launch traced here: 1030 us
  waiting for transfers between devices  412 us (40%)
  local copies, waits for them, and re-layouts  220 us (21%)
  matrix products  123 us (12%)
  other arithmetic  118 us (11%)
  starting transfers between devices  101 us (10%)
  blocking collectives  45 us (4%)
  between operations  15.4 us (1%)
    psum x1, waiting for transfers between devices, per_device(): lax.psum((grad_query, grad_key, grad_value, grad_input_gain, grad_up, gra...  150 us
    ppermute x8, waiting for transfers between devices, from_behind(): return lax.ppermute(x, axis, [(i, (i + by) % size) for i in range(size)])  131 us
    all_to_all x1, starting transfers between devices, per_device(): lax.all_to_all(attended, 'seg', split_axis=0, concat_axis=0, tiled=True)  59.4 us
    all_to_all x1, waiting for transfers between devices, per_device(): lax.all_to_all(sent_home, 'seg', split_axis=0, concat_axis=0, tiled=True)  46.9 us
    psum x1, blocking collectives, per_device(): lax.psum((grad_query, grad_key, grad_value, grad_input_gain, grad_up, gra...  45 us
    unnamed x163, local copies, waits for them, and re-layouts  35.2 us
    all_to_all x1, waiting for transfers between devices, per_device(): lax.all_to_all(send_out(payload), 'seg', split_axis=0, concat_axis=0, til...  31.5 us
    all_to_all x1, waiting for transfers between devices, per_device(): lax.all_to_all(attended, 'seg', split_axis=0, concat_axis=0, tiled=True)  30.5 us
  transfers between devices with their start and end apart: 13, of which 8 were waited for; matrix products, arithmetic and copies ran while one was open for 11% of the time, Pallas kernels for 0%

commit v1 on v0

v1 whole, which is shorter than its diff:
```python
import functools

import jax
import jax.numpy as jnp
import numpy as np
from jax import lax
from jax.experimental import pallas as pl
from jax.experimental.pallas import tpu as pltpu
from jax.sharding import PartitionSpec as P

HEADS = 8
HDIM = 64
SEGLEN = 16
RIGHT = 4
LEFT = 30
MEMS = 4
FRAMES = RIGHT + SEGLEN

GROUP = 4
BLOCK = 16
ROWS = BLOCK * FRAMES
GROUP_ROWS = GROUP * FRAMES
GROUPS = BLOCK // GROUP
EXTRA = 8
HALO = 2 * FRAMES
WINDOW = GROUP_ROWS + HALO + 2 * MEMS
STACK = 2 * GROUP_ROWS + 2 * EXTRA
PAIRS = HEADS // 2
PAIR = 2 * HDIM

EPSILON = 1e-05
MASKED_SCORE = -1e30
FAR = 1 << 20

BF = jnp.bfloat16
F32 = jnp.float32
VMEM_LIMIT = 60 * 1024 * 1024


def dot(a, b):
    return lax.dot_general(a, b, (((1,), (0,)), ((), ())), preferred_element_type=F32)


def dot_back(a, b):
    return lax.dot_general(a, b, (((1,), (1,)), ((), ())), preferred_element_type=F32)


def dot_outer(a, b):
    return lax.dot_general(a, b, (((0,), (0,)), ((), ())), preferred_element_type=F32)


def stack_tables():
    row = np.arange(STACK)
    extra = row >= 2 * GROUP_ROWS
    inner = (row - 2 * GROUP_ROWS) % EXTRA
    segment = np.where(extra, inner % GROUP, row % GROUP_ROWS // FRAMES)
    second = np.where(extra, row >= 2 * GROUP_ROWS + EXTRA, row >= GROUP_ROWS)
    key = np.arange(WINDOW)
    is_memory = key >= WINDOW - 2 * MEMS
    key_segment = np.where(is_memory, key - (WINDOW - 2 * MEMS) - MEMS, key // FRAMES - 2)
    within = key % FRAMES
    is_right = ~is_memory & (within < RIGHT)
    behind = segment[:, None] - key_segment[None, :]
    frame_ok = np.where(
        is_right[None],
        behind == 0,
        (behind == 0)
        | (behind == 1)
        | ((behind == 2) & (within >= RIGHT + 2 * SEGLEN - LEFT)[None]),
    )
    memory_ok = (behind >= 1) & (behind <= MEMS) & ~extra[:, None]
    ok = np.where(is_memory[None], memory_ok, frame_ok)
    need = np.where(ok, behind, FAR).astype(np.int32)
    segment_of = np.broadcast_to(segment[:, None], (STACK, WINDOW)).astype(np.int32)
    lanes = np.arange(PAIR)[None, :] >= HDIM
    head = (lanes == second[:, None]).astype(np.float32)
    return need, np.ascontiguousarray(segment_of), head


def row_stats(values):
    centered = values - jnp.mean(values, axis=-1, keepdims=True)
    spread = jnp.mean(centered * centered, axis=-1, keepdims=True)
    scale = lax.rsqrt(spread + EPSILON)
    return centered * scale, scale


def norm_back(unit, scale, gain, gradient):
    gained = gradient * gain
    along = jnp.mean(gained * unit, axis=-1, keepdims=True)
    grad = scale * (gained - jnp.mean(gained, axis=-1, keepdims=True) - unit * along)
    return grad, jnp.sum(gradient * unit, axis=0, keepdims=True)


def pack_rows(source, target, count, offset=0):
    for j in range(count):
        target[offset + j * FRAMES : offset + (j + 1) * FRAMES] = source[j].astype(F32)


def project_kernel(
    frames, before, halo, memory, memory_halo, gain, query_w, key_w, value_w,
    packed, shared, summary, query, query_extra, window,
    rows, memory_rows,
):
    step = pl.program_id(0)

    @pl.when(step == 0)
    def _():
        memory_rows[0:8] = memory_halo[...].astype(F32)
        memory_rows[8:] = memory[...].astype(F32)
        pack_rows(halo, rows, 2)

    @pl.when(step > 0)
    def _():
        pack_rows(before, rows, 2)

    pack_rows(frames, rows, BLOCK, HALO)
    packed[...] = rows[HALO:].astype(BF)
    unit, _ = row_stats(rows[...])
    normed = unit * gain[...]
    rows[...] = normed
    for j in range(BLOCK):
        at = HALO + j * FRAMES
        mean = jnp.sum(rows[at + RIGHT : at + FRAMES], axis=0, keepdims=True) * (1.0 / SEGLEN)
        spot = j // GROUP * EXTRA + j % GROUP
        summary[spot : spot + 1] = mean
        summary[spot + GROUP : spot + GROUP + 1] = jnp.zeros_like(mean)
    own = rows[HALO:].astype(BF)
    shared[...] = own
    extra = summary[...].astype(BF)
    query[...] = (dot(own, query_w[...]) * 0.125).astype(BF)
    extra_query = dot(extra, query_w[...]) * 0.125
    around = memory_rows[pl.ds(pl.multiple_of(step * BLOCK, 8), BLOCK + 8)]
    for g in range(GROUPS):
        part = extra_query[g * EXTRA : (g + 1) * EXTRA]
        query_extra[2 * g * EXTRA : 2 * (g + 1) * EXTRA] = jnp.concatenate([part, part], axis=0).astype(BF)
    wide = []
    for g in range(GROUPS):
        at = g * GROUP_ROWS
        wide.append(rows[at : at + GROUP_ROWS + HALO])
        wide.append(around[MEMS + g * GROUP : MEMS + g * GROUP + 2 * MEMS])
    wide = jnp.concatenate(wide, axis=0).astype(BF)
    width = wide.shape[1]
    window[:, :width] = dot(wide, key_w[...]).astype(BF)
    window[:, width:] = dot(wide, value_w[...]).astype(BF)


def query_stack(frames, extra, head):
    return jnp.concatenate([frames, frames, extra], axis=0) * head


def unstack(stacked, low):
    frames = jnp.where(low, stacked[:GROUP_ROWS], stacked[GROUP_ROWS : 2 * GROUP_ROWS])
    at = 2 * GROUP_ROWS
    extra = jnp.where(low, stacked[at : at + EXTRA], stacked[at + EXTRA : at + 2 * EXTRA])
    return frames, extra


def low_lanes():
    return lax.broadcasted_iota(jnp.int32, (1, PAIR), 1) < HDIM


def gelu_parts(lifted):
    bell = jnp.exp(lifted * lifted * -0.5) * 0.3989422804014327
    share = 0.5 + 0.5 * lax.erf(lifted * 0.7071067811865476)
    return lifted * share, share + lifted * bell


def forward_kernel(
    position, need, segment_of, head, query, query_extra, window, packed, out_grad,
    out_w, up_w, down_w, middle_gain, output_gain,
    attended, attended_extra, soft, residual_out, slope, grad_combined_out, result, memory_out, grad_down, grad_gain,
    rows, down_sum, hidden, memory_rows,
):
    step = pl.program_id(0)
    steps = pl.num_programs(0)
    width = packed.shape[1]
    low = low_lanes()
    head_mask = head[...]
    for g in range(GROUPS):
        first = step * BLOCK + g * GROUP
        where_row = segment_of[...]
        at_row = jnp.where(
            where_row < 2,
            jnp.where(where_row == 0, position[first], position[first + 1]),
            jnp.where(where_row == 2, position[first + 2], position[first + 3]),
        )
        bias = jnp.where(at_row >= need[...], 0.0, MASKED_SCORE)
        for p in range(PAIRS):
            lanes = slice(p * PAIR, (p + 1) * PAIR)
            value_lanes = slice(width + p * PAIR, width + (p + 1) * PAIR)
            keys = window[g * WINDOW : (g + 1) * WINDOW, lanes]
            values = window[g * WINDOW : (g + 1) * WINDOW, value_lanes]
            stack = query_stack(
                query[g * GROUP_ROWS : (g + 1) * GROUP_ROWS, lanes],
                query_extra[2 * g * EXTRA : 2 * (g + 1) * EXTRA, lanes],
                head_mask,
            )
            scores = dot_back(stack, keys) + bias
            powers = jnp.exp(scores - jnp.max(scores, axis=-1, keepdims=True))
            soft_low = (powers / jnp.sum(powers, axis=-1, keepdims=True)).astype(BF)
            at = (g * PAIRS + p) * STACK
            soft[at : at + STACK] = soft_low
            frames, extra = unstack(dot(soft_low, values), low)
            attended[g * GROUP_ROWS : (g + 1) * GROUP_ROWS, lanes] = frames.astype(BF)
            rows[g * EXTRA : (g + 1) * EXTRA, lanes] = extra
    attended_extra[...] = rows[: GROUPS * EXTRA].astype(BF)
    branch_extra = dot(attended_extra[...], out_w[...])
    rows[: GROUPS * EXTRA] = branch_extra
    for g in range(GROUPS):
        memory_rows[g * GROUP : (g + 1) * GROUP] = rows[g * EXTRA : g * EXTRA + GROUP]
    memory_out[...] = memory_rows[...].astype(BF)
    residual = packed[...].astype(F32) + dot(attended[...], out_w[...])
    residual_out[...] = residual
    unit, _ = row_stats(residual)
    middle = (unit * middle_gain[...]).astype(BF)
    ff = up_w.shape[1]
    tile = width
    combined = residual
    for c in range(ff // tile):
        columns = slice(c * tile, (c + 1) * tile)
        part, turn = gelu_parts(dot(middle, up_w[:, columns]))
        part = part.astype(BF)
        hidden[:, columns] = part
        slope[:, columns] = turn.astype(BF)
        combined = combined + dot(part, down_w[columns])
    unit, scale = row_stats(combined)
    rows[...] = unit * output_gain[...]
    for j in range(BLOCK):
        result[j] = rows[j * FRAMES : (j + 1) * FRAMES].astype(BF)
    pack_rows(out_grad, rows, BLOCK)
    grad_combined, gain_part = norm_back(unit, scale, output_gain[...], rows[...])
    grad_combined_out[...] = grad_combined
    grad_ff = grad_combined.astype(BF)

    @pl.when(step == 0)
    def _():
        grad_gain[...] = gain_part
        for c in range(ff // tile):
            down_sum[c * tile : (c + 1) * tile] = dot_outer(hidden[:, c * tile : (c + 1) * tile], grad_ff)

    @pl.when(step > 0)
    def _():
        grad_gain[...] += gain_part
        for c in range(ff // tile):
            down_sum[c * tile : (c + 1) * tile] += dot_outer(hidden[:, c * tile : (c + 1) * tile], grad_ff)

    @pl.when(step == steps - 1)
    def _():
        grad_down[...] = down_sum[...].astype(BF)


def backward_kernel(
    slope, grad_combined, residual, attended, attended_extra, memory_grad, out_w, up_w, down_w, middle_gain,
    grad_residual_out, grad_attended, grad_attended_extra, grad_up, grad_out, grad_gain,
    up_sum, out_sum, rows,
):
    step = pl.program_id(0)
    steps = pl.num_programs(0)

    @pl.when(step == 0)
    def _():
        up_sum[...] = jnp.zeros_like(up_sum)
        out_sum[...] = jnp.zeros_like(out_sum)
        grad_gain[...] = jnp.zeros_like(grad_gain)

    width = residual.shape[1]
    ff = up_w.shape[1]
    tile = width
    unit, scale = row_stats(residual[...])
    middle = (unit * middle_gain[...]).astype(BF)
    grad_combined_rows = grad_combined[...]
    grad_ff = grad_combined_rows.astype(BF)
    grad_middle = jnp.zeros_like(unit)
    for c in range(ff // tile):
        columns = slice(c * tile, (c + 1) * tile)
        lifted = (dot_back(grad_ff, down_w[columns]) * slope[:, columns].astype(F32)).astype(BF)
        up_sum[:, columns] += dot_outer(middle, lifted)
        grad_middle = grad_middle + dot_back(lifted, up_w[:, columns])
    grad_norm, gain_part = norm_back(unit, scale, middle_gain[...], grad_middle)
    grad_gain[...] += gain_part
    grad_residual = grad_combined_rows + grad_norm
    grad_residual_out[...] = grad_residual
    grad_branch = grad_residual.astype(BF)
    memory_rows = memory_grad[...].astype(F32)
    for g in range(GROUPS):
        rows[g * EXTRA : g * EXTRA + GROUP] = memory_rows[g * GROUP : (g + 1) * GROUP]
        rows[g * EXTRA + GROUP : (g + 1) * EXTRA] = jnp.zeros((EXTRA - GROUP, width), F32)
    extra = rows[...].astype(BF)
    out_sum[...] += dot_outer(attended[...], grad_branch) + dot_outer(attended_extra[...], extra)
    grad_attended[...] = dot_back(grad_branch, out_w[...]).astype(BF)
    back_extra = dot_back(extra, out_w[...])
    for g in range(GROUPS):
        part = back_extra[g * EXTRA : (g + 1) * EXTRA]
        grad_attended_extra[2 * g * EXTRA : 2 * (g + 1) * EXTRA] = jnp.concatenate([part, part], axis=0).astype(BF)

    @pl.when(step == steps - 1)
    def _():
        grad_up[...] = up_sum[...].astype(BF)
        grad_out[...] = out_sum[...].astype(BF)


def attention_back_kernel(
    head, query, query_extra, window, soft, grad_attended, grad_attended_extra,
    grad_query, grad_query_extra, pair_sum, pair_memory, halo_back, memory_back,
    rows,
):
    step = pl.program_id(0)
    width = query.shape[1]
    low = low_lanes()
    head_mask = head[...]

    @pl.when(step == 0)
    def _():
        pair_sum[...] = jnp.zeros_like(pair_sum)

    for g in range(GROUPS):
        start = pl.multiple_of((step * GROUPS + g) * GROUP_ROWS, GROUP_ROWS)
        for p in range(PAIRS):
            lanes = slice(p * PAIR, (p + 1) * PAIR)
            value_lanes = slice(width + p * PAIR, width + (p + 1) * PAIR)
            keys = window[g * WINDOW : (g + 1) * WINDOW, lanes]
            values = window[g * WINDOW : (g + 1) * WINDOW, value_lanes]
            stack = query_stack(
                query[g * GROUP_ROWS : (g + 1) * GROUP_ROWS, lanes],
                query_extra[2 * g * EXTRA : 2 * (g + 1) * EXTRA, lanes],
                head_mask,
            )
            grads = query_stack(
                grad_attended[g * GROUP_ROWS : (g + 1) * GROUP_ROWS, lanes],
                grad_attended_extra[2 * g * EXTRA : 2 * (g + 1) * EXTRA, lanes],
                head_mask,
            )
            at = (g * PAIRS + p) * STACK
            soft_low = soft[at : at + STACK]
            soft_wide = soft_low.astype(F32)
            grad_soft = dot_back(grads, values)
            weighted = grad_soft * soft_wide
            grad_scores = (weighted - soft_wide * jnp.sum(weighted, axis=-1, keepdims=True)).astype(BF)
            frames, extra = unstack(dot(grad_scores, keys), low)
            grad_query[g * GROUP_ROWS : (g + 1) * GROUP_ROWS, lanes] = frames.astype(BF)
            rows[g * EXTRA : (g + 1) * EXTRA, lanes] = extra
            grad_keys = dot_outer(grad_scores, stack)
            grad_values = dot_outer(soft_low, grads)
            own = GROUP_ROWS + HALO
            pair_sum[pl.ds(start, own), lanes] += grad_keys[:own]
            pair_sum[pl.ds(start, own), value_lanes] += grad_values[:own]
            pair_memory[g * 2 * MEMS : (g + 1) * 2 * MEMS, lanes] = grad_keys[own:]
            pair_memory[g * 2 * MEMS : (g + 1) * 2 * MEMS, value_lanes] = grad_values[own:]
    grad_query_extra[...] = rows[...].astype(BF)

    @pl.when(step == 0)
    def _():
        halo_back[...] = pair_sum[:HALO].astype(BF)
        memory_back[...] = pair_memory[: 2 * MEMS].astype(BF)


def projection_back_kernel(
    pair_sum, pair_memory, memory_next, halo_next, memory_halo_next,
    grad_query_rows, grad_query_extra, shared, summary, memory, packed, grad_residual,
    query_w, key_w, value_w, gain,
    grad_frames, grad_memory, grad_query, grad_key, grad_value, grad_gain,
    query_sum, key_sum, value_sum, rows,
):
    step = pl.program_id(0)
    steps = pl.num_programs(0)

    @pl.when(step == 0)
    def _():
        query_sum[...] = jnp.zeros_like(query_sum)
        key_sum[...] = jnp.zeros_like(key_sum)
        value_sum[...] = jnp.zeros_like(value_sum)
        grad_gain[...] = jnp.zeros_like(grad_gain)

    last = step == steps - 1
    width = shared.shape[1]
    start = pl.multiple_of(step * ROWS + HALO, 8)
    pair = pair_sum[pl.ds(start, ROWS)]
    late = jnp.where(last, halo_next[...].astype(F32), 0.0)
    pair = jnp.concatenate([pair[: ROWS - HALO], pair[ROWS - HALO :] + late], axis=0).astype(BF)
    memory_late = jnp.where(last, memory_halo_next[...].astype(F32), memory_next[...])
    memory_pair = []
    for g in range(GROUPS):
        this = pair_memory[g * 2 * MEMS + MEMS : (g + 1) * 2 * MEMS]
        if g + 1 < GROUPS:
            after = pair_memory[(g + 1) * 2 * MEMS : (g + 1) * 2 * MEMS + MEMS]
        else:
            after = memory_late[:MEMS]
        memory_pair.append(this + after)
    memory_pair = jnp.concatenate(memory_pair, axis=0).astype(BF)
    grad_keys, grad_values = pair[:, :width], pair[:, width:]
    memory_keys, memory_values = memory_pair[:, :width], memory_pair[:, width:]
    own, extra, own_memory = shared[...], summary[...].astype(BF), memory[...]
    queries, extra_queries = grad_query_rows[...], grad_query_extra[...]
    query_sum[...] += dot_outer(own, queries) + dot_outer(extra, extra_queries)
    key_sum[...] += dot_outer(own, grad_keys) + dot_outer(own_memory, memory_keys)
    value_sum[...] += dot_outer(own, grad_values) + dot_outer(own_memory, memory_values)
    back = dot_back(queries, query_w[...]) * 0.125 + dot_back(grad_keys, key_w[...]) + dot_back(grad_values, value_w[...])
    grad_memory[...] = (dot_back(memory_keys, key_w[...]) + dot_back(memory_values, value_w[...])).astype(BF)
    summary_back = dot_back(extra_queries, query_w[...]) * (0.125 / SEGLEN)
    rows[...] = back
    for j in range(BLOCK):
        spot = j // GROUP * EXTRA + j % GROUP
        rows[j * FRAMES + RIGHT : (j + 1) * FRAMES] += summary_back[spot : spot + 1]
    unit, scale = row_stats(packed[...].astype(F32))
    grad_norm, gain_part = norm_back(unit, scale, gain[...], rows[...])
    grad_gain[...] += gain_part
    rows[...] = grad_residual[...] + grad_norm
    for j in range(BLOCK):
        grad_frames[j] = rows[j * FRAMES : (j + 1) * FRAMES]

    @pl.when(last)
    def _():
        grad_query[...] = (query_sum[...] * 0.125).astype(BF)
        grad_key[...] = key_sum[...].astype(BF)
        grad_value[...] = value_sum[...].astype(BF)


def whole(shape):
    return pl.BlockSpec(shape, lambda i: (0,) * len(shape))


def rows_of(*shape):
    return pl.BlockSpec(shape, lambda i: (i,) + (0,) * (len(shape) - 1))


def params():
    return pltpu.CompilerParams(vmem_limit_bytes=VMEM_LIMIT)


def shape_of(dtype, *shape):
    return jax.ShapeDtypeStruct(shape, dtype)


def segment_position(counts_row, segment):
    order = jnp.arange(counts_row.shape[0], dtype=jnp.int32)
    starts = jnp.sum(jnp.where(order[None, :] < order[:, None], counts_row[None, :], 0), axis=1)
    first = jnp.max(jnp.where(starts[None, :] <= segment[:, None], starts[None, :], 0), axis=1)
    return segment - first


def shift(values, axis, by):
    size = lax.axis_size(axis)
    return lax.ppermute(values, axis, [(i, (i + by) % size) for i in range(size)])


def swap(values, axis, bit):
    size = lax.axis_size(axis)
    return lax.ppermute(values, axis, [(i, i ^ bit) for i in range(size)])


def axis_bits(axis):
    size = lax.axis_size(axis)
    return [1 << i for i in range(size.bit_length() - 1)]


def sum_everywhere(values):
    dtype = values.dtype
    steps = [("grp", b) for b in axis_bits("grp")] + [("seg", b) for b in axis_bits("seg")]
    sides = []
    for axis, bit in steps:
        side = (lax.axis_index(axis) // bit) % 2
        half = values.shape[0] // 2
        keep = lax.dynamic_slice_in_dim(values, side * half, half, 0)
        send = lax.dynamic_slice_in_dim(values, (1 - side) * half, half, 0)
        values = (keep.astype(F32) + swap(send, axis, bit).astype(F32)).astype(dtype)
        sides.append(side)
    for (axis, bit), side in zip(reversed(steps), reversed(sides)):
        other = swap(values, axis, bit)
        values = jnp.where(
            side == 0, jnp.concatenate([values, other], axis=0), jnp.concatenate([other, values], axis=0)
        )
    return values


def sum_small(values):
    for axis in ("grp", "seg"):
        for bit in axis_bits(axis):
            values = values + swap(values, axis, bit)
    return values


def per_device(
    frames_in, memory, counts, query_weight, key_weight, value_weight, out_weight, up_weight, down_weight,
    input_gain, middle_gain, output_gain, out_grad, memory_grad,
):
    slots, _, width = frames_in.shape
    ff = up_weight.shape[1]
    steps = slots // BLOCK
    total = slots * FRAMES
    groups = slots // GROUP
    grid = (steps,)
    need, segment_of, head = stack_tables()
    need, segment_of, head = jnp.asarray(need), jnp.asarray(segment_of), jnp.asarray(head, BF)
    input_gain, middle_gain, output_gain = (g.reshape(1, width) for g in (input_gain, middle_gain, output_gain))
    segment = lax.axis_index("seg") * slots + jnp.arange(slots, dtype=jnp.int32)
    position = segment_position(counts[0], segment)
    halo = shift(frames_in[slots - 2 :], "seg", 1)
    memory_halo = shift(memory[slots - 8 :], "seg", 1)

    packed, shared, summary, query, query_extra, window = pl.pallas_call(
        project_kernel,
        grid=grid,
        in_specs=[
            rows_of(BLOCK, FRAMES, width),
            pl.BlockSpec((2, FRAMES, width), lambda i: (jnp.maximum(i * (BLOCK // 2) - 1, 0), 0, 0)),
            whole((2, FRAMES, width)),
            whole((slots, width)),
            whole((8, width)),
            whole((1, width)),
            whole((width, width)),
            whole((width, width)),
            whole((width, width)),
        ],
        out_specs=[
            rows_of(ROWS, width),
            rows_of(ROWS, width),
            rows_of(GROUPS * EXTRA, width),
            rows_of(ROWS, width),
            rows_of(2 * GROUPS * EXTRA, width),
            rows_of(GROUPS * WINDOW, 2 * width),
        ],
        out_shape=[
            shape_of(BF, total, width),
            shape_of(BF, total, width),
            shape_of(F32, groups * EXTRA, width),
            shape_of(BF, total, width),
            shape_of(BF, 2 * groups * EXTRA, width),
            shape_of(BF, groups * WINDOW, 2 * width),
        ],
        scratch_shapes=[pltpu.VMEM((ROWS + HALO, width), F32), pltpu.VMEM((slots + 8, width), F32)],
        compiler_params=params(),
        name="project",
    )(frames_in, frames_in, halo, memory, memory_halo, input_gain, query_weight, key_weight, value_weight)

    (
        attended, attended_extra, soft, residual, slope, grad_combined, result, memory_out, grad_down, output_part,
    ) = pl.pallas_call(
        forward_kernel,
        grid=grid,
        in_specs=[
            pl.BlockSpec(memory_space=pltpu.SMEM),
            whole((STACK, WINDOW)),
            whole((STACK, WINDOW)),
            whole((STACK, PAIR)),
            rows_of(ROWS, width),
            rows_of(2 * GROUPS * EXTRA, width),
            rows_of(GROUPS * WINDOW, 2 * width),
            rows_of(ROWS, width),
            rows_of(BLOCK, FRAMES, width),
            whole((width, width)),
            whole((width, ff)),
            whole((ff, width)),
            whole((1, width)),
            whole((1, width)),
        ],
        out_specs=[
            rows_of(ROWS, width),
            rows_of(GROUPS * EXTRA, width),
            rows_of(GROUPS * PAIRS * STACK, WINDOW),
            rows_of(ROWS, width),
            rows_of(ROWS, ff),
            rows_of(ROWS, width),
            rows_of(BLOCK, FRAMES, width),
            rows_of(BLOCK, width),
            whole((ff, width)),
            whole((1, width)),
        ],
        out_shape=[
            shape_of(BF, total, width),
            shape_of(BF, groups * EXTRA, width),
            shape_of(BF, groups * PAIRS * STACK, WINDOW),
            shape_of(F32, total, width),
            shape_of(BF, total, ff),
            shape_of(F32, total, width),
            shape_of(BF, slots, FRAMES, width),
            shape_of(BF, slots, width),
            shape_of(BF, ff, width),
            shape_of(F32, 1, width),
        ],
        scratch_shapes=[
            pltpu.VMEM((ROWS, width), F32),
            pltpu.VMEM((ff, width), F32),
            pltpu.VMEM((ROWS, ff), BF),
            pltpu.VMEM((BLOCK, width), F32),
        ],
        compiler_params=params(),
        name="forward",
    )(
        position, need, segment_of, head, query, query_extra, window, packed, out_grad,
        out_weight, up_weight, down_weight, middle_gain, output_gain,
    )

    grad_residual, grad_attended, grad_attended_extra, grad_up, grad_out, middle_part = pl.pallas_call(
        backward_kernel,
        grid=grid,
        in_specs=[
            rows_of(ROWS, ff),
            rows_of(ROWS, width),
            rows_of(ROWS, width),
            rows_of(ROWS, width),
            rows_of(GROUPS * EXTRA, width),
            rows_of(BLOCK, width),
            whole((width, width)),
            whole((width, ff)),
            whole((ff, width)),
            whole((1, width)),
        ],
        out_specs=[
            rows_of(ROWS, width),
            rows_of(ROWS, width),
            rows_of(2 * GROUPS * EXTRA, width),
            whole((width, ff)),
            whole((width, width)),
            whole((1, width)),
        ],
        out_shape=[
            shape_of(F32, total, width),
            shape_of(BF, total, width),
            shape_of(BF, 2 * groups * EXTRA, width),
            shape_of(BF, width, ff),
            shape_of(BF, width, width),
            shape_of(F32, 1, width),
        ],
        scratch_shapes=[
            pltpu.VMEM((width, ff), F32),
            pltpu.VMEM((width, width), F32),
            pltpu.VMEM((GROUPS * EXTRA, width), F32),
        ],
        compiler_params=params(),
        name="backward",
    )(slope, grad_combined, residual, attended, attended_extra, memory_grad, out_weight, up_weight, down_weight, middle_gain)

    grad_query_rows, grad_query_extra, pair_sum, pair_memory, halo_back, memory_back = pl.pallas_call(
        attention_back_kernel,
        grid=grid,
        in_specs=[
            whole((STACK, PAIR)),
            rows_of(ROWS, width),
            rows_of(2 * GROUPS * EXTRA, width),
            rows_of(GROUPS * WINDOW, 2 * width),
            rows_of(GROUPS * PAIRS * STACK, WINDOW),
            rows_of(ROWS, width),
            rows_of(2 * GROUPS * EXTRA, width),
        ],
        out_specs=[
            rows_of(ROWS, width),
            rows_of(GROUPS * EXTRA, width),
            whole((total + HALO, 2 * width)),
            rows_of(GROUPS * 2 * MEMS, 2 * width),
            whole((HALO, 2 * width)),
            whole((2 * MEMS, 2 * width)),
        ],
        out_shape=[
            shape_of(BF, total, width),
            shape_of(BF, groups * EXTRA, width),
            shape_of(F32, total + HALO, 2 * width),
            shape_of(F32, groups * 2 * MEMS, 2 * width),
            shape_of(BF, HALO, 2 * width),
            shape_of(BF, 2 * MEMS, 2 * width),
        ],
        scratch_shapes=[pltpu.VMEM((GROUPS * EXTRA, width), F32)],
        compiler_params=params(),
        name="attention_back",
    )(head, query, query_extra, window, soft, grad_attended, grad_attended_extra)

    halo_next = shift(halo_back, "seg", -1)
    memory_halo_next = shift(memory_back, "seg", -1)

    grad_frames, grad_memory, grad_query, grad_key, grad_value, input_part = pl.pallas_call(
        projection_back_kernel,
        grid=grid,
        in_specs=[
            whole((total + HALO, 2 * width)),
            rows_of(GROUPS * 2 * MEMS, 2 * width),
            pl.BlockSpec((2 * MEMS, 2 * width), lambda i: (jnp.minimum((i + 1) * GROUPS, groups - 1), 0)),
            whole((HALO, 2 * width)),
            whole((2 * MEMS, 2 * width)),
            rows_of(ROWS, width),
            rows_of(GROUPS * EXTRA, width),
            rows_of(ROWS, width),
            rows_of(GROUPS * EXTRA, width),
            rows_of(BLOCK, width),
            rows_of(ROWS, width),
            rows_of(ROWS, width),
            whole((width, width)),
            whole((width, width)),
            whole((width, width)),
            whole((1, width)),
        ],
        out_specs=[
            rows_of(BLOCK, FRAMES, width),
            rows_of(BLOCK, width),
            whole((width, width)),
            whole((width, width)),
            whole((width, width)),
            whole((1, width)),
        ],
        out_shape=[
            shape_of(F32, slots, FRAMES, width),
            shape_of(BF, slots, width),
            shape_of(BF, width, width),
            shape_of(BF, width, width),
            shape_of(BF, width, width),
            shape_of(F32, 1, width),
        ],
        scratch_shapes=[
            pltpu.VMEM((width, width), F32),
            pltpu.VMEM((width, width), F32),
            pltpu.VMEM((width, width), F32),
            pltpu.VMEM((ROWS, width), F32),
        ],
        compiler_params=params(),
        name="projection_back",
    )(
        pair_sum, pair_memory, pair_memory, halo_next, memory_halo_next,
        grad_query_rows, grad_query_extra, shared, summary, memory, packed, grad_residual,
        query_weight, key_weight, value_weight, input_gain,
    )

    grad_down = sum_everywhere(grad_down).astype(F32)
    grad_up = sum_everywhere(grad_up).astype(F32)
    squares = sum_everywhere(jnp.concatenate([grad_out, grad_query, grad_key, grad_value], axis=0)).astype(F32)
    grad_out, grad_query, grad_key, grad_value = jnp.split(squares, 4)
    gains = sum_small(jnp.concatenate([input_part, middle_part, output_part], axis=0))
    return (
        result, memory_out, grad_frames, grad_memory,
        grad_query, grad_key, grad_value, grad_out, grad_up, grad_down,
        gains[0], gains[1], gains[2],
    )


def solution(mesh):
    rows = P(("grp", "seg"), None, None)
    singles = P(("grp", "seg"), None)
    return jax.shard_map(
        per_device,
        mesh=mesh,
        in_specs=(rows, singles, P("grp", None)) + (P(),) * 9 + (rows, singles),
        out_specs=(rows, singles, rows, singles) + (P(),) * 9,
        check_vma=False,
    )
```

time: 1040 us -> 271 us (0.26)
  waiting for transfers between devices: 412 us -> 83.5 us
  local copies, waits for them, and re-layouts: 220 us -> 22 us
  matrix products: 123 us -> 0 us
  Pallas kernels: 0 us -> 107 us
  other arithmetic: 118 us -> 18.9 us
  starting transfers between devices: 101 us -> 37.5 us
  blocking collectives: 45 us -> 0 us
  between operations: 15.4 us -> 1.47 us
    psum x1 -> x0, waiting for transfers between devices: 150 us -> none  [per_device(): lax.psum((grad_query, grad_key, grad_value, grad_input_gain, grad_up, gra...]
    all_to_all x4 -> x0, waiting for transfers between devices: 130 us -> none  [the longest x1 46.9 us: per_device(): lax.all_to_all(sent_home, 'seg', split_axis=0, concat_axis=0, tiled=True)]
    dot_general x22 -> x0, matrix products: 123 us -> none  [the longest x6 26.9 us: outer_sum(): jnp.einsum('nri,nrj->ij', operand, gradient, preferred_element_type=jnp.f...]
    pallas_call x0 -> x5, Pallas kernels: none -> 107 us  [the longest x1 33.4 us: per_device(): pl.pallas_call(forward_kernel, grid=grid, in_specs=[pl.BlockSpec(memory_s...]
    all_to_all x4 -> x0, starting transfers between devices: 81.7 us -> none  [the longest x1 59.4 us: per_device(): lax.all_to_all(attended, 'seg', split_axis=0, concat_axis=0, tiled=True)]
    reshape x6 -> x0, local copies, waits for them, and re-layouts: 52 us -> none  [the longest x1 12.3 us: per_device(): grad_keys.reshape(rows, key_count, model_width)]
    ppermute x8 -> x39, waiting for transfers between devices: 131 us -> 83.5 us  [the longest x35 79.7 us: swap(): return lax.ppermute(values, axis, [(i, i ^ bit) for i in range(size)])]
    psum x1 -> x0, blocking collectives: 45 us -> none  [per_device(): lax.psum((grad_query, grad_key, grad_value, grad_input_gain, grad_up, gra...]
  transfers between devices with their start and end apart: 13 -> 39, of which waited for: 8 -> 21; matrix products, arithmetic and copies ran while one was open for 11% -> 12% of each run, Pallas kernels for 0% -> 16%
where the time goes in v1:
time: 271 us; the launch traced here: 270 us
  Pallas kernels  107 us (39%)
  waiting for transfers between devices  83.5 us (31%)
  starting transfers between devices  37.5 us (14%)
  local copies, waits for them, and re-layouts  22 us (8%)
  other arithmetic  18.9 us (7%)
    ppermute x35, waiting for transfers between devices, swap(): return lax.ppermute(values, axis, [(i, i ^ bit) for i in range(size)])  79.7 us
    pallas_call x1, Pallas kernels, per_device(): pl.pallas_call(forward_kernel, grid=grid, in_specs=[pl.BlockSpec(memory_s...  33.4 us
    ppermute x35, starting transfers between devices, swap(): return lax.ppermute(values, axis, [(i, i ^ bit) for i in range(size)])  29.6 us
    pallas_call x1, Pallas kernels, per_device(): pl.pallas_call(attention_back_kernel, grid=grid, in_specs=[whole((STACK,...  27.1 us
    pallas_call x1, Pallas kernels, per_device(): pl.pallas_call(backward_kernel, grid=grid, in_specs=[rows_of(ROWS, ff), r...  22 us
    pallas_call x1, Pallas kernels, per_device(): pl.pallas_call(projection_back_kernel, grid=grid, in_specs=[whole((total...  16.5 us
    unnamed x37, local copies, waits for them, and re-layouts  15.8 us
    ppermute x4, starting transfers between devices, shift(): lax.ppermute(values, axis, [(i, (i + by) % size) for i in range(size)])  7.85 us
  transfers between devices with their start and end apart: 39, of which 21 were waited for; matrix products, arithmetic and copies ran while one was open for 12% of the time, Pallas kernels for 16%

profile of v1, /device:TPU:0, one launch (start us, length us, event | category | flops | bytes accessed | tf_op | source)
XLA Modules:
  0.0 270.1 jit_solution(302190640609807937)
XLA Ops:
  0.7 2.2 copy.37.frames.before
  2.8 3.0 %collective-permute-start = (bf16[2,20,512]{2,1,0:T(8,128)(2,1)S(1)}, bf16[2,20,512]{2,1,0:T(8,128)(2,1)S(1)}, u32[]{:S(2)}, u32[]{:S(2)}) collective-permute-start(bf16[2,20,512]{2,1,0:T(8,128)(2,1)S(1)} %slice.20), channel_id=1, source_target_pairs={{0,1},{1,2},{2,3},{3,4},{4,5},{5,6},{6,7},{7,8},{8,9},{9,10},{10,1... | collective-permute-start | bytes 122888 | tf_op jit(solution)/shard_map/ppermute | solution.py:443
  10.7 3.1 %collective-permute-done.1.memory_halo = bf16[8,512]{1,0:T(8,128)(2,1)S(1)} collective-permute-done((bf16[8,512]{1,0:T(8,128)(2,1)S(1)}, bf16[8,512]{1,0:T(8,128)(2,1)S(1)}, u32[]{:S(2)}, u32[]{:S(2)}) %collective-permute-start.1) | collective-permute-done | bytes 8224 | tf_op jit(solution)/shard_map/ppermute | solution.py:443
  14.4 7.8 %project.1 = (bf16[1280,512]{1,0:T(8,128)(2,1)}, bf16[1280,512]{1,0:T(8,128)(2,1)}, f32[128,512]{1,0:T(8,128)}, bf16[1280,512]{1,0:T(8,128)(2,1)}, bf16[256,512]{1,0:T(8,128)(2,1)}, /*index=5*/bf16[2048,1024]{1,0:T(8,128)(2,1)}) custom-call(bf16[64,20,512]{2,1,0:T(8,128)(2,1)} %copy-done, bf16[64,20,512]{2,1,0:T(8,128)(2,1)} %copy-done, ...), custom_call_target="tpu_custom_call" | custom-call | tf_op jit(solution)/shard_map/project/pallas_call | solution.py:500
  22.3 33.4 %forward.1 = (bf16[1280,512]{1,0:T(8,128)(2,1)}, bf16[128,512]{1,0:T(8,128)(2,1)}, bf16[11264,128]{1,0:T(8,128)(2,1)}, f32[1280,512]{1,0:T(8,128)}, bf16[1280,20...) custom-call(s32[64]{0:T(128)} %fusion.3.position, ...), custom_call_target="tpu_custom_call" | custom-call | tf_op jit(solution)/shard_map/forward/pallas_call | solution.py:537
  55.7 22.0 %backward.1 = (f32[1280,512]{1,0:T(8,128)}, bf16[1280,512]{1,0:T(8,128)(2,1)}, bf16[256,512]{1,0:T(8,128)(2,1)}, bf16[512,2048]{1,0:T(8,128)(2,1)}, bf16[512,512]{1,0:T(8,128)(2,1)}, /*index=5*/f32[1,512]{1,0:T(1,128)}) custom-call(bf16[1280,2048]{1,0:T(8,128)(2,1)} %get-tuple-element.54.slope, f32[1280,512]{1,0:T(8,128)} %get-tuple-element.55.grad_combined, ...), custom_call_target="tpu_custom_call" | custom-call | tf_op jit(solution)/shard_map/backward/pallas_call | solution.py:593
  79.3 27.1 %attention_back.1 = (bf16[1280,512]{1,0:T(8,128)(2,1)}, bf16[128,512]{1,0:T(8,128)(2,1)}, f32[1320,1024]{1,0:T(8,128)}, f32[128,1024]{1,0:T(8,128)}, bf16[40,1024]{1,0:T(8,128)(2,1)}, /*index=5*/bf16[8,1024]{1,0:T(8,128)(2,1)}) custom-call(bf16[176,128]{1,0:T(8,128)(2,1)} %constant.152.clone.head, bf16[1280,512]{1,0:T(8,128)(2,1)} %get-tuple-element.47.query, ...), custom_call_target="tpu_custom_call" | custom-call | tf_op jit(solution)/shard_map/attention_back/pallas_call | solution.py:633
  107.5 2.3 collective-permute-start.3
  112.3 16.5 %projection_back.1 = (f32[64,20,512]{2,1,0:T(8,128)}, bf16[64,512]{1,0:T(8,128)(2,1)}, bf16[512,512]{1,0:T(8,128)(2,1)}, bf16[512,512]{1,0:T(8,128)(2,1)}, bf16[512,512]{1,0:T(8,128)(2,1)}, /*index=5*/f32[1,512]{1,0:T(1,128)}) custom-call(f32[1320,1024]{1,0:T(8,128)} %get-tuple-element.61.pair_sum, f32[128,1024]{1,0:T(8,128)} %get-tuple-element.62.pair_memory.memory_next, ...), custom_call_target="tpu_custom_call" | custom-call | tf_op jit(solution)/shard_map/projection_back/pallas_call | solution.py:669
  139.5 9.0 %collective-permute-done.15 = bf16[128,2048]{1,0:T(8,128)(2,1)S(1)} collective-permute-done((bf16[128,2048]{1,0:T(8,128)(2,1)S(1)}, bf16[128,2048]{1,0:T(8,128)(2,1)S(1)}, u32[]{:S(2)}, u32[]{:S(2)}) %collective-permute-start.15) | collective-permute-done | bytes 524320 | tf_op jit(solution)/shard_map/ppermute | solution.py:448
  148.7 11.0 %collective-permute-done.25 = bf16[512,512]{1,0:T(8,128)(2,1)S(1)} collective-permute-done((bf16[512,512]{1,0:T(8,128)(2,1)S(1)}, bf16[512,512]{1,0:T(8,128)(2,1)S(1)}, u32[]{:S(2)}, u32[]{:S(2)}) %collective-permute-start.25) | collective-permute-done | bytes 524320 | tf_op jit(solution)/shard_map/ppermute | solution.py:448
  159.9 10.0 %collective-permute-done.5 = bf16[512,512]{1,0:T(8,128)(2,1)S(1)} collective-permute-done((bf16[512,512]{1,0:T(8,128)(2,1)S(1)}, bf16[512,512]{1,0:T(8,128)(2,1)S(1)}, u32[]{:S(2)}, u32[]{:S(2)}) %collective-permute-start.5) | collective-permute-done | bytes 524320 | tf_op jit(solution)/shard_map/ppermute | solution.py:448
  172.6 5.0 %collective-permute-done.6 = bf16[256,512]{1,0:T(8,128)(2,1)S(1)} collective-permute-done((bf16[256,512]{1,0:T(8,128)(2,1)S(1)}, bf16[256,512]{1,0:T(8,128)(2,1)S(1)}, u32[]{:S(2)}, u32[]{:S(2)}) %collective-permute-start.6) | collective-permute-done | bytes 262176 | tf_op jit(solution)/shard_map/ppermute | solution.py:448
  178.0 4.2 %collective-permute-start.18 = (bf16[16,2048]{1,0:T(8,128)(2,1)S(1)}, bf16[16,2048]{1,0:T(8,128)(2,1)S(1)}, u32[]{:S(2)}, u32[]{:S(2)}) collective-permute-start(bf16[16,2048]{1,0:T(8,128)(2,1)S(1)} %constant_dynamic-slice_fusion.4), channel_id=1, source_target_pairs={{0,8},{1,9},{2,10},{3,11},{4,12},{5,13},{6,14},{7,15},{8,0},{9,1},... | collective-permute-start | bytes 196616 | tf_op jit(solution)/shard_map/ppermute | solution.py:448
  182.3 3.9 %collective-permute-done.18 = bf16[16,2048]{1,0:T(8,128)(2,1)S(1)} collective-permute-done((bf16[16,2048]{1,0:T(8,128)(2,1)S(1)}, bf16[16,2048]{1,0:T(8,128)(2,1)S(1)}, u32[]{:S(2)}, u32[]{:S(2)}) %collective-permute-start.18) | collective-permute-done | bytes 65568 | tf_op jit(solution)/shard_map/ppermute | solution.py:448
  187.5 2.3 collective-permute-done.28
  190.0 3.0 %collective-permute-start.8 = (bf16[64,512]{1,0:T(8,128)(2,1)S(1)}, bf16[64,512]{1,0:T(8,128)(2,1)S(1)}, u32[]{:S(2)}, u32[]{:S(2)}) collective-permute-start(bf16[64,512]{1,0:T(8,128)(2,1)S(1)} %constant_dynamic-slice_fusion.9), channel_id=1, source_target_pairs={{0,8},{1,9},{2,10},{3,11},{4,12},{5,13},{6,14},{7,15},{8,0},{9,1},... | collective-permute-start | bytes 196616 | tf_op jit(solution)/shard_map/ppermute | solution.py:448
  193.5 4.3 %collective-permute-done.8 = bf16[64,512]{1,0:T(8,128)(2,1)S(1)} collective-permute-done((bf16[64,512]{1,0:T(8,128)(2,1)S(1)}, bf16[64,512]{1,0:T(8,128)(2,1)S(1)}, u32[]{:S(2)}, u32[]{:S(2)}) %collective-permute-start.8) | collective-permute-done | bytes 65568 | tf_op jit(solution)/shard_map/ppermute | solution.py:448
  199.7 2.5 collective-permute-start.21
  204.4 2.8 %collective-permute-done.30 = bf16[128,512]{1,0:T(8,128)(2,1)S(1)} collective-permute-done((bf16[128,512]{1,0:T(8,128)(2,1)S(1)}, bf16[128,512]{1,0:T(8,128)(2,1)S(1)}, u32[]{:S(2)}, u32[]{:S(2)}) %collective-permute-start.30) | collective-permute-done | bytes 131104 | tf_op jit(solution)/shard_map/ppermute | solution.py:448
  211.7 3.2 %collective-permute-done.31 = bf16[256,512]{1,0:T(8,128)(2,1)S(1)} collective-permute-done((bf16[256,512]{1,0:T(8,128)(2,1)S(1)}, bf16[256,512]{1,0:T(8,128)(2,1)S(1)}, u32[]{:S(2)}, u32[]{:S(2)}) %collective-permute-start.31) | collective-permute-done | bytes 262176 | tf_op jit(solution)/shard_map/ppermute | solution.py:448
  219.2 4.6 %collective-permute-done.22 = bf16[128,2048]{1,0:T(8,128)(2,1)S(1)} collective-permute-done((bf16[128,2048]{1,0:T(8,128)(2,1)S(1)}, bf16[128,2048]{1,0:T(8,128)(2,1)S(1)}, u32[]{:S(2)}, u32[]{:S(2)}) %collective-permute-start.22) | collective-permute-done | bytes 524320 | tf_op jit(solution)/shard_map/ppermute | solution.py:448
  224.7 9.9 %collective-permute-done.32 = bf16[512,512]{1,0:T(8,128)(2,1)} collective-permute-done((bf16[512,512]{1,0:T(8,128)(2,1)S(1)}, bf16[512,512]{1,0:T(8,128)(2,1)}, u32[]{:S(2)}, u32[]{:S(2)}) %collective-permute-start.32) | collective-permute-done | bytes 524320 | tf_op jit(solution)/shard_map/ppermute | solution.py:448
  237.6 2.6 collective-permute-done.12
  240.8 2.2 collective-permute-start.36
  244.8 3.4 %collective-permute-done.37 = f32[3,512]{1,0:T(4,128)S(1)} collective-permute-done((f32[3,512]{1,0:T(4,128)S(1)}, f32[3,512]{1,0:T(4,128)S(1)}, u32[]{:S(2)}, u32[]{:S(2)}) %collective-permute-start.37) | collective-permute-done | bytes 6176 | tf_op jit(solution)/shard_map/ppermute | solution.py:448
  249.1 2.9 %copy.40 = bf16[64,20,512]{2,0,1:T(8,128)(2,1)} copy(bf16[64,20,512]{2,1,0:T(8,128)(2,1)} %get-tuple-element.94) | data formatting | bytes 2621440
  251.9 4.9 %copy.41 = f32[64,20,512]{2,0,1:T(8,128)} copy(f32[64,20,512]{2,1,0:T(8,128)} %get-tuple-element.96) | data formatting | bytes 5242880
  257.4 4.2 %fusion.1 = f32[512,2048]{1,0:T(8,128)} fusion(bf16[256,2048]{1,0:T(8,128)(2,1)} %collective-permute-done.23, bf16[256,2048]{1,0:T(8,128)(2,1)S(1)} %maximum_select_fusion.4, pred[]{:T(512)S(6)} %eq.41), kind=kLoop, calls=%fused_computation.3 | loop fusion | flops 10485760 | bytes 6291457 | tf_op jit(solution)/shard_map/convert_element_type | solution.py:721
  261.7 4.2 %fusion.2 = f32[2048,512]{1,0:T(8,128)} fusion(bf16[1024,512]{1,0:T(8,128)(2,1)} %collective-permute-done.33, bf16[1024,512]{1,0:T(8,128)(2,1)S(1)} %maximum_select_fusion.5, pred[]{:T(512)S(6)} %eq.41), kind=kLoop, calls=%fused_computation.5 | loop fusion | flops 10485760 | bytes 6291457 | tf_op jit(solution)/shard_map/convert_element_type | solution.py:720
  265.9 2.2 fusion
  268.1 2.1 fusion.5
  (148 shorter events, 46.9 us)
Async XLA Ops:
  2.8 10.9 %collective-permute-start = (bf16[2,20,512]{2,1,0:T(8,128)(2,1)S(1)}, bf16[2,20,512]{2,1,0:T(8,128)(2,1)S(1)}, u32[]{:S(2)}, u32[]{:S(2)}) collective-permute-start(bf16[2,20,512]{2,1,0:T(8,128)(2,1)S(1)} %slice.20), channel_id=1, source_target_pairs={{0,1},{1,2},{2,3},{3,4},{4,5},{5,6},{6,7},{7,8},{8,9},{9,10},{10,1... | collective-permute-start | bytes 122888 | tf_op jit(solution)/shard_map/ppermute | solution.py:443
  6.5 7.2 %collective-permute-start.1 = (bf16[8,512]{1,0:T(8,128)(2,1)S(1)}, bf16[8,512]{1,0:T(8,128)(2,1)S(1)}, u32[]{:S(2)}, u32[]{:S(2)}) collective-permute-start(bf16[8,512]{1,0:T(8,128)(2,1)S(1)} %slice.16), channel_id=1, source_target_pairs={{0,1},{1,2},{2,3},{3,4},{4,5},{5,6},{6,7},{7,8},{8,9},{9,10},{10,1... | collective-permute-start | bytes 24584 | tf_op jit(solution)/shard_map/ppermute | solution.py:443
  79.0 52.4 %collective-permute-start.14 = (bf16[256,2048]{1,0:T(8,128)(2,1)S(1)}, bf16[256,2048]{1,0:T(8,128)(2,1)}, u32[]{:S(2)}, u32[]{:S(2)}) collective-permute-start(bf16[256,2048]{1,0:T(8,128)(2,1)S(1)} %constant_dynamic-slice_fusion.8), channel_id=1, source_target_pairs={{0,16},{16,0},{1,17},{17,1},{2,18},{18,2},{3,19},{19,3},{4,20},{20... | collective-permute-start | bytes 3145736 | tf_op jit(solution)/shard_map/ppermute | solution.py:448
  110.9 24.5 %collective-permute-start.24 = (bf16[1024,512]{1,0:T(8,128)(2,1)}, bf16[1024,512]{1,0:T(8,128)(2,1)}, u32[]{:S(2)}, u32[]{:S(2)}) collective-permute-start(bf16[1024,512]{1,0:T(8,128)(2,1)} %constant_dynamic-slice_fusion.3), channel_id=1, source_target_pairs={{0,16},{16,0},{1,17},{17,1},{2,18},{18,2},{3,19},{19,3},{4,20},{20... | collective-permute-start | bytes 3145736 | tf_op jit(solution)/shard_map/ppermute | solution.py:448
  131.4 6.0 %collective-permute-start.4 = (bf16[1024,512]{1,0:T(8,128)(2,1)S(1)}, bf16[1024,512]{1,0:T(8,128)(2,1)S(1)}, u32[]{:S(2)}, u32[]{:S(2)}) collective-permute-start(bf16[1024,512]{1,0:T(8,128)(2,1)S(1)} %constant_dynamic-slice_fusion.13), channel_id=1, source_target_pairs={{0,16},{16,0},{1,17},{17,1},{2,18},{18,2},{3,19},{19,3},{4,20},{20... | collective-permute-start | bytes 3145736 | tf_op jit(solution)/shard_map/ppermute | solution.py:448
  133.6 14.9 %collective-permute-start.15 = (bf16[128,2048]{1,0:T(8,128)(2,1)S(1)}, bf16[128,2048]{1,0:T(8,128)(2,1)S(1)}, u32[]{:S(2)}, u32[]{:S(2)}) collective-permute-start(bf16[128,2048]{1,0:T(8,128)(2,1)S(1)} %constant_dynamic-slice_fusion.7), channel_id=1, source_target_pairs={{0,1},{1,0},{2,3},{3,2},{4,5},{5,4},{6,7},{7,6},{8,9},{9,8},{10,11... | collective-permute-start | bytes 1572872 | tf_op jit(solution)/shard_map/ppermute | solution.py:448
  136.9 22.7 %collective-permute-start.25 = (bf16[512,512]{1,0:T(8,128)(2,1)S(1)}, bf16[512,512]{1,0:T(8,128)(2,1)S(1)}, u32[]{:S(2)}, u32[]{:S(2)}) collective-permute-start(bf16[512,512]{1,0:T(8,128)(2,1)S(1)} %constant_dynamic-slice_fusion.2), channel_id=1, source_target_pairs={{0,1},{1,0},{2,3},{3,2},{4,5},{5,4},{6,7},{7,6},{8,9},{9,8},{10,11... | collective-permute-start | bytes 1572872 | tf_op jit(solution)/shard_map/ppermute | solution.py:448
  137.7 32.3 %collective-permute-start.5 = (bf16[512,512]{1,0:T(8,128)(2,1)S(1)}, bf16[512,512]{1,0:T(8,128)(2,1)S(1)}, u32[]{:S(2)}, u32[]{:S(2)}) collective-permute-start(bf16[512,512]{1,0:T(8,128)(2,1)S(1)} %constant_dynamic-slice_fusion.12), channel_id=1, source_target_pairs={{0,1},{1,0},{2,3},{3,2},{4,5},{5,4},{6,7},{7,6},{8,9},{9,8},{10,11... | collective-permute-start | bytes 1572872 | tf_op jit(solution)/shard_map/ppermute | solution.py:448
  148.6 21.6 %collective-permute-start.16 = (bf16[64,2048]{1,0:T(8,128)(2,1)S(1)}, bf16[64,2048]{1,0:T(8,128)(2,1)S(1)}, u32[]{:S(2)}, u32[]{:S(2)}) collective-permute-start(bf16[64,2048]{1,0:T(8,128)(2,1)S(1)} %constant_dynamic-slice_fusion.6), channel_id=1, source_target_pairs={{0,2},{1,3},{2,0},{3,1},{4,6},{5,7},{6,4},{7,5},{8,10},{9,11},{10,... | collective-permute-start | bytes 786440 | tf_op jit(solution)/shard_map/ppermute | solution.py:448
  159.9 12.1 %collective-permute-start.26 = (bf16[256,512]{1,0:T(8,128)(2,1)S(1)}, bf16[256,512]{1,0:T(8,128)(2,1)S(1)}, u32[]{:S(2)}, u32[]{:S(2)}) collective-permute-start(bf16[256,512]{1,0:T(8,128)(2,1)S(1)} %constant_dynamic-slice_fusion.1), channel_id=1, source_target_pairs={{0,2},{1,3},{2,0},{3,1},{4,6},{5,7},{6,4},{7,5},{8,10},{9,11},{10,... | collective-permute-start | bytes 786440 | tf_op jit(solution)/shard_map/ppermute | solution.py:448
  170.2 7.5 %collective-permute-start.6 = (bf16[256,512]{1,0:T(8,128)(2,1)S(1)}, bf16[256,512]{1,0:T(8,128)(2,1)S(1)}, u32[]{:S(2)}, u32[]{:S(2)}) collective-permute-start(bf16[256,512]{1,0:T(8,128)(2,1)S(1)} %constant_dynamic-slice_fusion.11), channel_id=1, source_target_pairs={{0,2},{1,3},{2,0},{3,1},{4,6},{5,7},{6,4},{7,5},{8,10},{9,11},{10,... | collective-permute-start | bytes 786440 | tf_op jit(solution)/shard_map/ppermute | solution.py:448
  170.4 7.5 %collective-permute-start.17 = (bf16[32,2048]{1,0:T(8,128)(2,1)S(1)}, bf16[32,2048]{1,0:T(8,128)(2,1)S(1)}, u32[]{:S(2)}, u32[]{:S(2)}) collective-permute-start(bf16[32,2048]{1,0:T(8,128)(2,1)S(1)} %constant_dynamic-slice_fusion.5), channel_id=1, source_target_pairs={{0,4},{1,5},{2,6},{3,7},{4,0},{5,1},{6,2},{7,3},{8,12},{9,13},{10,... | collective-permute-start | bytes 393224 | tf_op jit(solution)/shard_map/ppermute | solution.py:448
  172.0 10.1 %collective-permute-start.27 = (bf16[128,512]{1,0:T(8,128)(2,1)S(1)}, bf16[128,512]{1,0:T(8,128)(2,1)S(1)}, u32[]{:S(2)}, u32[]{:S(2)}) collective-permute-start(bf16[128,512]{1,0:T(8,128)(2,1)S(1)} %constant_dynamic-slice_fusion), channel_id=1, source_target_pairs={{0,4},{1,5},{2,6},{3,7},{4,0},{5,1},{6,2},{7,3},{8,12},{9,13},{10,... | collective-permute-start | bytes 393224 | tf_op jit(solution)/shard_map/ppermute | solution.py:448
  177.7 12.2 %collective-permute-start.7 = (bf16[128,512]{1,0:T(8,128)(2,1)S(1)}, bf16[128,512]{1,0:T(8,128)(2,1)S(1)}, u32[]{:S(2)}, u32[]{:S(2)}) collective-permute-start(bf16[128,512]{1,0:T(8,128)(2,1)S(1)} %constant_dynamic-slice_fusion.10), channel_id=1, source_target_pairs={{0,4},{1,5},{2,6},{3,7},{4,0},{5,1},{6,2},{7,3},{8,12},{9,13},{10,... | collective-permute-start | bytes 393224 | tf_op jit(solution)/shard_map/ppermute | solution.py:448
  178.0 8.3 %collective-permute-start.18 = (bf16[16,2048]{1,0:T(8,128)(2,1)S(1)}, bf16[16,2048]{1,0:T(8,128)(2,1)S(1)}, u32[]{:S(2)}, u32[]{:S(2)}) collective-permute-start(bf16[16,2048]{1,0:T(8,128)(2,1)S(1)} %constant_dynamic-slice_fusion.4), channel_id=1, source_target_pairs={{0,8},{1,9},{2,10},{3,11},{4,12},{5,13},{6,14},{7,15},{8,0},{9,1},... | collective-permute-start | bytes 196616 | tf_op jit(solution)/shard_map/ppermute | solution.py:448
  182.2 7.6 %collective-permute-start.28 = (bf16[64,512]{1,0:T(8,128)(2,1)S(1)}, bf16[64,512]{1,0:T(8,128)(2,1)S(1)}, u32[]{:S(2)}, u32[]{:S(2)}) collective-permute-start(bf16[64,512]{1,0:T(8,128)(2,1)S(1)} %constant_dynamic-slice_fusion.14), channel_id=1, source_target_pairs={{0,8},{1,9},{2,10},{3,11},{4,12},{5,13},{6,14},{7,15},{8,0},{9,1},... | collective-permute-start | bytes 196616 | tf_op jit(solution)/shard_map/ppermute | solution.py:448
  186.2 7.2 %collective-permute-start.19 = (bf16[16,2048]{1,0:T(8,128)(2,1)S(1)}, bf16[16,2048]{1,0:T(8,128)(2,1)S(1)}, u32[]{:S(2)}, u32[]{:S(2)}) collective-permute-start(bf16[16,2048]{1,0:T(8,128)(2,1)S(1)} %add_convert_fusion.13), channel_id=1, source_target_pairs={{0,8},{1,9},{2,10},{3,11},{4,12},{5,13},{6,14},{7,15},{8,0},{9,1},... | collective-permute-start | bytes 196616 | tf_op jit(solution)/shard_map/ppermute | solution.py:448
  189.8 12.4 %collective-permute-start.29 = (bf16[64,512]{1,0:T(8,128)(2,1)S(1)}, bf16[64,512]{1,0:T(8,128)(2,1)S(1)}, u32[]{:S(2)}, u32[]{:S(2)}) collective-permute-start(bf16[64,512]{1,0:T(8,128)(2,1)S(1)} %add_convert_fusion.12), channel_id=1, source_target_pairs={{0,8},{1,9},{2,10},{3,11},{4,12},{5,13},{6,14},{7,15},{8,0},{9,1},... | collective-permute-start | bytes 196616 | tf_op jit(solution)/shard_map/ppermute | solution.py:448
  190.0 7.9 %collective-permute-start.8 = (bf16[64,512]{1,0:T(8,128)(2,1)S(1)}, bf16[64,512]{1,0:T(8,128)(2,1)S(1)}, u32[]{:S(2)}, u32[]{:S(2)}) collective-permute-start(bf16[64,512]{1,0:T(8,128)(2,1)S(1)} %constant_dynamic-slice_fusion.9), channel_id=1, source_target_pairs={{0,8},{1,9},{2,10},{3,11},{4,12},{5,13},{6,14},{7,15},{8,0},{9,1},... | collective-permute-start | bytes 196616 | tf_op jit(solution)/shard_map/ppermute | solution.py:448
  193.4 6.2 %collective-permute-start.20 = (bf16[32,2048]{1,0:T(8,128)(2,1)S(1)}, bf16[32,2048]{1,0:T(8,128)(2,1)S(1)}, u32[]{:S(2)}, u32[]{:S(2)}) collective-permute-start(bf16[32,2048]{1,0:T(8,128)(2,1)S(1)} %maximum_select_fusion.13), channel_id=1, source_target_pairs={{0,4},{1,5},{2,6},{3,7},{4,0},{5,1},{6,2},{7,3},{8,12},{9,13},{10,... | collective-permute-start | bytes 393224 | tf_op jit(solution)/shard_map/ppermute | solution.py:448
  199.7 9.2 %collective-permute-start.21 = (bf16[64,2048]{1,0:T(8,128)(2,1)S(1)}, bf16[64,2048]{1,0:T(8,128)(2,1)S(1)}, u32[]{:S(2)}, u32[]{:S(2)}) collective-permute-start(bf16[64,2048]{1,0:T(8,128)(2,1)S(1)} %maximum_select_fusion.10), channel_id=1, source_target_pairs={{0,2},{1,3},{2,0},{3,1},{4,6},{5,7},{6,4},{7,5},{8,10},{9,11},{10,... | collective-permute-start | bytes 786440 | tf_op jit(solution)/shard_map/ppermute | solution.py:448
  203.6 6.8 %collective-permute-start.10 = (bf16[128,512]{1,0:T(8,128)(2,1)S(1)}, bf16[128,512]{1,0:T(8,128)(2,1)S(1)}, u32[]{:S(2)}, u32[]{:S(2)}) collective-permute-start(bf16[128,512]{1,0:T(8,128)(2,1)S(1)} %maximum_select_fusion.12), channel_id=1, source_target_pairs={{0,4},{1,5},{2,6},{3,7},{4,0},{5,1},{6,2},{7,3},{8,12},{9,13},{10,... | collective-permute-start | bytes 393224 | tf_op jit(solution)/shard_map/ppermute | solution.py:448
  207.3 7.7 %collective-permute-start.31 = (bf16[256,512]{1,0:T(8,128)(2,1)S(1)}, bf16[256,512]{1,0:T(8,128)(2,1)S(1)}, u32[]{:S(2)}, u32[]{:S(2)}) collective-permute-start(bf16[256,512]{1,0:T(8,128)(2,1)S(1)} %maximum_select_fusion.11), channel_id=1, source_target_pairs={{0,2},{1,3},{2,0},{3,1},{4,6},{5,7},{6,4},{7,5},{8,10},{9,11},{10,... | collective-permute-start | bytes 786440 | tf_op jit(solution)/shard_map/ppermute | solution.py:448
  209.0 14.8 %collective-permute-start.22 = (bf16[128,2048]{1,0:T(8,128)(2,1)S(1)}, bf16[128,2048]{1,0:T(8,128)(2,1)S(1)}, u32[]{:S(2)}, u32[]{:S(2)}) collective-permute-start(bf16[128,2048]{1,0:T(8,128)(2,1)S(1)} %maximum_select_fusion.7), channel_id=1, source_target_pairs={{0,1},{1,0},{2,3},{3,2},{4,5},{5,4},{6,7},{7,6},{8,9},{9,8},{10,11... | collective-permute-start | bytes 1572872 | tf_op jit(solution)/shard_map/ppermute | solution.py:448
  210.5 7.2 %collective-permute-start.11 = (bf16[256,512]{1,0:T(8,128)(2,1)S(1)}, bf16[256,512]{1,0:T(8,128)(2,1)S(1)}, u32[]{:S(2)}, u32[]{:S(2)}) collective-permute-start(bf16[256,512]{1,0:T(8,128)(2,1)S(1)} %maximum_select_fusion.9), channel_id=1, source_target_pairs={{0,2},{1,3},{2,0},{3,1},{4,6},{5,7},{6,4},{7,5},{8,10},{9,11},{10,... | collective-permute-start | bytes 786440 | tf_op jit(solution)/shard_map/ppermute | solution.py:448
  215.2 19.4 %collective-permute-start.32 = (bf16[512,512]{1,0:T(8,128)(2,1)S(1)}, bf16[512,512]{1,0:T(8,128)(2,1)}, u32[]{:S(2)}, u32[]{:S(2)}) collective-permute-start(bf16[512,512]{1,0:T(8,128)(2,1)S(1)} %maximum_select_fusion.8), channel_id=1, source_target_pairs={{0,1},{1,0},{2,3},{3,2},{4,5},{5,4},{6,7},{7,6},{8,9},{9,8},{10,11... | collective-permute-start | bytes 1572872 | tf_op jit(solution)/shard_map/ppermute | solution.py:448
  218.0 22.2 %collective-permute-start.12 = (bf16[512,512]{1,0:T(8,128)(2,1)S(1)}, bf16[512,512]{1,0:T(8,128)(2,1)S(1)}, u32[]{:S(2)}, u32[]{:S(2)}) collective-permute-start(bf16[512,512]{1,0:T(8,128)(2,1)S(1)} %maximum_select_fusion.6), channel_id=1, source_target_pairs={{0,1},{1,0},{2,3},{3,2},{4,5},{5,4},{6,7},{7,6},{8,9},{9,8},{10,11... | collective-permute-start | bytes 1572872 | tf_op jit(solution)/shard_map/ppermute | solution.py:448
  224.1 33.4 %collective-permute-start.23 = (bf16[256,2048]{1,0:T(8,128)(2,1)S(1)}, bf16[256,2048]{1,0:T(8,128)(2,1)}, u32[]{:S(2)}, u32[]{:S(2)}) collective-permute-start(bf16[256,2048]{1,0:T(8,128)(2,1)S(1)} %maximum_select_fusion.4), channel_id=1, source_target_pairs={{0,16},{16,0},{1,17},{17,1},{2,18},{18,2},{3,19},{19,3},{4,20},{20... | collective-permute-start | bytes 3145736 | tf_op jit(solution)/shard_map/ppermute | solution.py:448
  224.2 12.1 %collective-permute-start.34 = (f32[3,512]{1,0:T(4,128)S(1)}, f32[3,512]{1,0:T(4,128)S(1)}, u32[]{:S(2)}, u32[]{:S(2)}) collective-permute-start(f32[3,512]{1,0:T(4,128)S(1)} %pad_maximum_fusion), channel_id=1, source_target_pairs={{0,16},{16,0},{1,17},{17,1},{2,18},{18,2},{3,19},{19,3},{4,20},{20... | collective-permute-start | bytes 18440 | tf_op jit(solution)/shard_map/ppermute | solution.py:448
  236.2 25.5 %collective-permute-start.33 = (bf16[1024,512]{1,0:T(8,128)(2,1)S(1)}, bf16[1024,512]{1,0:T(8,128)(2,1)}, u32[]{:S(2)}, u32[]{:S(2)}) collective-permute-start(bf16[1024,512]{1,0:T(8,128)(2,1)S(1)} %maximum_select_fusion.5), channel_id=1, source_target_pairs={{0,16},{16,0},{1,17},{17,1},{2,18},{18,2},{3,19},{19,3},{4,20},{20... | collective-permute-start | bytes 3145736 | tf_op jit(solution)/shard_map/ppermute | solution.py:448
  240.7 25.2 %collective-permute-start.13 = (bf16[1024,512]{1,0:T(8,128)(2,1)S(1)}, bf16[1024,512]{1,0:T(8,128)(2,1)}, u32[]{:S(2)}, u32[]{:S(2)}) collective-permute-start(bf16[1024,512]{1,0:T(8,128)(2,1)S(1)} %maximum_select_fusion.3), channel_id=1, source_target_pairs={{0,16},{16,0},{1,17},{17,1},{2,18},{18,2},{3,19},{19,3},{4,20},{20... | collective-permute-start | bytes 3145736 | tf_op jit(solution)/shard_map/ppermute | solution.py:448
  248.2 8.6 %collective-permute-start.38 = (f32[3,512]{1,0:T(4,128)S(1)}, f32[3,512]{1,0:T(4,128)S(1)}, u32[]{:S(2)}, u32[]{:S(2)}) collective-permute-start(f32[3,512]{1,0:T(4,128)S(1)} %add.216), channel_id=1, source_target_pairs={{0,8},{1,9},{2,10},{3,11},{4,12},{5,13},{6,14},{7,15},{8,0},{9,1},... | collective-permute-start | bytes 18440 | tf_op jit(solution)/shard_map/ppermute | solution.py:448
  (22 other events, 145.0 us)

commit v2 on v0

v2 whole, which is shorter than its diff:
```python
import jax
import jax.numpy as jnp
import numpy as np
from jax import lax
from jax.experimental import pallas as pl
from jax.experimental.pallas import tpu as pltpu
from jax.sharding import PartitionSpec as P

HEADS = 8
HDIM = 64
SEGLEN = 16
RIGHT = 4
LEFT = 30
MEMS = 4
FRAMES = RIGHT + SEGLEN

GROUP = 4
TILE = 128
PART = 8
PART_FRAMES = FRAMES * PART
PART_ROWS = PART_FRAMES + 2 * PART
PART_TILES = PART // GROUP * TILE
CARRY = 48
CARRY_FRAMES = 2 * FRAMES
BLOCK = 16
PARTS = BLOCK // PART
ROWS = BLOCK * FRAMES
FULL = PARTS * PART_ROWS
TILES = PARTS * PART_TILES
PAIRS = HEADS // 2
PAIR = 2 * HDIM

EPSILON = 1e-05
MASKED_SCORE = -1e30
FAR = 1 << 20

BF = jnp.bfloat16
F32 = jnp.float32
VMEM_LIMIT = 60 * 1024 * 1024


def dot(a, b):
    return lax.dot_general(a, b, (((1,), (0,)), ((), ())), preferred_element_type=F32)


def dot_back(a, b):
    return lax.dot_general(a, b, (((1,), (1,)), ((), ())), preferred_element_type=F32)


def dot_outer(a, b):
    return lax.dot_general(a, b, (((0,), (0,)), ((), ())), preferred_element_type=F32)


def tables():
    pick_query = np.zeros((PART_TILES, PART_ROWS), np.float32)
    pick_key = np.zeros((PART_TILES, PART_ROWS + CARRY), np.float32)
    pick_carry = np.zeros((CARRY, PART_ROWS), np.float32)
    for group in range(PART // GROUP):
        for row in range(GROUP * FRAMES):
            segment = group * GROUP + row // FRAMES
            pick_query[group * TILE + row, row % FRAMES * PART + segment] = 1
        for row in range(GROUP):
            pick_query[group * TILE + GROUP * FRAMES + row, PART_FRAMES + group * GROUP + row] = 1
        for row in range((GROUP + 2) * FRAMES):
            segment, frame = group * GROUP - 2 + row // FRAMES, row % FRAMES
            column = frame * PART + segment if segment >= 0 else PART_ROWS + frame * 2 + segment + 2
            pick_key[group * TILE + row, column] = 1
        for row in range(GROUP + MEMS):
            segment = group * GROUP - MEMS + row
            column = PART_FRAMES + segment if segment >= 0 else PART_ROWS + CARRY_FRAMES + segment + MEMS
            pick_key[group * TILE + (GROUP + 2) * FRAMES + row, column] = 1
    for frame in range(FRAMES):
        for back in range(2):
            pick_carry[frame * 2 + back, frame * PART + PART - 2 + back] = 1
    for back in range(MEMS):
        pick_carry[CARRY_FRAMES + back, PART_FRAMES + PART - MEMS + back] = 1
    row = np.arange(TILE)
    is_summary = (row >= GROUP * FRAMES) & (row < GROUP * FRAMES + GROUP)
    segment = np.where(is_summary, row - GROUP * FRAMES, np.where(row < GROUP * FRAMES, row // FRAMES, 0))
    is_memory = row >= (GROUP + 2) * FRAMES
    key_segment = np.where(is_memory, row - (GROUP + 2) * FRAMES - MEMS, row // FRAMES - 2)
    within = row % FRAMES
    is_right = ~is_memory & (within < RIGHT)
    behind = segment[None, :] - key_segment[:, None]
    late = (within >= RIGHT + 2 * SEGLEN - LEFT)[:, None]
    frame_ok = (behind == 0) | (~is_right[:, None] & ((behind == 1) | ((behind == 2) & late)))
    memory_ok = (behind >= 1) & (behind <= MEMS) & ~is_summary[None, :]
    need = np.where(np.where(is_memory[:, None], memory_ok, frame_ok), behind, FAR).astype(np.int32)
    segment_of = np.ascontiguousarray(np.broadcast_to(segment[None, :], (TILE, TILE))).astype(np.int32)
    return pick_query, pick_key, pick_carry, need, segment_of


def row_stats(values):
    centered = values - jnp.mean(values, axis=-1, keepdims=True)
    spread = jnp.mean(centered * centered, axis=-1, keepdims=True)
    scale = lax.rsqrt(spread + EPSILON)
    return centered * scale, scale


def norm_back(unit, scale, gain, gradient):
    gained = gradient * gain
    along = jnp.mean(gained * unit, axis=-1, keepdims=True)
    grad = scale * (gained - jnp.mean(gained, axis=-1, keepdims=True) - unit * along)
    return grad, jnp.sum(gradient * unit, axis=0, keepdims=True)


def by_part(slabs):
    frames, _, width = slabs.shape
    return [slabs[:, p * PART : (p + 1) * PART].reshape(frames * PART, width) for p in range(PARTS)]


def by_frame(parts):
    return jnp.concatenate([part.reshape(FRAMES, PART, part.shape[1]) for part in parts], axis=1)


def project_kernel(
    frames, memory, halo, gain, query_w, key_w, value_w, pick_query, pick_key, pick_carry,
    query_rows, key_rows, query, window,
    carry_rows, carry_pair,
):
    step = pl.program_id(0)
    width = query_w.shape[0]

    @pl.when(step == 0)
    def _():
        raw = halo[...].astype(F32)
        unit, _ = row_stats(raw)
        is_frame = lax.broadcasted_iota(jnp.int32, raw.shape, 0) < CARRY_FRAMES
        carried = jnp.where(is_frame, unit * gain[...], raw).astype(BF)
        carry_rows[...] = carried
        carry_pair[:, :width] = dot(carried, key_w[...]).astype(BF)
        carry_pair[:, width:] = dot(carried, value_w[...]).astype(BF)

    memories = memory[...].astype(F32)
    for p, part in enumerate(by_part(frames[...].astype(F32))):
        unit, _ = row_stats(part)
        normed = unit * gain[...]
        mean = normed[RIGHT * PART : (RIGHT + 1) * PART]
        for f in range(RIGHT + 1, FRAMES):
            mean = mean + normed[f * PART : (f + 1) * PART]
        mean = mean * (1.0 / SEGLEN)
        blank = jnp.zeros_like(mean)
        asks = jnp.concatenate([normed, mean, blank], axis=0).astype(BF)
        keys = jnp.concatenate([normed, memories[p * PART : (p + 1) * PART], blank], axis=0).astype(BF)
        query_rows[p * PART_ROWS : (p + 1) * PART_ROWS] = asks
        at = p * (PART_ROWS + CARRY)
        key_rows[at : at + PART_ROWS] = keys
        key_rows[at + PART_ROWS : at + PART_ROWS + CARRY] = carry_rows[...]
        asked = (dot(asks, query_w[...]) * 0.125).astype(BF)
        query[p * PART_TILES : (p + 1) * PART_TILES] = dot(pick_query[...], asked).astype(BF)
        pair = jnp.concatenate([dot(keys, key_w[...]), dot(keys, value_w[...])], axis=1).astype(BF)
        both = jnp.concatenate([pair, carry_pair[...]], axis=0)
        window[p * PART_TILES : (p + 1) * PART_TILES] = dot(pick_key[...], both).astype(BF)
        carry_rows[...] = dot(pick_carry[...], keys).astype(BF)
        carry_pair[...] = dot(pick_carry[...], pair).astype(BF)


def two_heads(rows):
    low = lax.broadcasted_iota(jnp.int32, (1, PAIR), 1) < HDIM
    wide = rows.astype(F32)
    return jnp.concatenate([jnp.where(low, wide, 0.0), jnp.where(low, 0.0, wide)], axis=0).astype(BF)


def of_two_heads(columns):
    return jnp.concatenate([columns[:HDIM, :TILE], columns[HDIM:, TILE:]], axis=0).astype(BF)


def gelu_parts(lifted):
    bell = jnp.exp(lifted * lifted * -0.5) * 0.3989422804014327
    share = 0.5 + 0.5 * lax.erf(lifted * 0.7071067811865476)
    return lifted * share, share + lifted * bell


def forward_kernel(
    position, need, segment_of, unpick_query, query, window, frames, out_grad,
    out_w, up_w, down_w, middle_gain, output_gain,
    attended, soft, residual_out, slope, grad_combined_out, result, memory_out, grad_down, grad_gain,
    turned, hidden, grad_ff_rows,
):
    step = pl.program_id(0)
    steps = pl.num_programs(0)
    width = out_w.shape[0]
    ff = up_w.shape[1]
    for p in range(PARTS):
        for g in range(PART // GROUP):
            tile = p * (PART // GROUP) + g
            first = step * BLOCK + tile * GROUP
            column = segment_of[...]
            at = jnp.where(
                column < 2,
                jnp.where(column == 0, position[first], position[first + 1]),
                jnp.where(column == 2, position[first + 2], position[first + 3]),
            )
            bias = jnp.where(at >= need[...], 0.0, MASKED_SCORE)
            bias = jnp.concatenate([bias, bias], axis=1)
            rows = slice(tile * TILE, (tile + 1) * TILE)
            for h in range(PAIRS):
                lanes = slice(h * PAIR, (h + 1) * PAIR)
                keys = window[rows, lanes]
                values = window[rows, width + h * PAIR : width + (h + 1) * PAIR]
                scores = dot_back(keys, two_heads(query[rows, lanes])) + bias
                powers = jnp.exp(scores - jnp.max(scores, axis=0, keepdims=True))
                soft_low = (powers * (1.0 / jnp.sum(powers, axis=0, keepdims=True))).astype(BF)
                spot = (tile * PAIRS + h) * TILE
                soft[spot : spot + TILE] = soft_low
                turned[lanes, g * TILE : (g + 1) * TILE] = of_two_heads(dot_outer(values, soft_low))
        attended[p * PART_ROWS : (p + 1) * PART_ROWS] = dot_back(unpick_query[...], turned[...]).astype(BF)
    branch = dot(attended[...], out_w[...])
    own = frames[...].astype(F32)
    residual, memory_rows = [], []
    for p, part in enumerate(by_part(own)):
        at = p * PART_ROWS
        residual.append(part + branch[at : at + PART_FRAMES])
        memory_rows.append(branch[at + PART_FRAMES : at + PART_FRAMES + PART])
    memory_out[...] = jnp.concatenate(memory_rows, axis=0).astype(BF)
    residual = jnp.concatenate(residual, axis=0)
    residual_out[...] = residual
    unit, _ = row_stats(residual)
    middle = (unit * middle_gain[...]).astype(BF)
    combined = residual
    span = pl.ds(pl.multiple_of(step * ROWS, ROWS), ROWS)
    for c in range(ff // width):
        columns = slice(c * width, (c + 1) * width)
        part, turn = gelu_parts(dot(middle, up_w[:, columns]))
        part = part.astype(BF)
        hidden[span, columns] = part
        slope[:, columns] = turn.astype(BF)
        combined = combined + dot(part, down_w[columns])
    unit, scale = row_stats(combined)
    final = unit * output_gain[...]
    result[...] = by_frame([final[p * PART_FRAMES : (p + 1) * PART_FRAMES] for p in range(PARTS)]).astype(BF)
    pulled = jnp.concatenate(by_part(out_grad[...].astype(F32)), axis=0)
    grad_combined, gain_part = norm_back(unit, scale, output_gain[...], pulled)
    grad_combined_out[...] = grad_combined
    grad_ff_rows[span] = grad_combined.astype(BF)

    @pl.when(step == 0)
    def _():
        grad_gain[...] = gain_part

    @pl.when(step > 0)
    def _():
        grad_gain[...] += gain_part

    @pl.when(step == steps - 1)
    def _():
        for c in range(ff // width):
            columns = slice(c * width, (c + 1) * width)
            grad_down[columns] = dot_outer(hidden[:, columns], grad_ff_rows[...]).astype(BF)


def backward_kernel(
    slope, grad_combined, residual, attended, memory_grad, out_w, up_w, down_w, middle_gain,
    grad_residual_out, grad_attended, grad_up_out, grad_gain,
    lifted, middle_rows, out_sum,
):
    step = pl.program_id(0)
    steps = pl.num_programs(0)
    width = out_w.shape[0]
    ff = up_w.shape[1]
    span = pl.ds(pl.multiple_of(step * ROWS, ROWS), ROWS)
    unit, scale = row_stats(residual[...])
    middle_rows[span] = (unit * middle_gain[...]).astype(BF)
    grad_combined_rows = grad_combined[...]
    grad_ff = grad_combined_rows.astype(BF)
    grad_middle = jnp.zeros_like(unit)
    for c in range(ff // width):
        columns = slice(c * width, (c + 1) * width)
        part = (dot_back(grad_ff, down_w[columns]) * slope[:, columns].astype(F32)).astype(BF)
        lifted[span, columns] = part
        grad_middle = grad_middle + dot_back(part, up_w[:, columns])
    grad_norm, gain_part = norm_back(unit, scale, middle_gain[...], grad_middle)
    grad_residual = grad_combined_rows + grad_norm
    grad_residual_out[...] = grad_residual
    memory_rows = memory_grad[...].astype(F32)
    blank = jnp.zeros((PART, width), F32)
    grad_branch = []
    for p in range(PARTS):
        grad_branch += [grad_residual[p * PART_FRAMES : (p + 1) * PART_FRAMES], memory_rows[p * PART : (p + 1) * PART], blank]
    grad_branch = jnp.concatenate(grad_branch, axis=0).astype(BF)
    grad_attended[...] = dot_back(grad_branch, out_w[...]).astype(BF)
    out_part = dot_outer(attended[...], grad_branch)

    @pl.when(step == 0)
    def _():
        grad_gain[...] = gain_part
        out_sum[...] = out_part

    @pl.when(step > 0)
    def _():
        grad_gain[...] += gain_part
        out_sum[...] += out_part

    @pl.when(step == steps - 1)
    def _():
        grad_up_out[:, ff:] = out_sum[...].astype(BF)
        for c in range(ff // width):
            columns = slice(c * width, (c + 1) * width)
            grad_up_out[:, columns] = dot_outer(middle_rows[...], lifted[:, columns]).astype(BF)


def attention_back_kernel(
    pick_query, unpick_query, unpick_key, query_rows, key_rows, query, window, soft, grad_attended,
    grad_query_rows, grad_pair, grad_carry, grad_projections,
    turned, grad_window, query_sum, pair_sum,
):
    step = pl.program_id(0)
    steps = pl.num_programs(0)
    width = query.shape[1]

    @pl.when(step == 0)
    def _():
        query_sum[...] = jnp.zeros_like(query_sum)
        pair_sum[...] = jnp.zeros_like(pair_sum)

    for p in range(PARTS):
        pulled = dot(pick_query[...], grad_attended[p * PART_ROWS : (p + 1) * PART_ROWS]).astype(BF)
        for g in range(PART // GROUP):
            tile = p * (PART // GROUP) + g
            rows = slice(tile * TILE, (tile + 1) * TILE)
            spread = slice(g * TILE, (g + 1) * TILE)
            for h in range(PAIRS):
                lanes = slice(h * PAIR, (h + 1) * PAIR)
                value_lanes = slice(width + h * PAIR, width + (h + 1) * PAIR)
                keys = window[rows, lanes]
                values = window[rows, value_lanes]
                asks = two_heads(query[rows, lanes])
                grads = two_heads(pulled[spread, lanes])
                spot = (tile * PAIRS + h) * TILE
                soft_low = soft[spot : spot + TILE]
                soft_wide = soft_low.astype(F32)
                weighted = dot_back(values, grads) * soft_wide
                grad_scores = (weighted - soft_wide * jnp.sum(weighted, axis=0, keepdims=True)).astype(BF)
                grad_window[spread, lanes] = dot(grad_scores, asks).astype(BF)
                grad_window[spread, value_lanes] = dot(soft_low, grads).astype(BF)
                turned[lanes, spread] = of_two_heads(dot_outer(keys, grad_scores))
        part = slice(p * PART_ROWS, (p + 1) * PART_ROWS)
        grad_asks = dot_back(unpick_query[...], turned[...]).astype(BF)
        grad_query_rows[part] = grad_asks
        both = dot(unpick_key[...], grad_window[...]).astype(BF)
        grad_pair[part] = both[:PART_ROWS]
        grad_carry[p * CARRY : (p + 1) * CARRY] = both[PART_ROWS:]
        query_sum[...] += dot_outer(query_rows[part], grad_asks)
        pair_sum[...] += dot_outer(key_rows[p * (PART_ROWS + CARRY) : (p + 1) * (PART_ROWS + CARRY)], both)

    @pl.when(step == steps - 1)
    def _():
        grad_projections[:, :width] = (query_sum[...] * 0.125).astype(BF)
        grad_projections[:, width:] = pair_sum[...].astype(BF)


def projection_back_kernel(
    unpick_carry, grad_pair, grad_carry, carry_next, grad_query_rows, frames, grad_residual, query_w, key_w, value_w, gain,
    grad_frames, grad_memory, grad_gain,
):
    step = pl.program_id(0)
    steps = pl.num_programs(0)
    width = query_w.shape[0]
    pairs = []
    for p in range(PARTS):
        after = step * PARTS + p + 1
        inside = jnp.minimum(after, steps * PARTS - 1)
        late = grad_carry[pl.ds(pl.multiple_of(inside * CARRY, CARRY), CARRY)]
        if p == PARTS - 1:
            late = jnp.where(step == steps - 1, carry_next[...].astype(F32), late.astype(F32)).astype(BF)
        pairs.append(grad_pair[p * PART_ROWS : (p + 1) * PART_ROWS].astype(F32) + dot(unpick_carry[...], late))
    pair = jnp.concatenate(pairs, axis=0).astype(BF)
    query_back = dot_back(grad_query_rows[...], query_w[...]) * 0.125
    key_back = dot_back(pair[:, :width], key_w[...]) + dot_back(pair[:, width:], value_w[...])
    memory_rows, results = [], []
    gain_part = jnp.zeros((1, width), F32)
    for p, part in enumerate(by_part(frames[...].astype(F32))):
        at = p * PART_ROWS
        end = at + PART_FRAMES
        memory_rows.append(key_back[end : end + PART])
        own = query_back[at:end] + key_back[at:end]
        share = query_back[end : end + PART] * (1.0 / SEGLEN)
        share = jnp.concatenate([jnp.zeros((RIGHT * PART, width), F32)] + [share] * SEGLEN, axis=0)
        unit, scale = row_stats(part)
        grad_norm, more = norm_back(unit, scale, gain[...], own + share)
        gain_part = gain_part + more
        results.append(grad_residual[p * PART_FRAMES : (p + 1) * PART_FRAMES] + grad_norm)
    grad_frames[...] = by_frame(results)
    grad_memory[...] = jnp.concatenate(memory_rows, axis=0).astype(BF)

    @pl.when(step == 0)
    def _():
        grad_gain[...] = gain_part

    @pl.when(step > 0)
    def _():
        grad_gain[...] += gain_part


def cost(us):
    return pl.CostEstimate(flops=int(us * 1e9), bytes_accessed=int(us * 1e5), transcendentals=0)


def segment_position(counts_row, segment):
    order = jnp.arange(counts_row.shape[0], dtype=jnp.int32)
    starts = jnp.sum(jnp.where(order[None, :] < order[:, None], counts_row[None, :], 0), axis=1)
    first = jnp.max(jnp.where(starts[None, :] <= segment[:, None], starts[None, :], 0), axis=1)
    return segment - first


def shift(values, axis, by):
    size = lax.axis_size(axis)
    return lax.ppermute(values, axis, [(i, (i + by) % size) for i in range(size)])


def axis_bits(axis):
    return [1 << i for i in range(lax.axis_size(axis).bit_length() - 1)]


def chain(turn):
    bits = axis_bits("seg")
    few = min(3, len(bits))

    def turned(by):
        by = by % max(1, few)
        return bits[by:few] + bits[:by] + bits[few:]

    return ["grp"] + list(zip(turned(turn), turned(turn + 1)))


def side(stage):
    if stage == "grp":
        return lax.axis_index("grp")
    place = lax.axis_index("seg")
    return jnp.where(lax.axis_index("grp") == 0, place // stage[0] % 2, place // stage[1] % 2)


def swap(values, stage):
    if stage == "grp":
        return lax.ppermute(values, "grp", [(0, 1), (1, 0)])
    size = lax.axis_size("seg")
    pairs = [(core * size + i, core * size + (i ^ stage[core])) for core in range(2) for i in range(size)]
    return lax.ppermute(values, ("grp", "seg"), pairs)


def split_sum(total):
    high = total.astype(BF)
    return high, (total - high.astype(F32)).astype(BF)


class Sum:
    def __init__(self, values, turn):
        self.values = values
        self.turn = turn
        self.steps = chain(turn)
        self.done = 0
        self.row = None

    def start(self, tie=None):
        count = len(self.steps)
        if self.done < count:
            stage = self.steps[self.done]
            rows = self.values.shape[0] // 2
            own = side(stage)
            self.values, send = (
                lax.dynamic_slice_in_dim(self.values, half * rows, rows, 0) for half in (own, 1 - own)
            )
        else:
            stage = self.steps[2 * count - 1 - self.done]
            send = self.values
            if self.row is not None:
                blank = jnp.zeros((6, self.row.shape[1]), BF)
                send = jnp.concatenate([send, *split_sum(self.row), blank], axis=0)
        if tie is not None:
            send, _ = lax.optimization_barrier((send, tie))
        self.arriving = swap(send, stage)
        return send

    def land(self, *ties):
        count = len(self.steps)
        other = lax.optimization_barrier((self.arriving,) + ties)[0] if ties else self.arriving
        if self.done < count:
            self.values = (self.values.astype(F32) + other.astype(F32)).astype(self.values.dtype)
        else:
            rows = self.values.shape[0]
            if self.row is not None:
                high, low = split_sum(self.row)
                theirs = other[rows : rows + 1].astype(F32) + other[rows + 1 : rows + 2].astype(F32)
                self.row = high.astype(F32) + low.astype(F32) + theirs
                other = other[:rows]
            if self.done < 2 * count - 1:
                self.values = jnp.concatenate([self.values, other], axis=0)
            else:
                self.other = other
        self.done += 1

    def complete(self):
        return self.done == 2 * len(self.steps)


def shares(turn):
    place = lax.axis_index("seg")
    found = []
    for core in range(2):
        share = 0
        for stage in chain(turn)[1:]:
            share = share * 2 + place // stage[core] % 2
        found.append(share)
    core = lax.axis_index("grp")
    own = jnp.where(core == 0, found[0], found[1])
    other = jnp.where(core == 0, found[1], found[0])
    return jnp.stack([core, own, other])


def finish(total, widths):
    own, other = total.values, total.other
    half = own.shape[0]
    count = lax.axis_size("seg")
    rows = half // count
    place = shares(total.turn)
    cuts = np.cumsum(widths)[:-1].tolist()
    if rows % 16:
        index = jnp.arange(count, dtype=jnp.int32)
        mine, theirs = (
            jnp.take(part.reshape(count, rows, -1), index ^ place[i], axis=0).reshape(half, -1)
            for part, i in ((own, 1), (other, 2))
        )
        whole = jnp.where(place[0] == 0, jnp.concatenate([mine, theirs]), jnp.concatenate([theirs, mine]))
        return jnp.split(whole.astype(F32), cuts, axis=1)
    halves = 2

    def kernel(place_ref, own_ref, other_ref, *outs):
        step = pl.program_id(0)
        mine = (step // halves) == place_ref[0]

        def fill(source, share):
            for j in range(count // halves):
                piece = (step % halves * (count // halves) + j) ^ share
                block = source[pl.ds(pl.multiple_of(piece * rows, rows), rows)].astype(F32)
                at = 0
                for out in outs:
                    out[j * rows : (j + 1) * rows] = block[:, at : at + out.shape[1]]
                    at += out.shape[1]

        @pl.when(mine)
        def _():
            fill(own_ref, place_ref[1])

        @pl.when(jnp.logical_not(mine))
        def _():
            fill(other_ref, place_ref[2])

    return pl.pallas_call(
        kernel,
        grid=(2 * halves,),
        in_specs=[pl.BlockSpec(memory_space=pltpu.SMEM)] + [pl.BlockSpec(own.shape, lambda i: (0, 0))] * 2,
        out_specs=[pl.BlockSpec((half // halves, w), lambda i: (i, 0)) for w in widths],
        out_shape=[jax.ShapeDtypeStruct((2 * half, w), F32) for w in widths],
        compiler_params=pltpu.CompilerParams(vmem_limit_bytes=VMEM_LIMIT),
        cost_estimate=cost(3),
        name="finish",
    )(place, own, other)


def call(kernel, steps, operands, outs, scratch, us):
    def spec(shape, block):
        if isinstance(block, pl.BlockSpec):
            return block
        if block is None:
            return pl.BlockSpec(shape, lambda i: (0,) * len(shape))
        if len(block) == 3:
            return pl.BlockSpec(block, lambda i: (0, i, 0))
        return pl.BlockSpec(block, lambda i: (i, 0))

    return pl.pallas_call(
        kernel,
        grid=(steps,),
        in_specs=[spec(array.shape, block) for array, block in operands],
        out_specs=[spec(shape, block) for _, shape, block in outs],
        out_shape=[jax.ShapeDtypeStruct(shape, dtype) for dtype, shape, _ in outs],
        scratch_shapes=[pltpu.VMEM(shape, dtype) for dtype, shape in scratch],
        compiler_params=pltpu.CompilerParams(vmem_limit_bytes=VMEM_LIMIT),
        cost_estimate=cost(us),
        name=kernel.__name__,
    )(*[array for array, _ in operands])


def per_device(
    frames_in, memory, counts, query_weight, key_weight, value_weight, out_weight, up_weight, down_weight,
    input_gain, middle_gain, output_gain, out_grad, memory_grad,
):
    slots, _, width = frames_in.shape
    ff = up_weight.shape[1]
    steps = slots // BLOCK
    total = slots * FRAMES
    parts = slots // PART
    tiles = slots // GROUP
    pick_query, pick_key, pick_carry, need, segment_of = tables()
    unpick_query, unpick_key, unpick_carry = (jnp.asarray(pick.T, BF) for pick in (pick_query, pick_key, pick_carry))
    pick_query, pick_key, pick_carry = (jnp.asarray(pick, BF) for pick in (pick_query, pick_key, pick_carry))
    need, segment_of = jnp.asarray(need), jnp.asarray(segment_of)
    input_gain, middle_gain, output_gain = (g.reshape(1, width) for g in (input_gain, middle_gain, output_gain))
    frames = jnp.transpose(frames_in, (1, 0, 2))
    pulls = jnp.transpose(out_grad, (1, 0, 2))
    segment = lax.axis_index("seg") * slots + jnp.arange(slots, dtype=jnp.int32)
    position = segment_position(counts[0], segment)
    halo = jnp.concatenate(
        [
            frames[:, slots - 2 :].reshape(CARRY_FRAMES, width),
            memory[slots - MEMS :],
            jnp.zeros((CARRY - CARRY_FRAMES - MEMS, width), BF),
        ],
        axis=0,
    )
    halo = shift(halo, "seg", 1)
    slab = (FRAMES, BLOCK, width)
    smem = pl.BlockSpec(memory_space=pltpu.SMEM)

    query_rows, key_rows, query, window = call(
        project_kernel,
        steps,
        [
            (frames, slab), (memory, (BLOCK, width)), (halo, None), (input_gain, None),
            (query_weight, None), (key_weight, None), (value_weight, None),
            (pick_query, None), (pick_key, None), (pick_carry, None),
        ],
        [
            (BF, (parts * PART_ROWS, width), (FULL, width)),
            (BF, (parts * (PART_ROWS + CARRY), width), (PARTS * (PART_ROWS + CARRY), width)),
            (BF, (tiles * TILE, width), (TILES, width)),
            (BF, (tiles * TILE, 2 * width), (TILES, 2 * width)),
        ],
        [(BF, (CARRY, width)), (BF, (CARRY, 2 * width))],
        8,
    )

    attended, soft, residual, slope, grad_combined, result, memory_out, grad_down, output_part = call(
        forward_kernel,
        steps,
        [
            (position, smem), (need, None), (segment_of, None), (unpick_query, None),
            (query, (TILES, width)), (window, (TILES, 2 * width)), (frames, slab), (pulls, slab),
            (out_weight, None), (up_weight, None), (down_weight, None), (middle_gain, None), (output_gain, None),
        ],
        [
            (BF, (parts * PART_ROWS, width), (FULL, width)),
            (BF, (tiles * PAIRS * TILE, 2 * TILE), (TILES * PAIRS, 2 * TILE)),
            (F32, (total, width), (ROWS, width)),
            (BF, (total, ff), (ROWS, ff)),
            (F32, (total, width), (ROWS, width)),
            (BF, (FRAMES, slots, width), slab),
            (BF, (slots, width), (BLOCK, width)),
            (BF, (ff, width), None),
            (F32, (1, width), None),
        ],
        [(BF, (width, PART_TILES)), (BF, (total, ff)), (BF, (total, width))],
        24,
    )

    down = Sum(grad_down, 2)
    down.start()

    grad_residual, grad_attended, grad_up_out, middle_part = call(
        backward_kernel,
        steps,
        [
            (slope, (ROWS, ff)), (grad_combined, (ROWS, width)), (residual, (ROWS, width)), (attended, (FULL, width)),
            (memory_grad, (BLOCK, width)), (out_weight, None), (up_weight, None), (down_weight, None), (middle_gain, None),
        ],
        [
            (F32, (total, width), (ROWS, width)),
            (BF, (parts * PART_ROWS, width), (FULL, width)),
            (BF, (width, ff + width), None),
            (F32, (1, width), None),
        ],
        [(BF, (total, ff)), (BF, (total, width)), (F32, (width, width))],
        16,
    )

    down.land()
    down.values, grad_attended = lax.optimization_barrier((down.values, grad_attended))
    up = Sum(grad_up_out, 0)
    up.start()
    down.start()

    grad_query_rows, grad_pair, grad_carry, grad_projections = call(
        attention_back_kernel,
        steps,
        [
            (pick_query, None), (unpick_query, None), (unpick_key, None),
            (query_rows, (FULL, width)), (key_rows, (PARTS * (PART_ROWS + CARRY), width)),
            (query, (TILES, width)), (window, (TILES, 2 * width)),
            (soft, (TILES * PAIRS, 2 * TILE)), (grad_attended, (FULL, width)),
        ],
        [
            (BF, (parts * PART_ROWS, width), (FULL, width)),
            (BF, (parts * PART_ROWS, 2 * width), (FULL, 2 * width)),
            (BF, (parts * CARRY, 2 * width), (PARTS * CARRY, 2 * width)),
            (BF, (width, 3 * width), None),
        ],
        [
            (BF, (width, PART_TILES)), (BF, (PART_TILES, 2 * width)), (F32, (width, width)), (F32, (width, 2 * width)),
        ],
        12,
    )

    projections = Sum(grad_projections, 2)
    down.land()
    up.land()
    down.values, up.values, projections.values, grad_carry = lax.optimization_barrier(
        (down.values, up.values, projections.values, grad_carry)
    )
    sent = projections.start()
    carry_next = shift(grad_carry[:CARRY], "seg", -1)
    sent = up.start(sent)
    sent = down.start(sent)

    grad_frames, grad_memory, input_part = call(
        projection_back_kernel,
        steps,
        [
            (unpick_carry, None), (grad_pair, (FULL, 2 * width)), (grad_carry, None), (carry_next, None),
            (grad_query_rows, (FULL, width)), (frames, slab), (grad_residual, (ROWS, width)),
            (query_weight, None), (key_weight, None), (value_weight, None), (input_gain, None),
        ],
        [
            (F32, (FRAMES, slots, width), slab),
            (BF, (slots, width), (BLOCK, width)),
            (F32, (1, width), None),
        ],
        [],
        8,
    )
    result = jnp.transpose(result, (1, 0, 2))
    grad_frames = jnp.transpose(grad_frames, (1, 0, 2))

    gains = jnp.concatenate([input_part, middle_part, output_part], axis=1)
    projections.land(sent)
    sent = projections.start(sent)
    up.land(sent, gains)
    projections.row = None
    order = (up, down, projections)
    turn = 0
    while not all(one.complete() for one in order):
        one = order[turn % 3]
        turn += 1
        if one.complete():
            continue
        if turn > 1:
            one.land(sent)
        if one is projections and one.done == len(one.steps):
            one.row = gains
        if not one.complete():
            sent = one.start(sent)
    gains = projections.row
    (grad_down,) = finish(down, [width])
    grad_up, grad_out = finish(up, [ff, width])
    grad_query, grad_key, grad_value = finish(projections, [width] * 3)
    gains = gains.reshape(3, width)
    return (
        result, memory_out, grad_frames, grad_memory,
        grad_query, grad_key, grad_value, grad_out, grad_up, grad_down,
        gains[0], gains[1], gains[2],
    )


def solution(mesh):
    rows = P(("grp", "seg"), None, None)
    singles = P(("grp", "seg"), None)
    return jax.shard_map(
        per_device,
        mesh=mesh,
        in_specs=(rows, singles, P("grp", None)) + (P(),) * 9 + (rows, singles),
        out_specs=(rows, singles, rows, singles) + (P(),) * 9,
        check_vma=False,
    )
```

time: 1040 us -> 201 us (0.19)
  waiting for transfers between devices: 412 us -> 38.1 us
  local copies, waits for them, and re-layouts: 220 us -> 22.1 us
  matrix products: 123 us -> 0 us
  other arithmetic: 118 us -> 10.3 us
  Pallas kernels: 0 us -> 98.9 us
  starting transfers between devices: 101 us -> 29.9 us
  blocking collectives: 45 us -> 0 us
  between operations: 15.4 us -> 1.15 us
    psum x1 -> x0, waiting for transfers between devices: 150 us -> none  [per_device(): lax.psum((grad_query, grad_key, grad_value, grad_input_gain, grad_up, gra...]
    all_to_all x4 -> x0, waiting for transfers between devices: 130 us -> none  [the longest x1 46.9 us: per_device(): lax.all_to_all(sent_home, 'seg', split_axis=0, concat_axis=0, tiled=True)]
    dot_general x22 -> x0, matrix products: 123 us -> none  [the longest x6 26.9 us: outer_sum(): jnp.einsum('nri,nrj->ij', operand, gradient, preferred_element_type=jnp.f...]
    pallas_call x0 -> x8, Pallas kernels: none -> 98.9 us  [the longest x5 86.8 us: call(): pl.pallas_call(kernel, grid=(steps,), in_specs=[spec(array.shape, block)...]
    ppermute x8 -> x32, waiting for transfers between devices: 131 us -> 38.1 us  [the longest x24 33.4 us: swap(): return lax.ppermute(values, ('grp', 'seg'), pairs)]
    all_to_all x4 -> x0, starting transfers between devices: 81.7 us -> none  [the longest x1 59.4 us: per_device(): lax.all_to_all(attended, 'seg', split_axis=0, concat_axis=0, tiled=True)]
    reshape x6 -> x1, local copies, waits for them, and re-layouts: 52 us -> 0.02 us  [per_device(): frames[:, slots - 2:].reshape(CARRY_FRAMES, width)]
    psum x1 -> x0, blocking collectives: 45 us -> none  [per_device(): lax.psum((grad_query, grad_key, grad_value, grad_input_gain, grad_up, gra...]
  transfers between devices with their start and end apart: 13 -> 32, of which waited for: 8 -> 14; matrix products, arithmetic and copies ran while one was open for 11% -> 13% of each run, Pallas kernels for 0% -> 27%
where the time goes in v2:
time: 201 us; the launch traced here: 200 us
  Pallas kernels  98.9 us (49%)
  waiting for transfers between devices  38.1 us (19%)
  starting transfers between devices  29.9 us (15%)
  local copies, waits for them, and re-layouts  22.1 us (11%)
  other arithmetic  10.3 us (5%)
    pallas_call x5, Pallas kernels, call(): pl.pallas_call(kernel, grid=(steps,), in_specs=[spec(array.shape, block)...  86.8 us
    ppermute x24, waiting for transfers between devices, swap(): return lax.ppermute(values, ('grp', 'seg'), pairs)  33.4 us
    ppermute x24, starting transfers between devices, swap(): return lax.ppermute(values, ('grp', 'seg'), pairs)  22.6 us
    pallas_call x3, Pallas kernels, finish(): pl.pallas_call(kernel, grid=(2 * halves,), in_specs=[pl.BlockSpec(memory_...  12 us
    unnamed x28, local copies, waits for them, and re-layouts  6.94 us
    dynamic_slice x15, local copies, waits for them, and re-layouts, start(): lax.dynamic_slice_in_dim(self.values, half * rows, rows, 0)  5.62 us
    ppermute x2, starting transfers between devices, shift(): lax.ppermute(values, axis, [(i, (i + by) % size) for i in range(size)])  5.42 us
    convert_element_type x12, other arithmetic, land(): (self.values.astype(F32) + other.astype(F32)).astype(self.values.dtype)  5.31 us
  transfers between devices with their start and end apart: 32, of which 14 were waited for; matrix products, arithmetic and copies ran while one was open for 13% of the time, Pallas kernels for 27%

profile of v2, /device:TPU:0, one launch (start us, length us, event | category | flops | bytes accessed | tf_op | source)
XLA Modules:
  0.0 200.5 jit_solution(3318074413613573614)
XLA Ops:
  2.5 3.0 %collective-permute-start = (bf16[48,512]{1,0:T(8,128)(2,1)S(1)}, bf16[48,512]{1,0:T(8,128)(2,1)S(1)}, u32[]{:S(2)}, u32[]{:S(2)}) collective-permute-start(bf16[48,512]{1,0:T(8,128)(2,1)S(1)} %maximum_maximum_fusion), channel_id=1, source_target_pairs={{0,1},{1,2},{2,3},{3,4},{4,5},{5,6},{6,7},{7,8},{8,9},{9,10},{10,1... | collective-permute-start | bytes 147464 | tf_op jit(solution)/shard_map/ppermute | solution.py:408
  6.9 4.7 %collective-permute-done.halo = bf16[48,512]{1,0:T(8,128)(2,1)S(1)} collective-permute-done((bf16[48,512]{1,0:T(8,128)(2,1)S(1)}, bf16[48,512]{1,0:T(8,128)(2,1)S(1)}, u32[]{:S(2)}, u32[]{:S(2)}) %collective-permute-start) | collective-permute-done | bytes 49184 | tf_op jit(solution)/shard_map/ppermute | solution.py:408
  12.2 11.3 %project_kernel.1 = (bf16[1408,512]{1,0:T(8,128)(2,1)}, bf16[1792,512]{1,0:T(8,128)(2,1)}, bf16[2048,512]{1,0:T(8,128)(2,1)}, bf16[2048,1024]{1,0:T(8,128)(2,1)}) custom-call(bf16[20,64,512]{2,1,0:T(8,128)(2,1)} %bitcast.20, bf16[64,512]{1,0:T(8,128)(2,1)} %memory.1, bf16[48,512]{1,0:T(8,128)(2,1)} %copy-done.9, f32[1,512]{1,0:T(1,128)} %bitcast.27, ...), custom_call_target="tpu_custom_call" | custom-call | flops 8000000000 | bytes 800000 | tf_op jit(solution)/shard_map/project_kernel/pallas_call | solution.py:570
  23.4 29.6 %forward_kernel.1 = (bf16[1408,512]{1,0:T(8,128)(2,1)}, bf16[8192,256]{1,0:T(8,128)(2,1)}, f32[1280,512]{1,0:T(8,128)}, bf16[1280,2048]{1,0:T(8,128)(2,1)}, f32[...) custom-call(s32[64]{0:T(128)} %fusion.position, ...), custom_call_target="tpu_custom_call" | custom-call | flops 24000000000 | bytes 2400000 | tf_op jit(solution)/shard_map/forward_kernel/pallas_call | solution.py:570
  54.4 19.0 %backward_kernel.1 = (f32[1280,512]{1,0:T(8,128)}, bf16[1408,512]{1,0:T(8,128)(2,1)}, bf16[512,2560]{1,0:T(8,128)(2,1)}, f32[1,512]{1,0:T(1,128)}) custom-call(bf16[1280,2048]{1,0:T(8,128)(2,1)} %get-tuple-element.109.slope, f32[1280,512]{1,0:T(8,128)} %get-tuple-element.110.grad_combined, f32[1280,512]{1,0:T(8,128)} %get-tuple-element.111.residual, ...), custom_call_target="tpu_custom_call" | custom-call | flops 16000000000 | bytes 1600000 | tf_op jit(solution)/shard_map/backward_kernel/pallas_call | solution.py:570
  73.5 1.6 constant_dynamic-slice_fusion.12
  76.0 17.9 %attention_back_kernel.1 = (bf16[1408,512]{1,0:T(8,128)(2,1)}, bf16[1408,1024]{1,0:T(8,128)(2,1)}, bf16[384,1024]{1,0:T(8,128)(2,1)}, bf16[512,1536]{1,0:T(8,128)(2,1)}) custom-call(bf16[256,176]{1,0:T(8,128)(2,1)} %constant.291.clone.pick_query, bf16[176,256]{1,0:T(8,128)(2,1)} %constant.288.clone.unpick_query, ...), custom_call_target="tpu_custom_call" | custom-call | flops 12000000000 | bytes 1200000 | tf_op jit(solution)/shard_map/attention_back_kernel/pallas_call | solution.py:570
  93.9 2.0 %add_convert_fusion = bf16[256,2560]{1,0:T(8,128)(2,1)S(1)} fusion(bf16[256,2560]{1,0:T(8,128)(2,1)} %collective-permute-done.3, bf16[512,2560]{1,0:T(8,128)(2,1)} %get-tuple-element.117, s32[]{:T(128)S(6)} %select_n.294), kind=kLoop, calls=%fused_computation | loop fusion | flops 2621440 | bytes 3932164 | tf_op jit(solution)/shard_map/convert_element_type | solution.py:478
  97.1 2.5 %collective-permute-start.4 = (bf16[48,1024]{1,0:T(8,128)(2,1)S(1)}, bf16[48,1024]{1,0:T(8,128)(2,1)S(1)}, u32[]{:S(2)}, u32[]{:S(2)}) collective-permute-start(bf16[48,1024]{1,0:T(8,128)(2,1)S(1)} %slice.68), channel_id=1, source_target_pairs={{0,15},{1,0},{2,1},{3,2},{4,3},{5,4},{6,5},{7,6},{8,7},{9,8},{10,9... | collective-permute-start | bytes 294920 | tf_op jit(solution)/shard_map/ppermute | solution.py:408
  102.9 2.0 %collective-permute-start.7 = (bf16[256,512]{1,0:T(8,128)(2,1)}, bf16[256,512]{1,0:T(8,128)(2,1)}, u32[]{:S(2)}, u32[]{:S(2)}) collective-permute-start(bf16[256,512]{1,0:T(8,128)(2,1)} %constant_dynamic-slice_fusion.10), channel_id=1, source_target_pairs={{0,1},{1,0},{2,3},{3,2},{4,5},{5,4},{6,7},{7,6},{8,9},{9,8},{10,11... | collective-permute-start | bytes 786440 | tf_op jit(solution)/shard_map/ppermute | solution.py:438
  105.5 9.1 %projection_back_kernel.1 = (f32[20,64,512]{2,1,0:T(8,128)}, bf16[64,512]{1,0:T(8,128)(2,1)}, f32[1,512]{1,0:T(1,128)}) custom-call(bf16[176,48]{1,0:T(8,128)(2,1)} %constant.290.clone.unpick_carry, bf16[1408,1024]{1,0:T(8,128)(2,1)} %get-tuple-element.115.grad_pair, bf16[384,1024]{1,0:T(8,128)(2,1)} %get-tuple-element.120.grad_carry, ...), custom_call_target="tpu_custom_call" | custom-call | flops 8000000000 | bytes 800000 | tf_op jit(solution)/shard_map/projection_back_kernel/pallas_call | solution.py:570
  115.3 1.3 add_convert_fusion.2
  118.2 2.1 %collective-permute-start.10 = (bf16[128,512]{1,0:T(8,128)(2,1)S(1)}, bf16[128,512]{1,0:T(8,128)(2,1)S(1)}, u32[]{:S(2)}, u32[]{:S(2)}) collective-permute-start(bf16[128,512]{1,0:T(8,128)(2,1)S(1)} %constant_dynamic-slice_fusion.6), channel_id=1, source_target_pairs={{0,2},{1,3},{2,0},{3,1},{4,6},{5,7},{6,4},{7,5},{8,10},{9,11},{10,... | collective-permute-start | bytes 393224 | tf_op jit(solution)/shard_map/ppermute | solution.py:438
  120.2 8.0 %collective-permute-done.6 = bf16[128,1536]{1,0:T(8,128)(2,1)S(1)} collective-permute-done((bf16[128,1536]{1,0:T(8,128)(2,1)S(1)}, bf16[128,1536]{1,0:T(8,128)(2,1)S(1)}, u32[]{:S(2)}, u32[]{:S(2)}) %collective-permute-start.6) | collective-permute-done | bytes 393248 | tf_op jit(solution)/shard_map/ppermute | solution.py:438
  128.7 1.3 collective-permute-start.14
  130.7 3.4 %collective-permute-done.9 = bf16[64,1536]{1,0:T(8,128)(2,1)S(1)} collective-permute-done((bf16[64,1536]{1,0:T(8,128)(2,1)S(1)}, bf16[64,1536]{1,0:T(8,128)(2,1)S(1)}, u32[]{:S(2)}, u32[]{:S(2)}) %collective-permute-start.9) | collective-permute-done | bytes 196640 | tf_op jit(solution)/shard_map/ppermute | solution.py:438
  135.1 1.4 collective-permute-done.14
  138.2 2.1 %collective-permute-start.16 = (bf16[64,512]{1,0:T(8,128)(2,1)S(1)}, bf16[64,512]{1,0:T(8,128)(2,1)S(1)}, u32[]{:S(2)}, u32[]{:S(2)}) collective-permute-start(bf16[64,512]{1,0:T(8,128)(2,1)S(1)} %get-tuple-element.147), channel_id=1, source_target_pairs={{0,8},{1,9},{2,10},{3,11},{4,12},{5,13},{6,14},{7,15},{8,0},{9,1},... | collective-permute-start | bytes 196616 | tf_op jit(solution)/shard_map/ppermute | solution.py:438
  141.2 2.5 %collective-permute-done.17 = bf16[16,2560]{1,0:T(8,128)(2,1)S(1)} collective-permute-done((bf16[16,2560]{1,0:T(8,128)(2,1)S(1)}, bf16[16,2560]{1,0:T(8,128)(2,1)S(1)}, u32[]{:S(2)}, u32[]{:S(2)}) %collective-permute-start.17) | collective-permute-done | bytes 81952 | tf_op jit(solution)/shard_map/ppermute | solution.py:438
  146.1 1.5 collective-permute-done.15
  149.7 3.9 %collective-permute-start.23 = (bf16[32,2560]{1,0:T(8,128)(2,1)S(1)}, bf16[32,2560]{1,0:T(8,128)(2,1)S(1)}, u32[]{:S(2)}, u32[]{:S(2)}) collective-permute-start(bf16[32,2560]{1,0:T(8,128)(2,1)S(1)} %pad_maximum_fusion.4), channel_id=1, source_target_pairs={{0,4},{1,5},{2,6},{3,7},{4,0},{5,1},{6,2},{7,3},{8,12},{9,13},{10,... | collective-permute-start | bytes 491528 | tf_op jit(solution)/shard_map/ppermute | solution.py:438
  154.2 1.8 collective-permute-start.22
  160.2 3.3 %collective-permute-done.22 = bf16[256,512]{1,0:T(8,128)(2,1)S(1)} collective-permute-done((bf16[256,512]{1,0:T(8,128)(2,1)S(1)}, bf16[256,512]{1,0:T(8,128)(2,1)S(1)}, u32[]{:S(2)}, u32[]{:S(2)}) %collective-permute-start.22) | collective-permute-done | bytes 262176 | tf_op jit(solution)/shard_map/ppermute | solution.py:438
  164.4 1.8 collective-permute-start.24
  166.9 1.8 collective-permute-done.26
  168.8 2.3 %collective-permute-start.28 = (bf16[128,2560]{1,0:T(8,128)(2,1)S(1)}, bf16[128,2560]{1,0:T(8,128)(2,1)S(1)}, u32[]{:S(2)}, u32[]{:S(2)}) collective-permute-start(bf16[128,2560]{1,0:T(8,128)(2,1)S(1)} %pad_maximum_fusion), channel_id=1, source_target_pairs={{0,1},{1,0},{2,3},{3,2},{4,5},{5,4},{6,7},{7,6},{8,9},{9,8},{10,11... | collective-permute-start | bytes 1966088 | tf_op jit(solution)/shard_map/ppermute | solution.py:438
  171.1 1.8 collective-permute-done.25
  172.9 1.9 constant_dynamic-update-slice_fusion.3.own_ref
  176.5 5.4 %collective-permute-done.28 = bf16[128,2560]{1,0:T(8,128)(2,1)S(1)} collective-permute-done((bf16[128,2560]{1,0:T(8,128)(2,1)S(1)}, bf16[128,2560]{1,0:T(8,128)(2,1)S(1)}, u32[]{:S(2)}, u32[]{:S(2)}) %collective-permute-start.28) | collective-permute-done | bytes 655392 | tf_op jit(solution)/shard_map/ppermute | solution.py:438
  186.9 4.0 %finish.5 = f32[2048,512]{1,0:T(8,128)} custom-call(s32[3]{0:T(128)} %pad_add_fusion.place_ref, bf16[1024,512]{1,0:T(8,128)(2,1)} %constant_dynamic-update-slice_fusion.3.own_ref, bf16[1024,512]{1,0:T(8,128)(2,1)} %collective-permute-done.31.other_ref), custom_call_target="tpu_custom_call" | custom-call | flops 3000000000 | bytes 300000 | tf_op jit(solution)/shard_map/finish/pallas_call | solution.py:548
  192.4 3.5 %finish.3 = (f32[512,512]{1,0:T(8,128)}, f32[512,512]{1,0:T(8,128)}, f32[512,512]{1,0:T(8,128)}) custom-call(s32[3]{0:T(128)} %pad_add_fusion.place_ref, bf16[256,1536]{1,0:T(8,128)(2,1)} %copy-done.5, bf16[256,1536]{1,0:T(8,128)(2,1)} %slice.81.other_ref), custom_call_target="tpu_custom_call" | custom-call | flops 3000000000 | bytes 300000 | tf_op jit(solution)/shard_map/finish/pallas_call | solution.py:548
  196.0 4.5 %finish.4 = (f32[512,2048]{1,0:T(8,128)}, f32[512,512]{1,0:T(8,128)}) custom-call(s32[3]{0:T(128)} %pad_add_fusion.1.place_ref, bf16[256,2560]{1,0:T(8,128)(2,1)} %constant_dynamic-update-slice_fusion.8.own_ref, bf16[256,2560]{1,0:T(8,128)(2,1)} %collective-permute-done.30.other_ref), custom_call_target="tpu_custom_call" | custom-call | flops 3000000000 | bytes 300000 | tf_op jit(solution)/shard_map/finish/pallas_call | solution.py:548
  (142 shorter events, 37.3 us)
Async XLA Ops:
  2.5 9.0 %collective-permute-start = (bf16[48,512]{1,0:T(8,128)(2,1)S(1)}, bf16[48,512]{1,0:T(8,128)(2,1)S(1)}, u32[]{:S(2)}, u32[]{:S(2)}) collective-permute-start(bf16[48,512]{1,0:T(8,128)(2,1)S(1)} %maximum_maximum_fusion), channel_id=1, source_target_pairs={{0,1},{1,2},{2,3},{3,4},{4,5},{5,6},{6,7},{7,8},{8,9},{9,10},{10,1... | collective-permute-start | bytes 147464 | tf_op jit(solution)/shard_map/ppermute | solution.py:408
  54.3 21.2 %collective-permute-start.1 = (bf16[1024,512]{1,0:T(8,128)(2,1)S(1)}, bf16[1024,512]{1,0:T(8,128)(2,1)S(1)}, u32[]{:S(2)}, u32[]{:S(2)}) collective-permute-start(bf16[1024,512]{1,0:T(8,128)(2,1)S(1)} %constant_dynamic-slice_fusion.14), channel_id=1, source_target_pairs={{0,16},{16,0},{1,17},{17,1},{2,18},{18,2},{3,19},{19,3},{4,20},{20... | collective-permute-start | bytes 3145736 | tf_op jit(solution)/shard_map/ppermute | solution.py:435
  75.0 18.9 %collective-permute-start.3 = (bf16[256,2560]{1,0:T(8,128)(2,1)S(1)}, bf16[256,2560]{1,0:T(8,128)(2,1)}, u32[]{:S(2)}, u32[]{:S(2)}) collective-permute-start(bf16[256,2560]{1,0:T(8,128)(2,1)S(1)} %constant_dynamic-slice_fusion.12), channel_id=1, source_target_pairs={{0,16},{16,0},{1,17},{17,1},{2,18},{18,2},{3,19},{19,3},{4,20},{20... | collective-permute-start | bytes 3932168 | tf_op jit(solution)/shard_map/ppermute | solution.py:435
  75.9 20.0 %collective-permute-start.2 = (bf16[512,512]{1,0:T(8,128)(2,1)S(1)}, bf16[512,512]{1,0:T(8,128)(2,1)S(1)}, u32[]{:S(2)}, u32[]{:S(2)}) collective-permute-start(bf16[512,512]{1,0:T(8,128)(2,1)S(1)} %constant_dynamic-slice_fusion.13), channel_id=1, source_target_pairs={{0,4},{1,5},{2,6},{3,7},{4,0},{5,1},{6,2},{7,3},{8,12},{9,13},{10,... | collective-permute-start | bytes 1572872 | tf_op jit(solution)/shard_map/ppermute | solution.py:438
  97.1 7.8 %collective-permute-start.4 = (bf16[48,1024]{1,0:T(8,128)(2,1)S(1)}, bf16[48,1024]{1,0:T(8,128)(2,1)S(1)}, u32[]{:S(2)}, u32[]{:S(2)}) collective-permute-start(bf16[48,1024]{1,0:T(8,128)(2,1)S(1)} %slice.68), channel_id=1, source_target_pairs={{0,15},{1,0},{2,1},{3,2},{4,3},{5,4},{6,5},{7,6},{8,7},{9,8},{10,9... | collective-permute-start | bytes 294920 | tf_op jit(solution)/shard_map/ppermute | solution.py:408
  100.5 14.8 %collective-permute-start.5 = (bf16[256,1536]{1,0:T(8,128)(2,1)}, bf16[256,1536]{1,0:T(8,128)(2,1)}, u32[]{:S(2)}, u32[]{:S(2)}) collective-permute-start(bf16[256,1536]{1,0:T(8,128)(2,1)} %constant_dynamic-slice_fusion.11), channel_id=1, source_target_pairs={{0,16},{16,0},{1,17},{17,1},{2,18},{18,2},{3,19},{19,3},{4,20},{20... | collective-permute-start | bytes 2359304 | tf_op jit(solution)/shard_map/ppermute | solution.py:435
  102.1 14.7 %collective-permute-start.8 = (bf16[128,2560]{1,0:T(8,128)(2,1)}, bf16[128,2560]{1,0:T(8,128)(2,1)S(1)}, u32[]{:S(2)}, u32[]{:S(2)}) collective-permute-start(bf16[128,2560]{1,0:T(8,128)(2,1)} %constant_dynamic-slice_fusion.9), channel_id=1, source_target_pairs={{0,1},{1,0},{2,3},{3,2},{4,5},{5,4},{6,7},{7,6},{8,9},{9,8},{10,11... | collective-permute-start | bytes 1966088 | tf_op jit(solution)/shard_map/ppermute | solution.py:438
  102.9 14.3 %collective-permute-start.7 = (bf16[256,512]{1,0:T(8,128)(2,1)}, bf16[256,512]{1,0:T(8,128)(2,1)}, u32[]{:S(2)}, u32[]{:S(2)}) collective-permute-start(bf16[256,512]{1,0:T(8,128)(2,1)} %constant_dynamic-slice_fusion.10), channel_id=1, source_target_pairs={{0,1},{1,0},{2,3},{3,2},{4,5},{5,4},{6,7},{7,6},{8,9},{9,8},{10,11... | collective-permute-start | bytes 786440 | tf_op jit(solution)/shard_map/ppermute | solution.py:438
  116.7 11.5 %collective-permute-start.6 = (bf16[128,1536]{1,0:T(8,128)(2,1)S(1)}, bf16[128,1536]{1,0:T(8,128)(2,1)S(1)}, u32[]{:S(2)}, u32[]{:S(2)}) collective-permute-start(bf16[128,1536]{1,0:T(8,128)(2,1)S(1)} %constant_dynamic-slice_fusion.8), channel_id=1, source_target_pairs={{0,4},{1,5},{2,6},{3,7},{4,0},{5,1},{6,2},{7,3},{8,12},{9,13},{10,... | collective-permute-start | bytes 1179656 | tf_op jit(solution)/shard_map/ppermute | solution.py:438
  117.0 11.6 %collective-permute-start.11 = (bf16[64,2560]{1,0:T(8,128)(2,1)S(1)}, bf16[64,2560]{1,0:T(8,128)(2,1)S(1)}, u32[]{:S(2)}, u32[]{:S(2)}) collective-permute-start(bf16[64,2560]{1,0:T(8,128)(2,1)S(1)} %constant_dynamic-slice_fusion.7), channel_id=1, source_target_pairs={{0,2},{1,3},{2,0},{3,1},{4,6},{5,7},{6,4},{7,5},{8,10},{9,11},{10,... | collective-permute-start | bytes 983048 | tf_op jit(solution)/shard_map/ppermute | solution.py:438
  118.2 11.8 %collective-permute-start.10 = (bf16[128,512]{1,0:T(8,128)(2,1)S(1)}, bf16[128,512]{1,0:T(8,128)(2,1)S(1)}, u32[]{:S(2)}, u32[]{:S(2)}) collective-permute-start(bf16[128,512]{1,0:T(8,128)(2,1)S(1)} %constant_dynamic-slice_fusion.6), channel_id=1, source_target_pairs={{0,2},{1,3},{2,0},{3,1},{4,6},{5,7},{6,4},{7,5},{8,10},{9,11},{10,... | collective-permute-start | bytes 393224 | tf_op jit(solution)/shard_map/ppermute | solution.py:438
  128.4 5.7 %collective-permute-start.9 = (bf16[64,1536]{1,0:T(8,128)(2,1)S(1)}, bf16[64,1536]{1,0:T(8,128)(2,1)S(1)}, u32[]{:S(2)}, u32[]{:S(2)}) collective-permute-start(bf16[64,1536]{1,0:T(8,128)(2,1)S(1)} %constant_dynamic-slice_fusion.5), channel_id=1, source_target_pairs={{0,1},{1,0},{2,3},{3,2},{4,5},{5,4},{6,7},{7,6},{8,9},{9,8},{10,11... | collective-permute-start | bytes 589832 | tf_op jit(solution)/shard_map/ppermute | solution.py:438
  128.7 7.8 %collective-permute-start.14 = (bf16[32,2560]{1,0:T(8,128)(2,1)S(1)}, bf16[32,2560]{1,0:T(8,128)(2,1)S(1)}, u32[]{:S(2)}, u32[]{:S(2)}) collective-permute-start(bf16[32,2560]{1,0:T(8,128)(2,1)S(1)} %constant_dynamic-slice_fusion.4), channel_id=1, source_target_pairs={{0,4},{1,5},{2,6},{3,7},{4,0},{5,1},{6,2},{7,3},{8,12},{9,13},{10,... | collective-permute-start | bytes 491528 | tf_op jit(solution)/shard_map/ppermute | solution.py:438
  130.0 7.5 %collective-permute-start.13 = (bf16[64,512]{1,0:T(8,128)(2,1)S(1)}, bf16[64,512]{1,0:T(8,128)(2,1)S(1)}, u32[]{:S(2)}, u32[]{:S(2)}) collective-permute-start(bf16[64,512]{1,0:T(8,128)(2,1)S(1)} %constant_dynamic-slice_fusion.3), channel_id=1, source_target_pairs={{0,8},{1,9},{2,10},{3,11},{4,12},{5,13},{6,14},{7,15},{8,0},{9,1},... | collective-permute-start | bytes 196616 | tf_op jit(solution)/shard_map/ppermute | solution.py:438
  134.2 6.0 %collective-permute-start.12 = (bf16[32,1536]{1,0:T(8,128)(2,1)S(1)}, bf16[32,1536]{1,0:T(8,128)(2,1)S(1)}, u32[]{:S(2)}, u32[]{:S(2)}) collective-permute-start(bf16[32,1536]{1,0:T(8,128)(2,1)S(1)} %constant_dynamic-slice_fusion.2), channel_id=1, source_target_pairs={{0,2},{1,3},{2,0},{3,1},{4,6},{5,7},{6,4},{7,5},{8,10},{9,11},{10,... | collective-permute-start | bytes 294920 | tf_op jit(solution)/shard_map/ppermute | solution.py:438
  136.6 7.1 %collective-permute-start.17 = (bf16[16,2560]{1,0:T(8,128)(2,1)S(1)}, bf16[16,2560]{1,0:T(8,128)(2,1)S(1)}, u32[]{:S(2)}, u32[]{:S(2)}) collective-permute-start(bf16[16,2560]{1,0:T(8,128)(2,1)S(1)} %constant_dynamic-slice_fusion.1), channel_id=1, source_target_pairs={{0,8},{1,9},{2,10},{3,11},{4,12},{5,13},{6,14},{7,15},{8,0},{9,1},... | collective-permute-start | bytes 245768 | tf_op jit(solution)/shard_map/ppermute | solution.py:438
  138.2 7.2 %collective-permute-start.16 = (bf16[64,512]{1,0:T(8,128)(2,1)S(1)}, bf16[64,512]{1,0:T(8,128)(2,1)S(1)}, u32[]{:S(2)}, u32[]{:S(2)}) collective-permute-start(bf16[64,512]{1,0:T(8,128)(2,1)S(1)} %get-tuple-element.147), channel_id=1, source_target_pairs={{0,8},{1,9},{2,10},{3,11},{4,12},{5,13},{6,14},{7,15},{8,0},{9,1},... | collective-permute-start | bytes 196616 | tf_op jit(solution)/shard_map/ppermute | solution.py:438
  140.3 7.3 %collective-permute-start.15 = (bf16[16,1536]{1,0:T(8,128)(2,1)S(1)}, bf16[16,1536]{1,0:T(8,128)(2,1)S(1)}, u32[]{:S(2)}, u32[]{:S(2)}) collective-permute-start(bf16[16,1536]{1,0:T(8,128)(2,1)S(1)} %constant_dynamic-slice_fusion), channel_id=1, source_target_pairs={{0,8},{1,9},{2,10},{3,11},{4,12},{5,13},{6,14},{7,15},{8,0},{9,1},... | collective-permute-start | bytes 147464 | tf_op jit(solution)/shard_map/ppermute | solution.py:438
  144.3 5.3 %collective-permute-start.20 = (bf16[16,2560]{1,0:T(8,128)(2,1)S(1)}, bf16[16,2560]{1,0:T(8,128)(2,1)S(1)}, u32[]{:S(2)}, u32[]{:S(2)}) collective-permute-start(bf16[16,2560]{1,0:T(8,128)(2,1)S(1)} %get-tuple-element.151), channel_id=1, source_target_pairs={{0,8},{1,9},{2,10},{3,11},{4,12},{5,13},{6,14},{7,15},{8,0},{9,1},... | collective-permute-start | bytes 245768 | tf_op jit(solution)/shard_map/ppermute | solution.py:438
  145.4 8.8 %collective-permute-start.19 = (bf16[128,512]{1,0:T(8,128)(2,1)S(1)}, bf16[128,512]{1,0:T(8,128)(2,1)S(1)}, u32[]{:S(2)}, u32[]{:S(2)}) collective-permute-start(bf16[128,512]{1,0:T(8,128)(2,1)S(1)} %pad_maximum_fusion.5), channel_id=1, source_target_pairs={{0,2},{1,3},{2,0},{3,1},{4,6},{5,7},{6,4},{7,5},{8,10},{9,11},{10,... | collective-permute-start | bytes 393224 | tf_op jit(solution)/shard_map/ppermute | solution.py:438
  148.3 7.7 %collective-permute-start.18 = (bf16[24,1536]{1,0:T(8,128)(2,1)S(1)}, bf16[24,1536]{1,0:T(8,128)(2,1)S(1)}, u32[]{:S(2)}, u32[]{:S(2)}) collective-permute-start(bf16[24,1536]{1,0:T(8,128)(2,1)S(1)} %pad_maximum_fusion.6), channel_id=1, source_target_pairs={{0,8},{1,9},{2,10},{3,11},{4,12},{5,13},{6,14},{7,15},{8,0},{9,1},... | collective-permute-start | bytes 221192 | tf_op jit(solution)/shard_map/ppermute | solution.py:438
  149.7 9.0 %collective-permute-start.23 = (bf16[32,2560]{1,0:T(8,128)(2,1)S(1)}, bf16[32,2560]{1,0:T(8,128)(2,1)S(1)}, u32[]{:S(2)}, u32[]{:S(2)}) collective-permute-start(bf16[32,2560]{1,0:T(8,128)(2,1)S(1)} %pad_maximum_fusion.4), channel_id=1, source_target_pairs={{0,4},{1,5},{2,6},{3,7},{4,0},{5,1},{6,2},{7,3},{8,12},{9,13},{10,... | collective-permute-start | bytes 491528 | tf_op jit(solution)/shard_map/ppermute | solution.py:438
  154.2 9.3 %collective-permute-start.22 = (bf16[256,512]{1,0:T(8,128)(2,1)S(1)}, bf16[256,512]{1,0:T(8,128)(2,1)S(1)}, u32[]{:S(2)}, u32[]{:S(2)}) collective-permute-start(bf16[256,512]{1,0:T(8,128)(2,1)S(1)} %pad_maximum_fusion.3), channel_id=1, source_target_pairs={{0,1},{1,0},{2,3},{3,2},{4,5},{5,4},{6,7},{7,6},{8,9},{9,8},{10,11... | collective-permute-start | bytes 786440 | tf_op jit(solution)/shard_map/ppermute | solution.py:438
  156.7 7.0 %collective-permute-start.21 = (bf16[40,1536]{1,0:T(8,128)(2,1)S(1)}, bf16[40,1536]{1,0:T(8,128)(2,1)S(1)}, u32[]{:S(2)}, u32[]{:S(2)}) collective-permute-start(bf16[40,1536]{1,0:T(8,128)(2,1)S(1)} %concatenate.98), channel_id=1, source_target_pairs={{0,2},{1,3},{2,0},{3,1},{4,6},{5,7},{6,4},{7,5},{8,10},{9,11},{10,... | collective-permute-start | bytes 368648 | tf_op jit(solution)/shard_map/ppermute | solution.py:438
  158.7 10.0 %collective-permute-start.26 = (bf16[64,2560]{1,0:T(8,128)(2,1)S(1)}, bf16[64,2560]{1,0:T(8,128)(2,1)S(1)}, u32[]{:S(2)}, u32[]{:S(2)}) collective-permute-start(bf16[64,2560]{1,0:T(8,128)(2,1)S(1)} %pad_maximum_fusion.2), channel_id=1, source_target_pairs={{0,2},{1,3},{2,0},{3,1},{4,6},{5,7},{6,4},{7,5},{8,10},{9,11},{10,... | collective-permute-start | bytes 983048 | tf_op jit(solution)/shard_map/ppermute | solution.py:438
  163.6 9.4 %collective-permute-start.25 = (bf16[512,512]{1,0:T(8,128)(2,1)S(1)}, bf16[512,512]{1,0:T(8,128)(2,1)}, u32[]{:S(2)}, u32[]{:S(2)}) collective-permute-start(bf16[512,512]{1,0:T(8,128)(2,1)S(1)} %pad_maximum_fusion.1), channel_id=1, source_target_pairs={{0,4},{1,5},{2,6},{3,7},{4,0},{5,1},{6,2},{7,3},{8,12},{9,13},{10,... | collective-permute-start | bytes 1572872 | tf_op jit(solution)/shard_map/ppermute | solution.py:438
  164.4 10.4 %collective-permute-start.24 = (bf16[72,1536]{1,0:T(8,128)(2,1)S(1)}, bf16[72,1536]{1,0:T(8,128)(2,1)S(1)}, u32[]{:S(2)}, u32[]{:S(2)}) collective-permute-start(bf16[72,1536]{1,0:T(8,128)(2,1)S(1)} %concatenate.101), channel_id=1, source_target_pairs={{0,1},{1,0},{2,3},{3,2},{4,5},{5,4},{6,7},{7,6},{8,9},{9,8},{10,11... | collective-permute-start | bytes 663560 | tf_op jit(solution)/shard_map/ppermute | solution.py:438
  168.8 13.1 %collective-permute-start.28 = (bf16[128,2560]{1,0:T(8,128)(2,1)S(1)}, bf16[128,2560]{1,0:T(8,128)(2,1)S(1)}, u32[]{:S(2)}, u32[]{:S(2)}) collective-permute-start(bf16[128,2560]{1,0:T(8,128)(2,1)S(1)} %pad_maximum_fusion), channel_id=1, source_target_pairs={{0,1},{1,0},{2,3},{3,2},{4,5},{5,4},{6,7},{7,6},{8,9},{9,8},{10,11... | collective-permute-start | bytes 1966088 | tf_op jit(solution)/shard_map/ppermute | solution.py:438
  175.7 8.1 %collective-permute-start.27 = (bf16[136,1536]{1,0:T(8,128)(2,1)S(1)}, bf16[136,1536]{1,0:T(8,128)(2,1)S(1)}, u32[]{:S(2)}, u32[]{:S(2)}) collective-permute-start(bf16[136,1536]{1,0:T(8,128)(2,1)S(1)} %concatenate.104), channel_id=1, source_target_pairs={{0,4},{1,5},{2,6},{3,7},{4,0},{5,1},{6,2},{7,3},{8,12},{9,13},{10,... | collective-permute-start | bytes 1253384 | tf_op jit(solution)/shard_map/ppermute | solution.py:438
  176.5 10.4 %collective-permute-start.31 = (bf16[1024,512]{1,0:T(8,128)(2,1)}, bf16[1024,512]{1,0:T(8,128)(2,1)}, u32[]{:S(2)}, u32[]{:S(2)}) collective-permute-start(bf16[1024,512]{1,0:T(8,128)(2,1)} %constant_dynamic-update-slice_fusion.3.own_ref), channel_id=1, source_target_pairs={{0,16},{16,0},{1,17},{17,1},{2,18},{18,2},{3,19},{19,3},{4,20},{20... | collective-permute-start | bytes 3145736 | tf_op jit(solution)/shard_map/ppermute | solution.py:435
  185.0 5.9 %collective-permute-start.29 = (bf16[264,1536]{1,0:T(8,128)(2,1)S(1)}, bf16[264,1536]{1,0:T(8,128)(2,1)S(1)}, u32[]{:S(2)}, u32[]{:S(2)}) collective-permute-start(bf16[264,1536]{1,0:T(8,128)(2,1)S(1)} %concatenate.107), channel_id=1, source_target_pairs={{0,16},{16,0},{1,17},{17,1},{2,18},{18,2},{3,19},{19,3},{4,20},{20... | collective-permute-start | bytes 2433032 | tf_op jit(solution)/shard_map/ppermute | solution.py:435
  185.8 10.2 %collective-permute-start.30 = (bf16[256,2560]{1,0:T(8,128)(2,1)S(1)}, bf16[256,2560]{1,0:T(8,128)(2,1)}, u32[]{:S(2)}, u32[]{:S(2)}) collective-permute-start(bf16[256,2560]{1,0:T(8,128)(2,1)S(1)} %copy-done.3), channel_id=1, source_target_pairs={{0,16},{16,0},{1,17},{17,1},{2,18},{18,2},{3,19},{19,3},{4,20},{20... | collective-permute-start | bytes 3932168 | tf_op jit(solution)/shard_map/ppermute | solution.py:435
  (10 other events, 47.3 us)

commit v3 on v2

--- a/solution.py
+++ b/solution.py
@@ -37,6 +37,7 @@
 BF = jnp.bfloat16
 F32 = jnp.float32
 VMEM_LIMIT = 60 * 1024 * 1024
+FINISH_VMEM = 60 * 1024 * 1024
 
 
 def dot(a, b):
@@ -114,24 +115,19 @@
 
 
 def project_kernel(
-    frames, memory, halo, gain, query_w, key_w, value_w, pick_query, pick_key, pick_carry,
+    frames, memory, gain, query_w, key_w, value_w, pick_query, pick_key, pick_carry,
     query_rows, key_rows, query, window,
     carry_rows, carry_pair,
 ):
     step = pl.program_id(0)
-    width = query_w.shape[0]
 
     @pl.when(step == 0)
     def _():
-        raw = halo[...].astype(F32)
-        unit, _ = row_stats(raw)
-        is_frame = lax.broadcasted_iota(jnp.int32, raw.shape, 0) < CARRY_FRAMES
-        carried = jnp.where(is_frame, unit * gain[...], raw).astype(BF)
-        carry_rows[...] = carried
-        carry_pair[:, :width] = dot(carried, key_w[...]).astype(BF)
-        carry_pair[:, width:] = dot(carried, value_w[...]).astype(BF)
+        carry_rows[...] = jnp.zeros_like(carry_rows)
+        carry_pair[...] = jnp.zeros_like(carry_pair)
 
     memories = memory[...].astype(F32)
+    asks, keys = [], []
     for p, part in enumerate(by_part(frames[...].astype(F32))):
         unit, _ = row_stats(part)
         normed = unit * gain[...]
@@ -140,19 +136,34 @@
             mean = mean + normed[f * PART : (f + 1) * PART]
         mean = mean * (1.0 / SEGLEN)
         blank = jnp.zeros_like(mean)
-        asks = jnp.concatenate([normed, mean, blank], axis=0).astype(BF)
-        keys = jnp.concatenate([normed, memories[p * PART : (p + 1) * PART], blank], axis=0).astype(BF)
-        query_rows[p * PART_ROWS : (p + 1) * PART_ROWS] = asks
+        asks += [normed, mean, blank]
+        keys += [normed, memories[p * PART : (p + 1) * PART], blank]
+    asks = jnp.concatenate(asks, axis=0).astype(BF)
+    keys = jnp.concatenate(keys, axis=0).astype(BF)
+    query_rows[...] = asks
+    asked = (dot(asks, query_w[...]) * 0.125).astype(BF)
+    pair = jnp.concatenate([dot(keys, key_w[...]), dot(keys, value_w[...])], axis=1).astype(BF)
+    for p in range(PARTS):
+        part = slice(p * PART_ROWS, (p + 1) * PART_ROWS)
         at = p * (PART_ROWS + CARRY)
-        key_rows[at : at + PART_ROWS] = keys
+        key_rows[at : at + PART_ROWS] = keys[part]
         key_rows[at + PART_ROWS : at + PART_ROWS + CARRY] = carry_rows[...]
-        asked = (dot(asks, query_w[...]) * 0.125).astype(BF)
-        query[p * PART_TILES : (p + 1) * PART_TILES] = dot(pick_query[...], asked).astype(BF)
-        pair = jnp.concatenate([dot(keys, key_w[...]), dot(keys, value_w[...])], axis=1).astype(BF)
-        both = jnp.concatenate([pair, carry_pair[...]], axis=0)
+        query[p * PART_TILES : (p + 1) * PART_TILES] = dot(pick_query[...], asked[part]).astype(BF)
+        both = jnp.concatenate([pair[part], carry_pair[...]], axis=0)
         window[p * PART_TILES : (p + 1) * PART_TILES] = dot(pick_key[...], both).astype(BF)
-        carry_rows[...] = dot(pick_carry[...], keys).astype(BF)
-        carry_pair[...] = dot(pick_carry[...], pair).astype(BF)
+        carry_rows[...] = dot(pick_carry[...], keys[part]).astype(BF)
+        carry_pair[...] = dot(pick_carry[...], pair[part]).astype(BF)
+
+
+def halo_kernel(halo, gain, key_w, value_w, pick_late, key_rows_in, window_in, key_rows, window):
+    raw = halo[...].astype(F32)
+    unit, _ = row_stats(raw)
+    is_frame = lax.broadcasted_iota(jnp.int32, raw.shape, 0) < CARRY_FRAMES
+    carried = jnp.where(is_frame, unit * gain[...], raw).astype(BF)
+    key_rows[:PART_ROWS] = key_rows_in[:PART_ROWS]
+    key_rows[PART_ROWS:] = carried
+    pair = jnp.concatenate([dot(carried, key_w[...]), dot(carried, value_w[...])], axis=1).astype(BF)
+    window[...] = (window_in[...].astype(F32) + dot(pick_late[...], pair)).astype(BF)
 
 
 def two_heads(rows):
@@ -172,9 +183,9 @@
 
 
 def forward_kernel(
-    position, need, segment_of, unpick_query, query, window, frames, out_grad,
-    out_w, up_w, down_w, middle_gain, output_gain,
-    attended, soft, residual_out, slope, grad_combined_out, result, memory_out, grad_down, grad_gain,
+    core, position, need, segment_of, unpick_query, query, window, frames, out_grad,
+    middle_gain, output_gain, out_w, up_w, down_w,
+    attended, soft, residual_out, slope, grad_combined_out, result, memory_out, down_keep, down_send, grad_gain,
     turned, hidden, grad_ff_rows,
 ):
     step = pl.program_id(0)
@@ -217,7 +228,6 @@
     residual_out[...] = residual
     unit, _ = row_stats(residual)
     middle = (unit * middle_gain[...]).astype(BF)
-    combined = residual
     span = pl.ds(pl.multiple_of(step * ROWS, ROWS), ROWS)
     for c in range(ff // width):
         columns = slice(c * width, (c + 1) * width)
@@ -225,7 +235,7 @@
         part = part.astype(BF)
         hidden[span, columns] = part
         slope[:, columns] = turn.astype(BF)
-        combined = combined + dot(part, down_w[columns])
+    combined = residual + dot(hidden[span], down_w[...])
     unit, scale = row_stats(combined)
     final = unit * output_gain[...]
     result[...] = by_frame([final[p * PART_FRAMES : (p + 1) * PART_FRAMES] for p in range(PARTS)]).astype(BF)
@@ -244,14 +254,15 @@
 
     @pl.when(step == steps - 1)
     def _():
-        for c in range(ff // width):
-            columns = slice(c * width, (c + 1) * width)
-            grad_down[columns] = dot_outer(hidden[:, columns], grad_ff_rows[...]).astype(BF)
+        for half, out in ((core[0], down_keep), (1 - core[0], down_send)):
+            for c in range(ff // width // 2):
+                columns = pl.ds(pl.multiple_of(half * (ff // 2) + c * width, width), width)
+                out[c * width : (c + 1) * width] = dot_outer(hidden[:, columns], grad_ff_rows[...]).astype(BF)
 
 
 def backward_kernel(
-    slope, grad_combined, residual, attended, memory_grad, out_w, up_w, down_w, middle_gain,
-    grad_residual_out, grad_attended, grad_up_out, grad_gain,
+    core, slope, grad_combined, residual, attended, memory_grad, middle_gain, out_w, up_w, down_w,
+    grad_residual_out, grad_attended, up_keep, up_send, grad_gain,
     lifted, middle_rows, out_sum,
 ):
     step = pl.program_id(0)
@@ -263,12 +274,11 @@
     middle_rows[span] = (unit * middle_gain[...]).astype(BF)
     grad_combined_rows = grad_combined[...]
     grad_ff = grad_combined_rows.astype(BF)
-    grad_middle = jnp.zeros_like(unit)
     for c in range(ff // width):
         columns = slice(c * width, (c + 1) * width)
         part = (dot_back(grad_ff, down_w[columns]) * slope[:, columns].astype(F32)).astype(BF)
         lifted[span, columns] = part
-        grad_middle = grad_middle + dot_back(part, up_w[:, columns])
+    grad_middle = dot_back(lifted[span], up_w[...])
     grad_norm, gain_part = norm_back(unit, scale, middle_gain[...], grad_middle)
     grad_residual = grad_combined_rows + grad_norm
     grad_residual_out[...] = grad_residual
@@ -293,16 +303,16 @@
 
     @pl.when(step == steps - 1)
     def _():
-        grad_up_out[:, ff:] = out_sum[...].astype(BF)
-        for c in range(ff // width):
-            columns = slice(c * width, (c + 1) * width)
-            grad_up_out[:, columns] = dot_outer(middle_rows[...], lifted[:, columns]).astype(BF)
+        for half, out in ((core[0], up_keep), (1 - core[0], up_send)):
+            rows = pl.ds(pl.multiple_of(half * (width // 2), width // 2), width // 2)
+            out[:, :ff] = dot_outer(middle_rows[:, rows], lifted[...]).astype(BF)
+            out[:, ff:] = out_sum[rows].astype(BF)
 
 
 def attention_back_kernel(
-    pick_query, unpick_query, unpick_key, query_rows, key_rows, query, window, soft, grad_attended,
-    grad_query_rows, grad_pair, grad_carry, grad_projections,
-    turned, grad_window, query_sum, pair_sum,
+    core, pick_query, unpick_query, unpick_key, query_rows, key_rows, query, window, soft, grad_attended,
+    grad_query_rows, grad_pair, grad_carry, projections_keep, projections_send,
+    turned, grad_window, both_rows, query_sum, pair_sum,
 ):
     step = pl.program_id(0)
     steps = pl.num_programs(0)
@@ -340,13 +350,16 @@
         both = dot(unpick_key[...], grad_window[...]).astype(BF)
         grad_pair[part] = both[:PART_ROWS]
         grad_carry[p * CARRY : (p + 1) * CARRY] = both[PART_ROWS:]
-        query_sum[...] += dot_outer(query_rows[part], grad_asks)
-        pair_sum[...] += dot_outer(key_rows[p * (PART_ROWS + CARRY) : (p + 1) * (PART_ROWS + CARRY)], both)
+        both_rows[p * (PART_ROWS + CARRY) : (p + 1) * (PART_ROWS + CARRY)] = both
+    query_sum[...] += dot_outer(query_rows[...], grad_query_rows[...])
+    pair_sum[...] += dot_outer(key_rows[...], both_rows[...])
 
     @pl.when(step == steps - 1)
     def _():
-        grad_projections[:, :width] = (query_sum[...] * 0.125).astype(BF)
-        grad_projections[:, width:] = pair_sum[...].astype(BF)
+        for half, out in ((core[0], projections_keep), (1 - core[0], projections_send)):
+            rows = pl.ds(pl.multiple_of(half * (width // 2), width // 2), width // 2)
+            out[:, :width] = (query_sum[rows] * 0.125).astype(BF)
+            out[:, width:] = pair_sum[rows].astype(BF)
 
 
 def projection_back_kernel(
@@ -444,8 +457,9 @@
 
 
 class Sum:
-    def __init__(self, values, turn):
-        self.values = values
+    def __init__(self, keep, send, turn):
+        self.values = keep
+        self.first = send
         self.turn = turn
         self.steps = chain(turn)
         self.done = 0
@@ -455,11 +469,14 @@
         count = len(self.steps)
         if self.done < count:
             stage = self.steps[self.done]
-            rows = self.values.shape[0] // 2
-            own = side(stage)
-            self.values, send = (
-                lax.dynamic_slice_in_dim(self.values, half * rows, rows, 0) for half in (own, 1 - own)
-            )
+            if self.done == 0:
+                send = self.first
+            else:
+                rows = self.values.shape[0] // 2
+                own = side(stage)
+                self.values, send = (
+                    lax.dynamic_slice_in_dim(self.values, half * rows, rows, 0) for half in (own, 1 - own)
+                )
         else:
             stage = self.steps[2 * count - 1 - self.done]
             send = self.values
@@ -493,40 +510,36 @@
         return self.done == 2 * len(self.steps)
 
 
-def shares(turn):
-    place = lax.axis_index("seg")
+def shares(turn, core, place):
     found = []
-    for core in range(2):
+    for which in range(2):
         share = 0
         for stage in chain(turn)[1:]:
-            share = share * 2 + place // stage[core] % 2
+            share = share * 2 + place // stage[which] % 2
         found.append(share)
-    core = lax.axis_index("grp")
-    own = jnp.where(core == 0, found[0], found[1])
-    other = jnp.where(core == 0, found[1], found[0])
-    return jnp.stack([core, own, other])
-
-
-def finish(total, widths):
+    return jnp.where(core == 0, found[0], found[1]), jnp.where(core == 0, found[1], found[0])
+
+
+def finish(total, widths, device):
     own, other = total.values, total.other
     half = own.shape[0]
     count = lax.axis_size("seg")
     rows = half // count
-    place = shares(total.turn)
     cuts = np.cumsum(widths)[:-1].tolist()
     if rows % 16:
         index = jnp.arange(count, dtype=jnp.int32)
         mine, theirs = (
-            jnp.take(part.reshape(count, rows, -1), index ^ place[i], axis=0).reshape(half, -1)
-            for part, i in ((own, 1), (other, 2))
+            jnp.take(part.reshape(count, rows, -1), index ^ share, axis=0).reshape(half, -1)
+            for part, share in zip((own, other[:half]), shares(total.turn, device[0], device[1]))
         )
-        whole = jnp.where(place[0] == 0, jnp.concatenate([mine, theirs]), jnp.concatenate([theirs, mine]))
+        whole = jnp.where(device[0] == 0, jnp.concatenate([mine, theirs]), jnp.concatenate([theirs, mine]))
         return jnp.split(whole.astype(F32), cuts, axis=1)
     halves = 2
 
-    def kernel(place_ref, own_ref, other_ref, *outs):
+    def kernel(device_ref, own_ref, other_ref, *outs):
         step = pl.program_id(0)
-        mine = (step // halves) == place_ref[0]
+        mine = (step // halves) == device_ref[0]
+        own_share, other_share = shares(total.turn, device_ref[0], device_ref[1])
 
         def fill(source, share):
             for j in range(count // halves):
@@ -539,25 +552,25 @@
 
         @pl.when(mine)
         def _():
-            fill(own_ref, place_ref[1])
+            fill(own_ref, own_share)
 
         @pl.when(jnp.logical_not(mine))
         def _():
-            fill(other_ref, place_ref[2])
+            fill(other_ref, other_share)
 
     return pl.pallas_call(
         kernel,
         grid=(2 * halves,),
-        in_specs=[pl.BlockSpec(memory_space=pltpu.SMEM)] + [pl.BlockSpec(own.shape, lambda i: (0, 0))] * 2,
+        in_specs=[pl.BlockSpec(memory_space=pltpu.SMEM)] + [pl.BlockSpec(part.shape, lambda i: (0, 0)) for part in (own, other)],
         out_specs=[pl.BlockSpec((half // halves, w), lambda i: (i, 0)) for w in widths],
         out_shape=[jax.ShapeDtypeStruct((2 * half, w), F32) for w in widths],
-        compiler_params=pltpu.CompilerParams(vmem_limit_bytes=VMEM_LIMIT),
+        compiler_params=pltpu.CompilerParams(vmem_limit_bytes=FINISH_VMEM),
         cost_estimate=cost(3),
         name="finish",
-    )(place, own, other)
-
-
-def call(kernel, steps, operands, outs, scratch, us):
+    )(device, own, other)
+
+
+def call(kernel, steps, operands, outs, scratch, us, aliases=None):
     def spec(shape, block):
         if isinstance(block, pl.BlockSpec):
             return block
@@ -574,6 +587,7 @@
         out_specs=[spec(shape, block) for _, shape, block in outs],
         out_shape=[jax.ShapeDtypeStruct(shape, dtype) for dtype, shape, _ in outs],
         scratch_shapes=[pltpu.VMEM(shape, dtype) for dtype, shape in scratch],
+        input_output_aliases=aliases or {},
         compiler_params=pltpu.CompilerParams(vmem_limit_bytes=VMEM_LIMIT),
         cost_estimate=cost(us),
         name=kernel.__name__,
@@ -592,7 +606,9 @@
     tiles = slots // GROUP
     pick_query, pick_key, pick_carry, need, segment_of = tables()
     unpick_query, unpick_key, unpick_carry = (jnp.asarray(pick.T, BF) for pick in (pick_query, pick_key, pick_carry))
+    pick_late = jnp.asarray(pick_key[:, PART_ROWS:], BF)
     pick_query, pick_key, pick_carry = (jnp.asarray(pick, BF) for pick in (pick_query, pick_key, pick_carry))
+    device = jnp.stack([lax.axis_index("grp"), lax.axis_index("seg")]).astype(jnp.int32)
     need, segment_of = jnp.asarray(need), jnp.asarray(segment_of)
     input_gain, middle_gain, output_gain = (g.reshape(1, width) for g in (input_gain, middle_gain, output_gain))
     frames = jnp.transpose(frames_in, (1, 0, 2))
@@ -615,7 +631,7 @@
         project_kernel,
         steps,
         [
-            (frames, slab), (memory, (BLOCK, width)), (halo, None), (input_gain, None),
+            (frames, slab), (memory, (BLOCK, width)), (input_gain, None),
             (query_weight, None), (key_weight, None), (value_weight, None),
             (pick_query, None), (pick_key, None), (pick_carry, None),
         ],
@@ -626,16 +642,31 @@
             (BF, (tiles * TILE, 2 * width), (TILES, 2 * width)),
         ],
         [(BF, (CARRY, width)), (BF, (CARRY, 2 * width))],
-        8,
-    )
-
-    attended, soft, residual, slope, grad_combined, result, memory_out, grad_down, output_part = call(
+        10,
+    )
+
+    key_block = pl.BlockSpec((PART_ROWS + CARRY, width), lambda i: (0, 0))
+    window_block = pl.BlockSpec((PART_TILES, 2 * width), lambda i: (0, 0))
+    key_rows, window = call(
+        halo_kernel,
+        1,
+        [
+            (halo, None), (input_gain, None), (key_weight, None), (value_weight, None), (pick_late, None),
+            (key_rows, key_block), (window, window_block),
+        ],
+        [(BF, key_rows.shape, key_block), (BF, window.shape, window_block)],
+        [],
+        2,
+        {5: 0, 6: 1},
+    )
+
+    attended, soft, residual, slope, grad_combined, result, memory_out, keep, send, output_part = call(
         forward_kernel,
         steps,
         [
-            (position, smem), (need, None), (segment_of, None), (unpick_query, None),
+            (device, smem), (position, smem), (need, None), (segment_of, None), (unpick_query, None),
             (query, (TILES, width)), (window, (TILES, 2 * width)), (frames, slab), (pulls, slab),
-            (out_weight, None), (up_weight, None), (down_weight, None), (middle_gain, None), (output_gain, None),
+            (middle_gain, None), (output_gain, None), (out_weight, None), (up_weight, None), (down_weight, None),
         ],
         [
             (BF, (parts * PART_ROWS, width), (FULL, width)),
@@ -645,27 +676,29 @@
             (F32, (total, width), (ROWS, width)),
             (BF, (FRAMES, slots, width), slab),
             (BF, (slots, width), (BLOCK, width)),
-            (BF, (ff, width), None),
+            (BF, (ff // 2, width), None),
+            (BF, (ff // 2, width), None),
             (F32, (1, width), None),
         ],
         [(BF, (width, PART_TILES)), (BF, (total, ff)), (BF, (total, width))],
         24,
     )
 
-    down = Sum(grad_down, 2)
+    down = Sum(keep, send, 2)
     down.start()
 
-    grad_residual, grad_attended, grad_up_out, middle_part = call(
+    grad_residual, grad_attended, keep, send, middle_part = call(
         backward_kernel,
         steps,
         [
-            (slope, (ROWS, ff)), (grad_combined, (ROWS, width)), (residual, (ROWS, width)), (attended, (FULL, width)),
-            (memory_grad, (BLOCK, width)), (out_weight, None), (up_weight, None), (down_weight, None), (middle_gain, None),
+            (device, smem), (slope, (ROWS, ff)), (grad_combined, (ROWS, width)), (residual, (ROWS, width)), (attended, (FULL, width)),
+            (memory_grad, (BLOCK, width)), (middle_gain, None), (out_weight, None), (up_weight, None), (down_weight, None),
         ],
         [
             (F32, (total, width), (ROWS, width)),
             (BF, (parts * PART_ROWS, width), (FULL, width)),
-            (BF, (width, ff + width), None),
+            (BF, (width // 2, ff + width), None),
+            (BF, (width // 2, ff + width), None),
             (F32, (1, width), None),
         ],
         [(BF, (total, ff)), (BF, (total, width)), (F32, (width, width))],
@@ -674,15 +707,15 @@
 
     down.land()
     down.values, grad_attended = lax.optimization_barrier((down.values, grad_attended))
-    up = Sum(grad_up_out, 0)
+    up = Sum(keep, send, 0)
     up.start()
     down.start()
 
-    grad_query_rows, grad_pair, grad_carry, grad_projections = call(
+    grad_query_rows, grad_pair, grad_carry, keep, send = call(
         attention_back_kernel,
         steps,
         [
-            (pick_query, None), (unpick_query, None), (unpick_key, None),
+            (device, smem), (pick_query, None), (unpick_query, None), (unpick_key, None),
             (query_rows, (FULL, width)), (key_rows, (PARTS * (PART_ROWS + CARRY), width)),
             (query, (TILES, width)), (window, (TILES, 2 * width)),
             (soft, (TILES * PAIRS, 2 * TILE)), (grad_attended, (FULL, width)),
@@ -691,25 +724,26 @@
             (BF, (parts * PART_ROWS, width), (FULL, width)),
             (BF, (parts * PART_ROWS, 2 * width), (FULL, 2 * width)),
             (BF, (parts * CARRY, 2 * width), (PARTS * CARRY, 2 * width)),
-            (BF, (width, 3 * width), None),
-        ],
-        [
-            (BF, (width, PART_TILES)), (BF, (PART_TILES, 2 * width)), (F32, (width, width)), (F32, (width, 2 * width)),
+            (BF, (width // 2, 3 * width), None),
+            (BF, (width // 2, 3 * width), None),
+        ],
+        [
+            (BF, (width, PART_TILES)), (BF, (PART_TILES, 2 * width)), (BF, (PARTS * (PART_ROWS + CARRY), 2 * width)),
+            (F32, (width, width)), (F32, (width, 2 * width)),
         ],
         12,
     )
 
-    projections = Sum(grad_projections, 2)
     down.land()
     up.land()
-    down.values, up.values, projections.values, grad_carry = lax.optimization_barrier(
-        (down.values, up.values, projections.values, grad_carry)
-    )
+    down.values, up.values, keep, send, grad_carry = lax.optimization_barrier(
+        (down.values, up.values, keep, send, grad_carry)
+    )
+    projections = Sum(keep, send, 0)
     sent = projections.start()
     carry_next = shift(grad_carry[:CARRY], "seg", -1)
     sent = up.start(sent)
     sent = down.start(sent)
-
     grad_frames, grad_memory, input_part = call(
         projection_back_kernel,
         steps,
@@ -735,6 +769,9 @@
     up.land(sent, gains)
     projections.row = None
     order = (up, down, projections)
+    cuts = {up: [ff, width], down: [width], projections: [width] * 3}
+    ready = {}
+    held = ()
     turn = 0
     while not all(one.complete() for one in order):
         one = order[turn % 3]
@@ -742,15 +779,18 @@
         if one.complete():
             continue
         if turn > 1:
-            one.land(sent)
+            one.land(sent, *(held if one is projections else ()))
         if one is projections and one.done == len(one.steps):
             one.row = gains
-        if not one.complete():
+        if one.complete():
+            ready[one] = finish(one, cuts[one], device)
+            held = held + tuple(ready[one])
+        else:
             sent = one.start(sent)
     gains = projections.row
-    (grad_down,) = finish(down, [width])
-    grad_up, grad_out = finish(up, [ff, width])
-    grad_query, grad_key, grad_value = finish(projections, [width] * 3)
+    (grad_down,) = ready[down]
+    grad_up, grad_out = ready[up]
+    grad_query, grad_key, grad_value = ready[projections]
     gains = gains.reshape(3, width)
     return (
         result, memory_out, grad_frames, grad_memory,

time: 201 us -> 187 us (0.930)
  waiting for transfers between devices: 38.1 us -> 30.4 us
  local copies, waits for them, and re-layouts: 22.1 us -> 17.5 us
    ppermute x2, waiting for transfers between devices: 4.67 us -> 0.01 us  [shift(): lax.ppermute(values, axis, [(i, (i + by) % size) for i in range(size)])]
    dynamic_slice x15 -> x12, local copies, waits for them, and re-layouts: 5.62 us -> 1.92 us  [start(): lax.dynamic_slice_in_dim(self.values, half * rows, rows, 0)]
    ppermute x24, waiting for transfers between devices: 33.4 us -> 30.4 us  [swap(): return lax.ppermute(values, ('grp', 'seg'), pairs)]
    pallas_call x5 -> x6, Pallas kernels: 86.8 us -> 85.8 us  [call(): pl.pallas_call(kernel, grid=(steps,), in_specs=[spec(array.shape, block)...]
    unnamed x28 -> x26, local copies, waits for them, and re-layouts: 6.94 us -> 6.06 us
  transfers between devices with their start and end apart: 32 -> 32, of which waited for: 14 -> 15; matrix products, arithmetic and copies ran while one was open for 13% -> 11% of each run, Pallas kernels for 27% -> 34%
where the time goes in v3:
time: 187 us; the launch traced here: 186 us
  Pallas kernels  98.1 us (52%)
  waiting for transfers between devices  30.4 us (16%)
  starting transfers between devices  29.3 us (16%)
  local copies, waits for them, and re-layouts  17.5 us (9%)
  other arithmetic  9.18 us (5%)
    pallas_call x6, Pallas kernels, call(): pl.pallas_call(kernel, grid=(steps,), in_specs=[spec(array.shape, block)...  85.8 us
    ppermute x24, waiting for transfers between devices, swap(): return lax.ppermute(values, ('grp', 'seg'), pairs)  30.4 us
    ppermute x24, starting transfers between devices, swap(): return lax.ppermute(values, ('grp', 'seg'), pairs)  21.3 us
    pallas_call x3, Pallas kernels, finish(): pl.pallas_call(kernel, grid=(2 * halves,), in_specs=[pl.BlockSpec(memory_...  12.3 us
    ppermute x2, starting transfers between devices, shift(): lax.ppermute(values, axis, [(i, (i + by) % size) for i in range(size)])  7.3 us
    unnamed x26, local copies, waits for them, and re-layouts  6.06 us
    convert_element_type x12, other arithmetic, land(): (self.values.astype(F32) + other.astype(F32)).astype(self.values.dtype)  4.93 us
  transfers between devices with their start and end apart: 32, of which 15 were waited for; matrix products, arithmetic and copies ran while one was open for 11% of the time, Pallas kernels for 34%

profile of v3, /device:TPU:0, one launch (start us, length us, event | category | flops | bytes accessed | tf_op | source)
XLA Modules:
  0.0 185.6 jit_solution(8634648864056626618)
XLA Ops:
  2.5 3.0 %collective-permute-start = (bf16[48,512]{1,0:T(8,128)(2,1)S(1)}, bf16[48,512]{1,0:T(8,128)(2,1)S(1)}, u32[]{:S(2)}, u32[]{:S(2)}) collective-permute-start(bf16[48,512]{1,0:T(8,128)(2,1)S(1)} %maximum_maximum_fusion), channel_id=1, source_target_pairs={{0,1},{1,2},{2,3},{3,4},{4,5},{5,6},{6,7},{7,8},{8,9},{9,10},{10,1... | collective-permute-start | bytes 147464 | tf_op jit(solution)/shard_map/ppermute | solution.py:421
  6.9 9.2 %project_kernel.1 = (bf16[1408,512]{1,0:T(8,128)(2,1)}, bf16[1792,512]{1,0:T(8,128)(2,1)}, bf16[2048,512]{1,0:T(8,128)(2,1)}, bf16[2048,1024]{1,0:T(8,128)(2,1)}) custom-call(bf16[20,64,512]{2,1,0:T(8,128)(2,1)} %bitcast.17, bf16[64,512]{1,0:T(8,128)(2,1)} %memory.1, f32[1,512]{1,0:T(1,128)} %bitcast.24, bf16[512,512]{1,0:T(8,128)(2,1)} %query_w.3, ...), custom_call_target="tpu_custom_call" | custom-call | flops 10000000000 | bytes 1000000 | tf_op jit(solution)/shard_map/project_kernel/pallas_call | solution.py:583
  17.3 2.9 %halo_kernel.1 = (bf16[1792,512]{1,0:T(8,128)(2,1)}, bf16[2048,1024]{1,0:T(8,128)(2,1)}) custom-call(bf16[48,512]{1,0:T(8,128)(2,1)} %copy-done.8, f32[1,512]{1,0:T(1,128)} %bitcast.25, bf16[512,512]{1,0:T(8,128)(2,1)} %key_w.5, bf16[512,512]{1,0:T(8,128)(2,1)} %value_w.5, ...), custom_call_target="tpu_custom_call", output_to_operand_aliasing={{0}: (5, {}), {1}: (6, {})} | custom-call | flops 2000000000 | bytes 200000 | tf_op jit(solution)/shard_map/halo_kernel/pallas_call | solution.py:583
  20.2 28.3 %forward_kernel.1 = (bf16[1408,512]{1,0:T(8,128)(2,1)}, bf16[8192,256]{1,0:T(8,128)(2,1)}, f32[1280,512]{1,0:T(8,128)}, bf16[1280,2048]{1,0:T(8,128)(2,1)}, f32[...) custom-call(s32[2]{0:T(128)} %pad_add_fusion.core.device_ref, ...), custom_call_target="tpu_custom_call" | custom-call | flops 24000000000 | bytes 2400000 | tf_op jit(solution)/shard_map/forward_kernel/pallas_call | solution.py:583
  48.6 18.4 %backward_kernel.1 = (f32[1280,512]{1,0:T(8,128)}, bf16[1408,512]{1,0:T(8,128)(2,1)}, bf16[256,2560]{1,0:T(8,128)(2,1)}, bf16[256,2560]{1,0:T(8,128)(2,1)}, f32[1,512]{1,0:T(1,128)}) custom-call(s32[2]{0:T(128)} %pad_add_fusion.core.device_ref, bf16[1280,2048]{1,0:T(8,128)(2,1)} %get-tuple-element.118.slope, f32[1280,512]{1,0:T(8,128)} %get-tuple-element.119.grad_combined, ...), custom_call_target="tpu_custom_call" | custom-call | flops 16000000000 | bytes 1600000 | tf_op jit(solution)/shard_map/backward_kernel/pallas_call | solution.py:583
  68.7 1.6 collective-permute-start.2
  70.3 18.0 %attention_back_kernel.1 = (bf16[1408,512]{1,0:T(8,128)(2,1)}, bf16[1408,1024]{1,0:T(8,128)(2,1)}, bf16[384,1024]{1,0:T(8,128)(2,1)}, bf16[256,1536]{1,0:T(8,128)(2,1)}, bf16[256,1536]{1,0:T(8,128)(2,1)}) custom-call(s32[2]{0:T(128)} %pad_add_fusion.core.device_ref, bf16[256,176]{1,0:T(8,128)(2,1)} %constant.196.clone.pick_query, ...), custom_call_target="tpu_custom_call" | custom-call | flops 12000000000 | bytes 1200000 | tf_op jit(solution)/shard_map/attention_back_kernel/pallas_call | solution.py:583
  88.3 1.6 add_convert_fusion
  92.0 4.3 %collective-permute-start.4 = (bf16[48,1024]{1,0:T(8,128)(2,1)S(1)}, bf16[48,1024]{1,0:T(8,128)(2,1)S(1)}, u32[]{:S(2)}, u32[]{:S(2)}) collective-permute-start(bf16[48,1024]{1,0:T(8,128)(2,1)S(1)} %slice.68), channel_id=1, source_target_pairs={{0,15},{1,0},{2,1},{3,2},{4,3},{5,4},{6,5},{7,6},{8,7},{9,8},{10,9... | collective-permute-start | bytes 294920 | tf_op jit(solution)/shard_map/ppermute | solution.py:421
  97.2 2.1 %collective-permute-start.7 = (bf16[256,512]{1,0:T(8,128)(2,1)S(1)}, bf16[256,512]{1,0:T(8,128)(2,1)S(1)}, u32[]{:S(2)}, u32[]{:S(2)}) collective-permute-start(bf16[256,512]{1,0:T(8,128)(2,1)S(1)} %constant_dynamic-slice_fusion.10), channel_id=1, source_target_pairs={{0,1},{1,0},{2,3},{3,2},{4,5},{5,4},{6,7},{7,6},{8,9},{9,8},{10,11... | collective-permute-start | bytes 786440 | tf_op jit(solution)/shard_map/ppermute | solution.py:451
  100.0 8.9 %projection_back_kernel.1 = (f32[20,64,512]{2,1,0:T(8,128)}, bf16[64,512]{1,0:T(8,128)(2,1)}, f32[1,512]{1,0:T(1,128)}) custom-call(bf16[176,48]{1,0:T(8,128)(2,1)} %constant.194.clone.unpick_carry, bf16[1408,1024]{1,0:T(8,128)(2,1)} %get-tuple-element.124.grad_pair, bf16[384,1024]{1,0:T(8,128)(2,1)} %get-tuple-element.131.grad_carry, ...), custom_call_target="tpu_custom_call" | custom-call | flops 8000000000 | bytes 800000 | tf_op jit(solution)/shard_map/projection_back_kernel/pallas_call | solution.py:583
  110.0 1.2 add_convert_fusion.3
  111.3 2.2 %collective-permute-start.11 = (bf16[64,2560]{1,0:T(8,128)(2,1)S(1)}, bf16[64,2560]{1,0:T(8,128)(2,1)S(1)}, u32[]{:S(2)}, u32[]{:S(2)}) collective-permute-start(bf16[64,2560]{1,0:T(8,128)(2,1)S(1)} %constant_dynamic-slice_fusion.7), channel_id=1, source_target_pairs={{0,2},{1,3},{2,0},{3,1},{4,6},{5,7},{6,4},{7,5},{8,10},{9,11},{10,... | collective-permute-start | bytes 983048 | tf_op jit(solution)/shard_map/ppermute | solution.py:451
  113.7 4.0 %collective-permute-done.6 = bf16[128,1536]{1,0:T(8,128)(2,1)S(1)} collective-permute-done((bf16[128,1536]{1,0:T(8,128)(2,1)S(1)}, bf16[128,1536]{1,0:T(8,128)(2,1)S(1)}, u32[]{:S(2)}, u32[]{:S(2)}) %collective-permute-start.6) | collective-permute-done | bytes 393248 | tf_op jit(solution)/shard_map/ppermute | solution.py:451
  118.1 2.1 %collective-permute-done.11 = bf16[64,2560]{1,0:T(8,128)(2,1)S(1)} collective-permute-done((bf16[64,2560]{1,0:T(8,128)(2,1)S(1)}, bf16[64,2560]{1,0:T(8,128)(2,1)S(1)}, u32[]{:S(2)}, u32[]{:S(2)}) %collective-permute-start.11) | collective-permute-done | bytes 327712 | tf_op jit(solution)/shard_map/ppermute | solution.py:451
  121.7 2.0 %collective-permute-start.13 = (bf16[64,512]{1,0:T(8,128)(2,1)S(1)}, bf16[64,512]{1,0:T(8,128)(2,1)S(1)}, u32[]{:S(2)}, u32[]{:S(2)}) collective-permute-start(bf16[64,512]{1,0:T(8,128)(2,1)S(1)} %constant_dynamic-slice_fusion.3), channel_id=1, source_target_pairs={{0,8},{1,9},{2,10},{3,11},{4,12},{5,13},{6,14},{7,15},{8,0},{9,1},... | collective-permute-start | bytes 196616 | tf_op jit(solution)/shard_map/ppermute | solution.py:451
  123.8 1.3 collective-permute-start.12
  125.9 1.3 collective-permute-start.17
  128.3 1.8 collective-permute-start.16
  131.3 2.6 %collective-permute-done.17 = bf16[16,2560]{1,0:T(8,128)(2,1)S(1)} collective-permute-done((bf16[16,2560]{1,0:T(8,128)(2,1)S(1)}, bf16[16,2560]{1,0:T(8,128)(2,1)S(1)}, u32[]{:S(2)}, u32[]{:S(2)}) %collective-permute-start.17) | collective-permute-done | bytes 81952 | tf_op jit(solution)/shard_map/ppermute | solution.py:451
  134.6 2.3 %collective-permute-done.16 = bf16[64,512]{1,0:T(8,128)(2,1)S(1)} collective-permute-done((bf16[64,512]{1,0:T(8,128)(2,1)S(1)}, bf16[64,512]{1,0:T(8,128)(2,1)S(1)}, u32[]{:S(2)}, u32[]{:S(2)}) %collective-permute-start.16) | collective-permute-done | bytes 65568 | tf_op jit(solution)/shard_map/ppermute | solution.py:451
  138.5 1.5 collective-permute-start.18
  140.0 2.1 %collective-permute-done.20 = bf16[16,2560]{1,0:T(8,128)(2,1)S(1)} collective-permute-done((bf16[16,2560]{1,0:T(8,128)(2,1)S(1)}, bf16[16,2560]{1,0:T(8,128)(2,1)S(1)}, u32[]{:S(2)}, u32[]{:S(2)}) %collective-permute-start.20) | collective-permute-done | bytes 81952 | tf_op jit(solution)/shard_map/ppermute | solution.py:451
  142.1 3.2 %collective-permute-start.23 = (bf16[32,2560]{1,0:T(8,128)(2,1)S(1)}, bf16[32,2560]{1,0:T(8,128)(2,1)S(1)}, u32[]{:S(2)}, u32[]{:S(2)}) collective-permute-start(bf16[32,2560]{1,0:T(8,128)(2,1)S(1)} %pad_maximum_fusion.4), channel_id=1, source_target_pairs={{0,4},{1,5},{2,6},{3,7},{4,0},{5,1},{6,2},{7,3},{8,12},{9,13},{10,... | collective-permute-start | bytes 491528 | tf_op jit(solution)/shard_map/ppermute | solution.py:451
  146.7 1.7 collective-permute-start.21
  150.9 4.2 %collective-permute-done.22 = bf16[256,512]{1,0:T(8,128)(2,1)S(1)} collective-permute-done((bf16[256,512]{1,0:T(8,128)(2,1)S(1)}, bf16[256,512]{1,0:T(8,128)(2,1)S(1)}, u32[]{:S(2)}, u32[]{:S(2)}) %collective-permute-start.22) | collective-permute-done | bytes 262176 | tf_op jit(solution)/shard_map/ppermute | solution.py:451
  158.1 6.5 %collective-permute-done.25 = bf16[512,512]{1,0:T(8,128)(2,1)} collective-permute-done((bf16[512,512]{1,0:T(8,128)(2,1)S(1)}, bf16[512,512]{1,0:T(8,128)(2,1)}, u32[]{:S(2)}, u32[]{:S(2)}) %collective-permute-start.25) | collective-permute-done | bytes 524320 | tf_op jit(solution)/shard_map/ppermute | solution.py:451
  164.5 1.9 %constant_dynamic-update-slice_fusion.3.own_ref = bf16[1024,512]{1,0:T(8,128)(2,1)} fusion(bf16[1024,512]{1,0:T(8,128)(2,1)} %constant_dynamic-update-slice_fusion.4, bf16[512,512]{1,0:T(8,128)(2,1)} %collective-permute-done.25), kind=kLoop, calls=%fused_computation.26 | loop fusion | bytes 1048576 | tf_op jit(solution)/shard_map/concatenate | solution.py:504
  169.5 4.2 %finish.3 = f32[2048,512]{1,0:T(8,128)} custom-call(s32[2]{0:T(128)} %pad_add_fusion.core.device_ref, bf16[1024,512]{1,0:T(8,128)(2,1)} %constant_dynamic-update-slice_fusion.3.own_ref, bf16[1024,512]{1,0:T(8,128)(2,1)} %collective-permute-done.29.other_ref), custom_call_target="tpu_custom_call" | custom-call | flops 3000000000 | bytes 300000 | tf_op jit(solution)/shard_map/finish/pallas_call | solution.py:561
  173.6 1.7 collective-permute-done.27
  175.9 4.5 %finish.4 = (f32[512,2048]{1,0:T(8,128)}, f32[512,512]{1,0:T(8,128)}) custom-call(s32[2]{0:T(128)} %pad_add_fusion.core.device_ref, bf16[256,2560]{1,0:T(8,128)(2,1)} %constant_dynamic-update-slice_fusion.8.own_ref, bf16[256,2560]{1,0:T(8,128)(2,1)} %collective-permute-done.31.other_ref), custom_call_target="tpu_custom_call" | custom-call | flops 3000000000 | bytes 300000 | tf_op jit(solution)/shard_map/finish/pallas_call | solution.py:561
  182.0 3.6 %finish.5 = (f32[512,512]{1,0:T(8,128)}, f32[512,512]{1,0:T(8,128)}, f32[512,512]{1,0:T(8,128)}) custom-call(s32[2]{0:T(128)} %pad_add_fusion.core.device_ref, bf16[256,1536]{1,0:T(8,128)(2,1)} %copy-done.4, bf16[256,1536]{1,0:T(8,128)(2,1)} %slice.81.other_ref), custom_call_target="tpu_custom_call" | custom-call | flops 3000000000 | bytes 300000 | tf_op jit(solution)/shard_map/finish/pallas_call | solution.py:561
  (137 shorter events, 30.2 us)
Async XLA Ops:
  2.5 14.2 %collective-permute-start = (bf16[48,512]{1,0:T(8,128)(2,1)S(1)}, bf16[48,512]{1,0:T(8,128)(2,1)S(1)}, u32[]{:S(2)}, u32[]{:S(2)}) collective-permute-start(bf16[48,512]{1,0:T(8,128)(2,1)S(1)} %maximum_maximum_fusion), channel_id=1, source_target_pairs={{0,1},{1,2},{2,3},{3,4},{4,5},{5,6},{6,7},{7,8},{8,9},{9,10},{10,1... | collective-permute-start | bytes 147464 | tf_op jit(solution)/shard_map/ppermute | solution.py:421
  48.5 19.0 %collective-permute-start.1 = (bf16[1024,512]{1,0:T(8,128)(2,1)}, bf16[1024,512]{1,0:T(8,128)(2,1)S(1)}, u32[]{:S(2)}, u32[]{:S(2)}) collective-permute-start(bf16[1024,512]{1,0:T(8,128)(2,1)} %get-tuple-element.117), channel_id=1, source_target_pairs={{0,16},{16,0},{1,17},{17,1},{2,18},{18,2},{3,19},{19,3},{4,20},{20... | collective-permute-start | bytes 3145736 | tf_op jit(solution)/shard_map/ppermute | solution.py:448
  67.0 21.2 %collective-permute-start.3 = (bf16[256,2560]{1,0:T(8,128)(2,1)}, bf16[256,2560]{1,0:T(8,128)(2,1)}, u32[]{:S(2)}, u32[]{:S(2)}) collective-permute-start(bf16[256,2560]{1,0:T(8,128)(2,1)} %get-tuple-element.127), channel_id=1, source_target_pairs={{0,16},{16,0},{1,17},{17,1},{2,18},{18,2},{3,19},{19,3},{4,20},{20... | collective-permute-start | bytes 3932168 | tf_op jit(solution)/shard_map/ppermute | solution.py:448
  68.7 21.2 %collective-permute-start.2 = (bf16[512,512]{1,0:T(8,128)(2,1)}, bf16[512,512]{1,0:T(8,128)(2,1)}, u32[]{:S(2)}, u32[]{:S(2)}) collective-permute-start(bf16[512,512]{1,0:T(8,128)(2,1)} %constant_dynamic-slice_fusion.11), channel_id=1, source_target_pairs={{0,4},{1,5},{2,6},{3,7},{4,0},{5,1},{6,2},{7,3},{8,12},{9,13},{10,... | collective-permute-start | bytes 1572872 | tf_op jit(solution)/shard_map/ppermute | solution.py:451
  92.0 7.3 %collective-permute-start.4 = (bf16[48,1024]{1,0:T(8,128)(2,1)S(1)}, bf16[48,1024]{1,0:T(8,128)(2,1)S(1)}, u32[]{:S(2)}, u32[]{:S(2)}) collective-permute-start(bf16[48,1024]{1,0:T(8,128)(2,1)S(1)} %slice.68), channel_id=1, source_target_pairs={{0,15},{1,0},{2,1},{3,2},{4,3},{5,4},{6,5},{7,6},{8,7},{9,8},{10,9... | collective-permute-start | bytes 294920 | tf_op jit(solution)/shard_map/ppermute | solution.py:421
  96.3 13.3 %collective-permute-start.5 = (bf16[256,1536]{1,0:T(8,128)(2,1)}, bf16[256,1536]{1,0:T(8,128)(2,1)S(1)}, u32[]{:S(2)}, u32[]{:S(2)}) collective-permute-start(bf16[256,1536]{1,0:T(8,128)(2,1)} %get-tuple-element.137), channel_id=1, source_target_pairs={{0,16},{16,0},{1,17},{17,1},{2,18},{18,2},{3,19},{19,3},{4,20},{20... | collective-permute-start | bytes 2359304 | tf_op jit(solution)/shard_map/ppermute | solution.py:448
  97.2 12.8 %collective-permute-start.8 = (bf16[128,2560]{1,0:T(8,128)(2,1)}, bf16[128,2560]{1,0:T(8,128)(2,1)}, u32[]{:S(2)}, u32[]{:S(2)}) collective-permute-start(bf16[128,2560]{1,0:T(8,128)(2,1)} %constant_dynamic-slice_fusion.9), channel_id=1, source_target_pairs={{0,1},{1,0},{2,3},{3,2},{4,5},{5,4},{6,7},{7,6},{8,9},{9,8},{10,11... | collective-permute-start | bytes 1966088 | tf_op jit(solution)/shard_map/ppermute | solution.py:451
  97.2 16.3 %collective-permute-start.7 = (bf16[256,512]{1,0:T(8,128)(2,1)S(1)}, bf16[256,512]{1,0:T(8,128)(2,1)S(1)}, u32[]{:S(2)}, u32[]{:S(2)}) collective-permute-start(bf16[256,512]{1,0:T(8,128)(2,1)S(1)} %constant_dynamic-slice_fusion.10), channel_id=1, source_target_pairs={{0,1},{1,0},{2,3},{3,2},{4,5},{5,4},{6,7},{7,6},{8,9},{9,8},{10,11... | collective-permute-start | bytes 786440 | tf_op jit(solution)/shard_map/ppermute | solution.py:451
  109.9 7.8 %collective-permute-start.6 = (bf16[128,1536]{1,0:T(8,128)(2,1)S(1)}, bf16[128,1536]{1,0:T(8,128)(2,1)S(1)}, u32[]{:S(2)}, u32[]{:S(2)}) collective-permute-start(bf16[128,1536]{1,0:T(8,128)(2,1)S(1)} %constant_dynamic-slice_fusion.8), channel_id=1, source_target_pairs={{0,1},{1,0},{2,3},{3,2},{4,5},{5,4},{6,7},{7,6},{8,9},{9,8},{10,11... | collective-permute-start | bytes 1179656 | tf_op jit(solution)/shard_map/ppermute | solution.py:451
  111.3 9.0 %collective-permute-start.11 = (bf16[64,2560]{1,0:T(8,128)(2,1)S(1)}, bf16[64,2560]{1,0:T(8,128)(2,1)S(1)}, u32[]{:S(2)}, u32[]{:S(2)}) collective-permute-start(bf16[64,2560]{1,0:T(8,128)(2,1)S(1)} %constant_dynamic-slice_fusion.7), channel_id=1, source_target_pairs={{0,2},{1,3},{2,0},{3,1},{4,6},{5,7},{6,4},{7,5},{8,10},{9,11},{10,... | collective-permute-start | bytes 983048 | tf_op jit(solution)/shard_map/ppermute | solution.py:451
  113.6 8.0 %collective-permute-start.10 = (bf16[128,512]{1,0:T(8,128)(2,1)S(1)}, bf16[128,512]{1,0:T(8,128)(2,1)S(1)}, u32[]{:S(2)}, u32[]{:S(2)}) collective-permute-start(bf16[128,512]{1,0:T(8,128)(2,1)S(1)} %constant_dynamic-slice_fusion.6), channel_id=1, source_target_pairs={{0,2},{1,3},{2,0},{3,1},{4,6},{5,7},{6,4},{7,5},{8,10},{9,11},{10,... | collective-permute-start | bytes 393224 | tf_op jit(solution)/shard_map/ppermute | solution.py:451
  117.9 5.9 %collective-permute-start.9 = (bf16[64,1536]{1,0:T(8,128)(2,1)S(1)}, bf16[64,1536]{1,0:T(8,128)(2,1)S(1)}, u32[]{:S(2)}, u32[]{:S(2)}) collective-permute-start(bf16[64,1536]{1,0:T(8,128)(2,1)S(1)} %constant_dynamic-slice_fusion.5), channel_id=1, source_target_pairs={{0,2},{1,3},{2,0},{3,1},{4,6},{5,7},{6,4},{7,5},{8,10},{9,11},{10,... | collective-permute-start | bytes 589832 | tf_op jit(solution)/shard_map/ppermute | solution.py:451
  120.3 5.5 %collective-permute-start.14 = (bf16[32,2560]{1,0:T(8,128)(2,1)S(1)}, bf16[32,2560]{1,0:T(8,128)(2,1)S(1)}, u32[]{:S(2)}, u32[]{:S(2)}) collective-permute-start(bf16[32,2560]{1,0:T(8,128)(2,1)S(1)} %constant_dynamic-slice_fusion.4), channel_id=1, source_target_pairs={{0,4},{1,5},{2,6},{3,7},{4,0},{5,1},{6,2},{7,3},{8,12},{9,13},{10,... | collective-permute-start | bytes 491528 | tf_op jit(solution)/shard_map/ppermute | solution.py:451
  121.7 5.9 %collective-permute-start.13 = (bf16[64,512]{1,0:T(8,128)(2,1)S(1)}, bf16[64,512]{1,0:T(8,128)(2,1)S(1)}, u32[]{:S(2)}, u32[]{:S(2)}) collective-permute-start(bf16[64,512]{1,0:T(8,128)(2,1)S(1)} %constant_dynamic-slice_fusion.3), channel_id=1, source_target_pairs={{0,8},{1,9},{2,10},{3,11},{4,12},{5,13},{6,14},{7,15},{8,0},{9,1},... | collective-permute-start | bytes 196616 | tf_op jit(solution)/shard_map/ppermute | solution.py:451
  123.8 6.4 %collective-permute-start.12 = (bf16[32,1536]{1,0:T(8,128)(2,1)S(1)}, bf16[32,1536]{1,0:T(8,128)(2,1)S(1)}, u32[]{:S(2)}, u32[]{:S(2)}) collective-permute-start(bf16[32,1536]{1,0:T(8,128)(2,1)S(1)} %constant_dynamic-slice_fusion.2), channel_id=1, source_target_pairs={{0,4},{1,5},{2,6},{3,7},{4,0},{5,1},{6,2},{7,3},{8,12},{9,13},{10,... | collective-permute-start | bytes 294920 | tf_op jit(solution)/shard_map/ppermute | solution.py:451
  125.9 8.1 %collective-permute-start.17 = (bf16[16,2560]{1,0:T(8,128)(2,1)S(1)}, bf16[16,2560]{1,0:T(8,128)(2,1)S(1)}, u32[]{:S(2)}, u32[]{:S(2)}) collective-permute-start(bf16[16,2560]{1,0:T(8,128)(2,1)S(1)} %constant_dynamic-slice_fusion.1), channel_id=1, source_target_pairs={{0,8},{1,9},{2,10},{3,11},{4,12},{5,13},{6,14},{7,15},{8,0},{9,1},... | collective-permute-start | bytes 245768 | tf_op jit(solution)/shard_map/ppermute | solution.py:451
  128.3 8.6 %collective-permute-start.16 = (bf16[64,512]{1,0:T(8,128)(2,1)S(1)}, bf16[64,512]{1,0:T(8,128)(2,1)S(1)}, u32[]{:S(2)}, u32[]{:S(2)}) collective-permute-start(bf16[64,512]{1,0:T(8,128)(2,1)S(1)} %get-tuple-element.159), channel_id=1, source_target_pairs={{0,8},{1,9},{2,10},{3,11},{4,12},{5,13},{6,14},{7,15},{8,0},{9,1},... | collective-permute-start | bytes 196616 | tf_op jit(solution)/shard_map/ppermute | solution.py:451
  130.3 7.5 %collective-permute-start.15 = (bf16[16,1536]{1,0:T(8,128)(2,1)S(1)}, bf16[16,1536]{1,0:T(8,128)(2,1)S(1)}, u32[]{:S(2)}, u32[]{:S(2)}) collective-permute-start(bf16[16,1536]{1,0:T(8,128)(2,1)S(1)} %constant_dynamic-slice_fusion), channel_id=1, source_target_pairs={{0,8},{1,9},{2,10},{3,11},{4,12},{5,13},{6,14},{7,15},{8,0},{9,1},... | collective-permute-start | bytes 147464 | tf_op jit(solution)/shard_map/ppermute | solution.py:451
  134.6 7.5 %collective-permute-start.20 = (bf16[16,2560]{1,0:T(8,128)(2,1)S(1)}, bf16[16,2560]{1,0:T(8,128)(2,1)S(1)}, u32[]{:S(2)}, u32[]{:S(2)}) collective-permute-start(bf16[16,2560]{1,0:T(8,128)(2,1)S(1)} %get-tuple-element.163), channel_id=1, source_target_pairs={{0,8},{1,9},{2,10},{3,11},{4,12},{5,13},{6,14},{7,15},{8,0},{9,1},... | collective-permute-start | bytes 245768 | tf_op jit(solution)/shard_map/ppermute | solution.py:451
  136.9 9.0 %collective-permute-start.19 = (bf16[128,512]{1,0:T(8,128)(2,1)S(1)}, bf16[128,512]{1,0:T(8,128)(2,1)S(1)}, u32[]{:S(2)}, u32[]{:S(2)}) collective-permute-start(bf16[128,512]{1,0:T(8,128)(2,1)S(1)} %pad_maximum_fusion.5), channel_id=1, source_target_pairs={{0,2},{1,3},{2,0},{3,1},{4,6},{5,7},{6,4},{7,5},{8,10},{9,11},{10,... | collective-permute-start | bytes 393224 | tf_op jit(solution)/shard_map/ppermute | solution.py:451
  138.5 7.5 %collective-permute-start.18 = (bf16[24,1536]{1,0:T(8,128)(2,1)S(1)}, bf16[24,1536]{1,0:T(8,128)(2,1)S(1)}, u32[]{:S(2)}, u32[]{:S(2)}) collective-permute-start(bf16[24,1536]{1,0:T(8,128)(2,1)S(1)} %pad_maximum_fusion.6), channel_id=1, source_target_pairs={{0,8},{1,9},{2,10},{3,11},{4,12},{5,13},{6,14},{7,15},{8,0},{9,1},... | collective-permute-start | bytes 221192 | tf_op jit(solution)/shard_map/ppermute | solution.py:451
  142.1 7.8 %collective-permute-start.23 = (bf16[32,2560]{1,0:T(8,128)(2,1)S(1)}, bf16[32,2560]{1,0:T(8,128)(2,1)S(1)}, u32[]{:S(2)}, u32[]{:S(2)}) collective-permute-start(bf16[32,2560]{1,0:T(8,128)(2,1)S(1)} %pad_maximum_fusion.4), channel_id=1, source_target_pairs={{0,4},{1,5},{2,6},{3,7},{4,0},{5,1},{6,2},{7,3},{8,12},{9,13},{10,... | collective-permute-start | bytes 491528 | tf_op jit(solution)/shard_map/ppermute | solution.py:451
  145.9 9.2 %collective-permute-start.22 = (bf16[256,512]{1,0:T(8,128)(2,1)S(1)}, bf16[256,512]{1,0:T(8,128)(2,1)S(1)}, u32[]{:S(2)}, u32[]{:S(2)}) collective-permute-start(bf16[256,512]{1,0:T(8,128)(2,1)S(1)} %pad_maximum_fusion.3), channel_id=1, source_target_pairs={{0,1},{1,0},{2,3},{3,2},{4,5},{5,4},{6,7},{7,6},{8,9},{9,8},{10,11... | collective-permute-start | bytes 786440 | tf_op jit(solution)/shard_map/ppermute | solution.py:451
  146.7 8.5 %collective-permute-start.21 = (bf16[40,1536]{1,0:T(8,128)(2,1)S(1)}, bf16[40,1536]{1,0:T(8,128)(2,1)S(1)}, u32[]{:S(2)}, u32[]{:S(2)}) collective-permute-start(bf16[40,1536]{1,0:T(8,128)(2,1)S(1)} %concatenate.98), channel_id=1, source_target_pairs={{0,4},{1,5},{2,6},{3,7},{4,0},{5,1},{6,2},{7,3},{8,12},{9,13},{10,... | collective-permute-start | bytes 368648 | tf_op jit(solution)/shard_map/ppermute | solution.py:451
  149.9 7.3 %collective-permute-start.26 = (bf16[64,2560]{1,0:T(8,128)(2,1)S(1)}, bf16[64,2560]{1,0:T(8,128)(2,1)S(1)}, u32[]{:S(2)}, u32[]{:S(2)}) collective-permute-start(bf16[64,2560]{1,0:T(8,128)(2,1)S(1)} %pad_maximum_fusion.2), channel_id=1, source_target_pairs={{0,2},{1,3},{2,0},{3,1},{4,6},{5,7},{6,4},{7,5},{8,10},{9,11},{10,... | collective-permute-start | bytes 983048 | tf_op jit(solution)/shard_map/ppermute | solution.py:451
  155.2 9.4 %collective-permute-start.25 = (bf16[512,512]{1,0:T(8,128)(2,1)S(1)}, bf16[512,512]{1,0:T(8,128)(2,1)}, u32[]{:S(2)}, u32[]{:S(2)}) collective-permute-start(bf16[512,512]{1,0:T(8,128)(2,1)S(1)} %pad_maximum_fusion.1), channel_id=1, source_target_pairs={{0,4},{1,5},{2,6},{3,7},{4,0},{5,1},{6,2},{7,3},{8,12},{9,13},{10,... | collective-permute-start | bytes 1572872 | tf_op jit(solution)/shard_map/ppermute | solution.py:451
  156.0 10.4 %collective-permute-start.24 = (bf16[72,1536]{1,0:T(8,128)(2,1)S(1)}, bf16[72,1536]{1,0:T(8,128)(2,1)S(1)}, u32[]{:S(2)}, u32[]{:S(2)}) collective-permute-start(bf16[72,1536]{1,0:T(8,128)(2,1)S(1)} %concatenate.101), channel_id=1, source_target_pairs={{0,2},{1,3},{2,0},{3,1},{4,6},{5,7},{6,4},{7,5},{8,10},{9,11},{10,... | collective-permute-start | bytes 663560 | tf_op jit(solution)/shard_map/ppermute | solution.py:451
  158.0 10.6 %collective-permute-start.28 = (bf16[128,2560]{1,0:T(8,128)(2,1)S(1)}, bf16[128,2560]{1,0:T(8,128)(2,1)S(1)}, u32[]{:S(2)}, u32[]{:S(2)}) collective-permute-start(bf16[128,2560]{1,0:T(8,128)(2,1)S(1)} %pad_maximum_fusion), channel_id=1, source_target_pairs={{0,1},{1,0},{2,3},{3,2},{4,5},{5,4},{6,7},{7,6},{8,9},{9,8},{10,11... | collective-permute-start | bytes 1966088 | tf_op jit(solution)/shard_map/ppermute | solution.py:451
  166.4 3.1 %collective-permute-start.29 = (bf16[1024,512]{1,0:T(8,128)(2,1)}, bf16[1024,512]{1,0:T(8,128)(2,1)}, u32[]{:S(2)}, u32[]{:S(2)}) collective-permute-start(bf16[1024,512]{1,0:T(8,128)(2,1)} %constant_dynamic-update-slice_fusion.3.own_ref), channel_id=1, source_target_pairs={{0,16},{16,0},{1,17},{17,1},{2,18},{18,2},{3,19},{19,3},{4,20},{20... | collective-permute-start | bytes 3145736 | tf_op jit(solution)/shard_map/ppermute | solution.py:448
  167.3 8.1 %collective-permute-start.27 = (bf16[136,1536]{1,0:T(8,128)(2,1)S(1)}, bf16[136,1536]{1,0:T(8,128)(2,1)S(1)}, u32[]{:S(2)}, u32[]{:S(2)}) collective-permute-start(bf16[136,1536]{1,0:T(8,128)(2,1)S(1)} %concatenate.104), channel_id=1, source_target_pairs={{0,1},{1,0},{2,3},{3,2},{4,5},{5,4},{6,7},{7,6},{8,9},{9,8},{10,11... | collective-permute-start | bytes 1253384 | tf_op jit(solution)/shard_map/ppermute | solution.py:451
  169.5 6.4 %collective-permute-start.31 = (bf16[256,2560]{1,0:T(8,128)(2,1)}, bf16[256,2560]{1,0:T(8,128)(2,1)}, u32[]{:S(2)}, u32[]{:S(2)}) collective-permute-start(bf16[256,2560]{1,0:T(8,128)(2,1)} %constant_dynamic-update-slice_fusion.8.own_ref), channel_id=1, source_target_pairs={{0,16},{16,0},{1,17},{17,1},{2,18},{18,2},{3,19},{19,3},{4,20},{20... | collective-permute-start | bytes 3932168 | tf_op jit(solution)/shard_map/ppermute | solution.py:448
  175.8 4.6 %collective-permute-start.30 = (bf16[264,1536]{1,0:T(8,128)(2,1)S(1)}, bf16[264,1536]{1,0:T(8,128)(2,1)S(1)}, u32[]{:S(2)}, u32[]{:S(2)}) collective-permute-start(bf16[264,1536]{1,0:T(8,128)(2,1)S(1)} %concatenate.107), channel_id=1, source_target_pairs={{0,16},{16,0},{1,17},{17,1},{2,18},{18,2},{3,19},{19,3},{4,20},{20... | collective-permute-start | bytes 2433032 | tf_op jit(solution)/shard_map/ppermute | solution.py:448
  (9 other events, 78.0 us)

commit v4 on v3

--- a/solution.py
+++ b/solution.py
@@ -155,11 +155,11 @@
         carry_pair[...] = dot(pick_carry[...], pair[part]).astype(BF)
 
 
-def halo_kernel(halo, gain, key_w, value_w, pick_late, key_rows_in, window_in, key_rows, window):
-    raw = halo[...].astype(F32)
-    unit, _ = row_stats(raw)
-    is_frame = lax.broadcasted_iota(jnp.int32, raw.shape, 0) < CARRY_FRAMES
-    carried = jnp.where(is_frame, unit * gain[...], raw).astype(BF)
+def halo_kernel(halo, gain, key_w, value_w, pick_carry, pick_late, key_rows_in, window_in, key_rows, window):
+    slabs = halo[...].astype(F32)
+    unit, _ = row_stats(slabs[:FRAMES].reshape(PART_FRAMES, slabs.shape[2]))
+    rows = jnp.concatenate([unit * gain[...], slabs[FRAMES], jnp.zeros_like(slabs[FRAMES])], axis=0).astype(BF)
+    carried = dot(pick_carry[...], rows).astype(BF)
     key_rows[:PART_ROWS] = key_rows_in[:PART_ROWS]
     key_rows[PART_ROWS:] = carried
     pair = jnp.concatenate([dot(carried, key_w[...]), dot(carried, value_w[...])], axis=1).astype(BF)
@@ -241,8 +241,9 @@
     result[...] = by_frame([final[p * PART_FRAMES : (p + 1) * PART_FRAMES] for p in range(PARTS)]).astype(BF)
     pulled = jnp.concatenate(by_part(out_grad[...].astype(F32)), axis=0)
     grad_combined, gain_part = norm_back(unit, scale, output_gain[...], pulled)
-    grad_combined_out[...] = grad_combined
-    grad_ff_rows[span] = grad_combined.astype(BF)
+    grad_ff = grad_combined.astype(BF)
+    grad_combined_out[...] = grad_ff
+    grad_ff_rows[span] = grad_ff
 
     @pl.when(step == 0)
     def _():
@@ -272,16 +273,15 @@
     span = pl.ds(pl.multiple_of(step * ROWS, ROWS), ROWS)
     unit, scale = row_stats(residual[...])
     middle_rows[span] = (unit * middle_gain[...]).astype(BF)
-    grad_combined_rows = grad_combined[...]
-    grad_ff = grad_combined_rows.astype(BF)
+    grad_ff = grad_combined[...]
     for c in range(ff // width):
         columns = slice(c * width, (c + 1) * width)
         part = (dot_back(grad_ff, down_w[columns]) * slope[:, columns].astype(F32)).astype(BF)
         lifted[span, columns] = part
     grad_middle = dot_back(lifted[span], up_w[...])
     grad_norm, gain_part = norm_back(unit, scale, middle_gain[...], grad_middle)
-    grad_residual = grad_combined_rows + grad_norm
-    grad_residual_out[...] = grad_residual
+    grad_residual = grad_ff.astype(F32) + grad_norm
+    grad_residual_out[...] = grad_residual.astype(BF)
     memory_rows = memory_grad[...].astype(F32)
     blank = jnp.zeros((PART, width), F32)
     grad_branch = []
@@ -309,9 +309,15 @@
             out[:, ff:] = out_sum[rows].astype(BF)
 
 
+def store_first(out, values, step):
+    @pl.when(step == 0)
+    def _():
+        out[...] = values
+
+
 def attention_back_kernel(
     core, pick_query, unpick_query, unpick_key, query_rows, key_rows, query, window, soft, grad_attended,
-    grad_query_rows, grad_pair, grad_carry, projections_keep, projections_send,
+    grad_query_rows, grad_pair, grad_carry, first_carry, projections_keep, projections_send,
     turned, grad_window, both_rows, query_sum, pair_sum,
 ):
     step = pl.program_id(0)
@@ -350,6 +356,8 @@
         both = dot(unpick_key[...], grad_window[...]).astype(BF)
         grad_pair[part] = both[:PART_ROWS]
         grad_carry[p * CARRY : (p + 1) * CARRY] = both[PART_ROWS:]
+        if p == 0:
+            store_first(first_carry, both[PART_ROWS:], step)
         both_rows[p * (PART_ROWS + CARRY) : (p + 1) * (PART_ROWS + CARRY)] = both
     query_sum[...] += dot_outer(query_rows[...], grad_query_rows[...])
     pair_sum[...] += dot_outer(key_rows[...], both_rows[...])
@@ -392,7 +400,7 @@
         unit, scale = row_stats(part)
         grad_norm, more = norm_back(unit, scale, gain[...], own + share)
         gain_part = gain_part + more
-        results.append(grad_residual[p * PART_FRAMES : (p + 1) * PART_FRAMES] + grad_norm)
+        results.append(grad_residual[p * PART_FRAMES : (p + 1) * PART_FRAMES].astype(F32) + grad_norm)
     grad_frames[...] = by_frame(results)
     grad_memory[...] = jnp.concatenate(memory_rows, axis=0).astype(BF)
 
@@ -615,14 +623,7 @@
     pulls = jnp.transpose(out_grad, (1, 0, 2))
     segment = lax.axis_index("seg") * slots + jnp.arange(slots, dtype=jnp.int32)
     position = segment_position(counts[0], segment)
-    halo = jnp.concatenate(
-        [
-            frames[:, slots - 2 :].reshape(CARRY_FRAMES, width),
-            memory[slots - MEMS :],
-            jnp.zeros((CARRY - CARRY_FRAMES - MEMS, width), BF),
-        ],
-        axis=0,
-    )
+    halo = jnp.concatenate([frames[:, slots - PART :], memory[None, slots - PART :]], axis=0)
     halo = shift(halo, "seg", 1)
     slab = (FRAMES, BLOCK, width)
     smem = pl.BlockSpec(memory_space=pltpu.SMEM)
@@ -651,13 +652,14 @@
         halo_kernel,
         1,
         [
-            (halo, None), (input_gain, None), (key_weight, None), (value_weight, None), (pick_late, None),
+            (halo, pl.BlockSpec(halo.shape, lambda i: (0, 0, 0))), (input_gain, None), (key_weight, None), (value_weight, None),
+            (pick_carry, None), (pick_late, None),
             (key_rows, key_block), (window, window_block),
         ],
         [(BF, key_rows.shape, key_block), (BF, window.shape, window_block)],
         [],
         2,
-        {5: 0, 6: 1},
+        {6: 0, 7: 1},
     )
 
     attended, soft, residual, slope, grad_combined, result, memory_out, keep, send, output_part = call(
@@ -673,7 +675,7 @@
             (BF, (tiles * PAIRS * TILE, 2 * TILE), (TILES * PAIRS, 2 * TILE)),
             (F32, (total, width), (ROWS, width)),
             (BF, (total, ff), (ROWS, ff)),
-            (F32, (total, width), (ROWS, width)),
+            (BF, (total, width), (ROWS, width)),
             (BF, (FRAMES, slots, width), slab),
             (BF, (slots, width), (BLOCK, width)),
             (BF, (ff // 2, width), None),
@@ -695,7 +697,7 @@
             (memory_grad, (BLOCK, width)), (middle_gain, None), (out_weight, None), (up_weight, None), (down_weight, None),
         ],
         [
-            (F32, (total, width), (ROWS, width)),
+            (BF, (total, width), (ROWS, width)),
             (BF, (parts * PART_ROWS, width), (FULL, width)),
             (BF, (width // 2, ff + width), None),
             (BF, (width // 2, ff + width), None),
@@ -711,7 +713,7 @@
     up.start()
     down.start()
 
-    grad_query_rows, grad_pair, grad_carry, keep, send = call(
+    grad_query_rows, grad_pair, grad_carry, first_carry, keep, send = call(
         attention_back_kernel,
         steps,
         [
@@ -724,6 +726,7 @@
             (BF, (parts * PART_ROWS, width), (FULL, width)),
             (BF, (parts * PART_ROWS, 2 * width), (FULL, 2 * width)),
             (BF, (parts * CARRY, 2 * width), (PARTS * CARRY, 2 * width)),
+            (BF, (CARRY, 2 * width), None),
             (BF, (width // 2, 3 * width), None),
             (BF, (width // 2, 3 * width), None),
         ],
@@ -734,16 +737,18 @@
         12,
     )
 
+    projections = Sum(keep, send, 0)
+    sent = projections.start()
+    carry_next = shift(first_carry, "seg", -1)
     down.land()
     up.land()
-    down.values, up.values, keep, send, grad_carry = lax.optimization_barrier(
-        (down.values, up.values, keep, send, grad_carry)
-    )
-    projections = Sum(keep, send, 0)
-    sent = projections.start()
-    carry_next = shift(grad_carry[:CARRY], "seg", -1)
+    down.values, up.values, grad_pair = lax.optimization_barrier((down.values, up.values, grad_pair))
     sent = up.start(sent)
     sent = down.start(sent)
+    projections.land(sent)
+    sent = projections.start(sent)
+    grad_pair, _ = lax.optimization_barrier((grad_pair, sent))
+
     grad_frames, grad_memory, input_part = call(
         projection_back_kernel,
         steps,
@@ -764,8 +769,6 @@
     grad_frames = jnp.transpose(grad_frames, (1, 0, 2))
 
     gains = jnp.concatenate([input_part, middle_part, output_part], axis=1)
-    projections.land(sent)
-    sent = projections.start(sent)
     up.land(sent, gains)
     projections.row = None
     order = (up, down, projections)

time: 187 us -> 181 us (0.968)
  waiting for transfers between devices: 30.4 us -> 22.8 us
  starting transfers between devices: 29.3 us -> 31.7 us
    ppermute x24, waiting for transfers between devices: 30.4 us -> 22.7 us  [swap(): return lax.ppermute(values, ('grp', 'seg'), pairs)]
  transfers between devices with their start and end apart: 32 -> 32, of which waited for: 15 -> 14; matrix products, arithmetic and copies ran while one was open for 11% -> 12% of each run, Pallas kernels for 34% -> 35%
where the time goes in v4:
time: 181 us
  Pallas kernels  98.7 us (55%)
  starting transfers between devices  31.7 us (18%)
  waiting for transfers between devices  22.8 us (13%)
  local copies, waits for them, and re-layouts  17.3 us (10%)
  other arithmetic  9.09 us (5%)
    pallas_call x6, Pallas kernels, call(): pl.pallas_call(kernel, grid=(steps,), in_specs=[spec(array.shape, block)...  86.5 us
    ppermute x24, starting transfers between devices, swap(): return lax.ppermute(values, ('grp', 'seg'), pairs)  23.2 us
    ppermute x24, waiting for transfers between devices, swap(): return lax.ppermute(values, ('grp', 'seg'), pairs)  22.7 us
    pallas_call x3, Pallas kernels, finish(): pl.pallas_call(kernel, grid=(2 * halves,), in_specs=[pl.BlockSpec(memory_...  12.3 us
    ppermute x2, starting transfers between devices, shift(): lax.ppermute(values, axis, [(i, (i + by) % size) for i in range(size)])  7.41 us
    unnamed x26, local copies, waits for them, and re-layouts  6.11 us
    convert_element_type x12, other arithmetic, land(): (self.values.astype(F32) + other.astype(F32)).astype(self.values.dtype)  4.82 us
  transfers between devices with their start and end apart: 32, of which 14 were waited for; matrix products, arithmetic and copies ran while one was open for 12% of the time, Pallas kernels for 35%

profile of v4, /device:TPU:0, one launch (start us, length us, event | category | flops | bytes accessed | tf_op | source)
XLA Modules:
  0.0 180.7 jit_solution(18084184746156741370)
XLA Ops:
  2.3 3.0 %collective-permute-start = (bf16[21,8,512]{2,1,0:T(8,128)(2,1)S(1)}, bf16[21,8,512]{2,1,0:T(8,128)(2,1)S(1)}, u32[]{:S(2)}, u32[]{:S(2)}) collective-permute-start(bf16[21,8,512]{2,1,0:T(8,128)(2,1)S(1)} %pad_maximum_fusion.4), channel_id=1, source_target_pairs={{0,1},{1,2},{2,3},{3,4},{4,5},{5,6},{6,7},{7,8},{8,9},{9,10},{10,1... | collective-permute-start | bytes 516104 | tf_op jit(solution)/shard_map/ppermute | solution.py:429
  6.9 9.3 %project_kernel.1 = (bf16[1408,512]{1,0:T(8,128)(2,1)}, bf16[1792,512]{1,0:T(8,128)(2,1)}, bf16[2048,512]{1,0:T(8,128)(2,1)}, bf16[2048,1024]{1,0:T(8,128)(2,1)}) custom-call(bf16[20,64,512]{2,1,0:T(8,128)(2,1)} %bitcast.16, bf16[64,512]{1,0:T(8,128)(2,1)} %memory.1, f32[1,512]{1,0:T(1,128)} %bitcast.26, bf16[512,512]{1,0:T(8,128)(2,1)} %query_w.3, ...), custom_call_target="tpu_custom_call" | custom-call | flops 10000000000 | bytes 1000000 | tf_op jit(solution)/shard_map/project_kernel/pallas_call | solution.py:591
  17.4 3.1 %halo_kernel.1 = (bf16[1792,512]{1,0:T(8,128)(2,1)}, bf16[2048,1024]{1,0:T(8,128)(2,1)}) custom-call(bf16[21,8,512]{2,1,0:T(8,128)(2,1)} %copy-done.7, f32[1,512]{1,0:T(1,128)} %bitcast.27, bf16[512,512]{1,0:T(8,128)(2,1)} %key_w.5, bf16[512,512]{1,0:T(8,128)(2,1)} %value_w.5, ...), custom_call_target="tpu_custom_call", output_to_operand_aliasing={{0}: (6, {}), {1}: (7, {})} | custom-call | flops 2000000000 | bytes 200000 | tf_op jit(solution)/shard_map/halo_kernel/pallas_call | solution.py:591
  20.5 28.3 %forward_kernel.1 = (bf16[1408,512]{1,0:T(8,128)(2,1)}, bf16[8192,256]{1,0:T(8,128)(2,1)}, f32[1280,512]{1,0:T(8,128)}, bf16[1280,2048]{1,0:T(8,128)(2,1)}, bf16...) custom-call(s32[2]{0:T(128)} %pad_add_fusion.core.device_ref, ...), custom_call_target="tpu_custom_call" | custom-call | flops 24000000000 | bytes 2400000 | tf_op jit(solution)/shard_map/forward_kernel/pallas_call | solution.py:591
  48.9 17.9 %backward_kernel.1 = (bf16[1280,512]{1,0:T(8,128)(2,1)}, bf16[1408,512]{1,0:T(8,128)(2,1)}, bf16[256,2560]{1,0:T(8,128)(2,1)}, bf16[256,2560]{1,0:T(8,128)(2,1)}, f32[1,512]{1,0:T(1,128)}) custom-call(s32[2]{0:T(128)} %pad_add_fusion.core.device_ref, bf16[1280,2048]{1,0:T(8,128)(2,1)} %get-tuple-element.115.slope, ...), custom_call_target="tpu_custom_call" | custom-call | flops 16000000000 | bytes 1600000 | tf_op jit(solution)/shard_map/backward_kernel/pallas_call | solution.py:591
  68.5 1.6 collective-permute-start.2
  70.0 19.1 %attention_back_kernel.1 = (bf16[1408,512]{1,0:T(8,128)(2,1)}, bf16[1408,1024]{1,0:T(8,128)(2,1)}, bf16[384,1024]{1,0:T(8,128)(2,1)}, bf16[48,1024]{1,0:T(8,128)...) custom-call(s32[2]{0:T(128)} %pad_add_fusion.core.device_ref, bf16[256,176]{1,0:T(8,128)(2,1)} %constant.195.clone.pick_query, ...), custom_call_target="tpu_custom_call" | custom-call | flops 12000000000 | bytes 1200000 | tf_op jit(solution)/shard_map/attention_back_kernel/pallas_call | solution.py:591
  89.2 4.4 %collective-permute-start.5 = (bf16[48,1024]{1,0:T(8,128)(2,1)}, bf16[48,1024]{1,0:T(8,128)(2,1)S(1)}, u32[]{:S(2)}, u32[]{:S(2)}) collective-permute-start(bf16[48,1024]{1,0:T(8,128)(2,1)} %get-tuple-element.139), channel_id=1, source_target_pairs={{0,15},{1,0},{2,1},{3,2},{4,3},{5,4},{6,5},{7,6},{8,7},{9,8},{10,9... | collective-permute-start | bytes 294920 | tf_op jit(solution)/shard_map/ppermute | solution.py:429
  93.7 1.6 add_convert_fusion
  97.4 2.1 %collective-permute-start.7 = (bf16[256,512]{1,0:T(8,128)(2,1)S(1)}, bf16[256,512]{1,0:T(8,128)(2,1)}, u32[]{:S(2)}, u32[]{:S(2)}) collective-permute-start(bf16[256,512]{1,0:T(8,128)(2,1)S(1)} %constant_dynamic-slice_fusion.10), channel_id=1, source_target_pairs={{0,1},{1,0},{2,3},{3,2},{4,5},{5,4},{6,7},{7,6},{8,9},{9,8},{10,11... | collective-permute-start | bytes 786440 | tf_op jit(solution)/shard_map/ppermute | solution.py:459
  101.2 8.7 %projection_back_kernel.1 = (f32[20,64,512]{2,1,0:T(8,128)}, bf16[64,512]{1,0:T(8,128)(2,1)}, f32[1,512]{1,0:T(1,128)}) custom-call(bf16[176,48]{1,0:T(8,128)(2,1)} %constant.193.clone.unpick_carry, bf16[1408,1024]{1,0:T(8,128)(2,1)} %get-tuple-element.137.grad_pair, bf16[384,1024]{1,0:T(8,128)(2,1)} %get-tuple-element.138.grad_carry, ...), custom_call_target="tpu_custom_call" | custom-call | flops 8000000000 | bytes 800000 | tf_op jit(solution)/shard_map/projection_back_kernel/pallas_call | solution.py:591
  112.1 1.9 %collective-permute-start.10 = (bf16[128,512]{1,0:T(8,128)(2,1)S(1)}, bf16[128,512]{1,0:T(8,128)(2,1)S(1)}, u32[]{:S(2)}, u32[]{:S(2)}) collective-permute-start(bf16[128,512]{1,0:T(8,128)(2,1)S(1)} %constant_dynamic-slice_fusion.6), channel_id=1, source_target_pairs={{0,2},{1,3},{2,0},{3,1},{4,6},{5,7},{6,4},{7,5},{8,10},{9,11},{10,... | collective-permute-start | bytes 393224 | tf_op jit(solution)/shard_map/ppermute | solution.py:459
  115.4 2.6 %collective-permute-done.11 = bf16[64,2560]{1,0:T(8,128)(2,1)S(1)} collective-permute-done((bf16[64,2560]{1,0:T(8,128)(2,1)S(1)}, bf16[64,2560]{1,0:T(8,128)(2,1)S(1)}, u32[]{:S(2)}, u32[]{:S(2)}) %collective-permute-start.11) | collective-permute-done | bytes 327712 | tf_op jit(solution)/shard_map/ppermute | solution.py:459
  118.2 1.2 collective-permute-done.10
  119.7 1.8 collective-permute-done.9
  121.7 2.9 %collective-permute-done.14 = bf16[32,2560]{1,0:T(8,128)(2,1)S(1)} collective-permute-done((bf16[32,2560]{1,0:T(8,128)(2,1)S(1)}, bf16[32,2560]{1,0:T(8,128)(2,1)S(1)}, u32[]{:S(2)}, u32[]{:S(2)}) %collective-permute-start.14) | collective-permute-done | bytes 163872 | tf_op jit(solution)/shard_map/ppermute | solution.py:459
  124.7 2.1 %collective-permute-done.13 = bf16[64,512]{1,0:T(8,128)(2,1)S(1)} collective-permute-done((bf16[64,512]{1,0:T(8,128)(2,1)S(1)}, bf16[64,512]{1,0:T(8,128)(2,1)S(1)}, u32[]{:S(2)}, u32[]{:S(2)}) %collective-permute-start.13) | collective-permute-done | bytes 65568 | tf_op jit(solution)/shard_map/ppermute | solution.py:459
  128.3 2.1 %collective-permute-start.15 = (bf16[16,1536]{1,0:T(8,128)(2,1)S(1)}, bf16[16,1536]{1,0:T(8,128)(2,1)S(1)}, u32[]{:S(2)}, u32[]{:S(2)}) collective-permute-start(bf16[16,1536]{1,0:T(8,128)(2,1)S(1)} %constant_dynamic-slice_fusion), channel_id=1, source_target_pairs={{0,8},{1,9},{2,10},{3,11},{4,12},{5,13},{6,14},{7,15},{8,0},{9,1},... | collective-permute-start | bytes 147464 | tf_op jit(solution)/shard_map/ppermute | solution.py:459
  130.4 2.6 %collective-permute-done.17 = bf16[16,2560]{1,0:T(8,128)(2,1)S(1)} collective-permute-done((bf16[16,2560]{1,0:T(8,128)(2,1)S(1)}, bf16[16,2560]{1,0:T(8,128)(2,1)S(1)}, u32[]{:S(2)}, u32[]{:S(2)}) %collective-permute-start.17) | collective-permute-done | bytes 81952 | tf_op jit(solution)/shard_map/ppermute | solution.py:459
  134.5 1.4 collective-permute-start.19
  136.5 2.2 %collective-permute-start.18 = (bf16[24,1536]{1,0:T(8,128)(2,1)S(1)}, bf16[24,1536]{1,0:T(8,128)(2,1)S(1)}, u32[]{:S(2)}, u32[]{:S(2)}) collective-permute-start(bf16[24,1536]{1,0:T(8,128)(2,1)S(1)} %pad_maximum_fusion.7), channel_id=1, source_target_pairs={{0,8},{1,9},{2,10},{3,11},{4,12},{5,13},{6,14},{7,15},{8,0},{9,1},... | collective-permute-start | bytes 221192 | tf_op jit(solution)/shard_map/ppermute | solution.py:459
  139.4 1.2 collective-permute-done.20
  141.4 1.5 collective-permute-start.22
  143.6 1.6 collective-permute-start.21
  146.2 1.3 collective-permute-start.26
  148.2 3.1 %collective-permute-start.25 = (bf16[512,512]{1,0:T(8,128)(2,1)S(1)}, bf16[512,512]{1,0:T(8,128)(2,1)}, u32[]{:S(2)}, u32[]{:S(2)}) collective-permute-start(bf16[512,512]{1,0:T(8,128)(2,1)S(1)} %pad_maximum_fusion.1), channel_id=1, source_target_pairs={{0,4},{1,5},{2,6},{3,7},{4,0},{5,1},{6,2},{7,3},{8,12},{9,13},{10,... | collective-permute-start | bytes 1572872 | tf_op jit(solution)/shard_map/ppermute | solution.py:459
  155.4 3.6 %collective-permute-done.25 = bf16[512,512]{1,0:T(8,128)(2,1)} collective-permute-done((bf16[512,512]{1,0:T(8,128)(2,1)S(1)}, bf16[512,512]{1,0:T(8,128)(2,1)}, u32[]{:S(2)}, u32[]{:S(2)}) %collective-permute-start.25) | collective-permute-done | bytes 524320 | tf_op jit(solution)/shard_map/ppermute | solution.py:459
  159.0 1.9 %constant_dynamic-update-slice_fusion.3.own_ref = bf16[1024,512]{1,0:T(8,128)(2,1)} fusion(bf16[1024,512]{1,0:T(8,128)(2,1)} %constant_dynamic-update-slice_fusion.4, bf16[512,512]{1,0:T(8,128)(2,1)} %collective-permute-done.25), kind=kLoop, calls=%fused_computation.26 | loop fusion | bytes 1048576 | tf_op jit(solution)/shard_map/concatenate | solution.py:512
  162.8 2.4 %collective-permute-done.28 = bf16[128,2560]{1,0:T(8,128)(2,1)S(1)} collective-permute-done((bf16[128,2560]{1,0:T(8,128)(2,1)S(1)}, bf16[128,2560]{1,0:T(8,128)(2,1)S(1)}, u32[]{:S(2)}, u32[]{:S(2)}) %collective-permute-start.28) | collective-permute-done | bytes 655392 | tf_op jit(solution)/shard_map/ppermute | solution.py:459
  166.0 4.2 %finish.3 = f32[2048,512]{1,0:T(8,128)} custom-call(s32[2]{0:T(128)} %pad_add_fusion.core.device_ref, bf16[1024,512]{1,0:T(8,128)(2,1)} %constant_dynamic-update-slice_fusion.3.own_ref, bf16[1024,512]{1,0:T(8,128)(2,1)} %collective-permute-done.29.other_ref), custom_call_target="tpu_custom_call" | custom-call | flops 3000000000 | bytes 300000 | tf_op jit(solution)/shard_map/finish/pallas_call | solution.py:569
  171.1 4.5 %finish.4 = (f32[512,2048]{1,0:T(8,128)}, f32[512,512]{1,0:T(8,128)}) custom-call(s32[2]{0:T(128)} %pad_add_fusion.core.device_ref, bf16[256,2560]{1,0:T(8,128)(2,1)} %constant_dynamic-update-slice_fusion.8.own_ref, bf16[256,2560]{1,0:T(8,128)(2,1)} %collective-permute-done.31.other_ref), custom_call_target="tpu_custom_call" | custom-call | flops 3000000000 | bytes 300000 | tf_op jit(solution)/shard_map/finish/pallas_call | solution.py:569
  177.1 3.6 %finish.5 = (f32[512,512]{1,0:T(8,128)}, f32[512,512]{1,0:T(8,128)}, f32[512,512]{1,0:T(8,128)}) custom-call(s32[2]{0:T(128)} %pad_add_fusion.core.device_ref, bf16[256,1536]{1,0:T(8,128)(2,1)} %copy-done.4, bf16[256,1536]{1,0:T(8,128)(2,1)} %slice.77.other_ref), custom_call_target="tpu_custom_call" | custom-call | flops 3000000000 | bytes 300000 | tf_op jit(solution)/shard_map/finish/pallas_call | solution.py:569
  (133 shorter events, 30.8 us)
Async XLA Ops:
  2.3 14.4 %collective-permute-start = (bf16[21,8,512]{2,1,0:T(8,128)(2,1)S(1)}, bf16[21,8,512]{2,1,0:T(8,128)(2,1)S(1)}, u32[]{:S(2)}, u32[]{:S(2)}) collective-permute-start(bf16[21,8,512]{2,1,0:T(8,128)(2,1)S(1)} %pad_maximum_fusion.4), channel_id=1, source_target_pairs={{0,1},{1,2},{2,3},{3,4},{4,5},{5,6},{6,7},{7,8},{8,9},{9,10},{10,1... | collective-permute-start | bytes 516104 | tf_op jit(solution)/shard_map/ppermute | solution.py:429
  48.8 18.6 %collective-permute-start.1 = (bf16[1024,512]{1,0:T(8,128)(2,1)}, bf16[1024,512]{1,0:T(8,128)(2,1)S(1)}, u32[]{:S(2)}, u32[]{:S(2)}) collective-permute-start(bf16[1024,512]{1,0:T(8,128)(2,1)} %get-tuple-element.114), channel_id=1, source_target_pairs={{0,16},{16,0},{1,17},{17,1},{2,18},{18,2},{3,19},{19,3},{4,20},{20... | collective-permute-start | bytes 3145736 | tf_op jit(solution)/shard_map/ppermute | solution.py:456
  66.8 26.8 %collective-permute-start.3 = (bf16[256,2560]{1,0:T(8,128)(2,1)}, bf16[256,2560]{1,0:T(8,128)(2,1)}, u32[]{:S(2)}, u32[]{:S(2)}) collective-permute-start(bf16[256,2560]{1,0:T(8,128)(2,1)} %get-tuple-element.122), channel_id=1, source_target_pairs={{0,16},{16,0},{1,17},{17,1},{2,18},{18,2},{3,19},{19,3},{4,20},{20... | collective-permute-start | bytes 3932168 | tf_op jit(solution)/shard_map/ppermute | solution.py:456
  68.5 26.8 %collective-permute-start.2 = (bf16[512,512]{1,0:T(8,128)(2,1)}, bf16[512,512]{1,0:T(8,128)(2,1)}, u32[]{:S(2)}, u32[]{:S(2)}) collective-permute-start(bf16[512,512]{1,0:T(8,128)(2,1)} %constant_dynamic-slice_fusion.11), channel_id=1, source_target_pairs={{0,4},{1,5},{2,6},{3,7},{4,0},{5,1},{6,2},{7,3},{8,12},{9,13},{10,... | collective-permute-start | bytes 1572872 | tf_op jit(solution)/shard_map/ppermute | solution.py:459
  89.2 10.3 %collective-permute-start.4 = (bf16[256,1536]{1,0:T(8,128)(2,1)}, bf16[256,1536]{1,0:T(8,128)(2,1)S(1)}, u32[]{:S(2)}, u32[]{:S(2)}) collective-permute-start(bf16[256,1536]{1,0:T(8,128)(2,1)} %get-tuple-element.130), channel_id=1, source_target_pairs={{0,16},{16,0},{1,17},{17,1},{2,18},{18,2},{3,19},{19,3},{4,20},{20... | collective-permute-start | bytes 2359304 | tf_op jit(solution)/shard_map/ppermute | solution.py:456
  89.2 11.3 %collective-permute-start.5 = (bf16[48,1024]{1,0:T(8,128)(2,1)}, bf16[48,1024]{1,0:T(8,128)(2,1)S(1)}, u32[]{:S(2)}, u32[]{:S(2)}) collective-permute-start(bf16[48,1024]{1,0:T(8,128)(2,1)} %get-tuple-element.139), channel_id=1, source_target_pairs={{0,15},{1,0},{2,1},{3,2},{4,3},{5,4},{6,5},{7,6},{8,7},{9,8},{10,9... | collective-permute-start | bytes 294920 | tf_op jit(solution)/shard_map/ppermute | solution.py:429
  97.4 13.3 %collective-permute-start.8 = (bf16[128,2560]{1,0:T(8,128)(2,1)}, bf16[128,2560]{1,0:T(8,128)(2,1)S(1)}, u32[]{:S(2)}, u32[]{:S(2)}) collective-permute-start(bf16[128,2560]{1,0:T(8,128)(2,1)} %constant_dynamic-slice_fusion.9), channel_id=1, source_target_pairs={{0,1},{1,0},{2,3},{3,2},{4,5},{5,4},{6,7},{7,6},{8,9},{9,8},{10,11... | collective-permute-start | bytes 1966088 | tf_op jit(solution)/shard_map/ppermute | solution.py:459
  97.4 13.7 %collective-permute-start.7 = (bf16[256,512]{1,0:T(8,128)(2,1)S(1)}, bf16[256,512]{1,0:T(8,128)(2,1)}, u32[]{:S(2)}, u32[]{:S(2)}) collective-permute-start(bf16[256,512]{1,0:T(8,128)(2,1)S(1)} %constant_dynamic-slice_fusion.10), channel_id=1, source_target_pairs={{0,1},{1,0},{2,3},{3,2},{4,5},{5,4},{6,7},{7,6},{8,9},{9,8},{10,11... | collective-permute-start | bytes 786440 | tf_op jit(solution)/shard_map/ppermute | solution.py:459
  100.5 14.7 %collective-permute-start.6 = (bf16[128,1536]{1,0:T(8,128)(2,1)}, bf16[128,1536]{1,0:T(8,128)(2,1)S(1)}, u32[]{:S(2)}, u32[]{:S(2)}) collective-permute-start(bf16[128,1536]{1,0:T(8,128)(2,1)} %constant_dynamic-slice_fusion.8), channel_id=1, source_target_pairs={{0,1},{1,0},{2,3},{3,2},{4,5},{5,4},{6,7},{7,6},{8,9},{9,8},{10,11... | collective-permute-start | bytes 1179656 | tf_op jit(solution)/shard_map/ppermute | solution.py:459
  110.9 7.1 %collective-permute-start.11 = (bf16[64,2560]{1,0:T(8,128)(2,1)S(1)}, bf16[64,2560]{1,0:T(8,128)(2,1)S(1)}, u32[]{:S(2)}, u32[]{:S(2)}) collective-permute-start(bf16[64,2560]{1,0:T(8,128)(2,1)S(1)} %constant_dynamic-slice_fusion.7), channel_id=1, source_target_pairs={{0,2},{1,3},{2,0},{3,1},{4,6},{5,7},{6,4},{7,5},{8,10},{9,11},{10,... | collective-permute-start | bytes 983048 | tf_op jit(solution)/shard_map/ppermute | solution.py:459
  112.1 7.3 %collective-permute-start.10 = (bf16[128,512]{1,0:T(8,128)(2,1)S(1)}, bf16[128,512]{1,0:T(8,128)(2,1)S(1)}, u32[]{:S(2)}, u32[]{:S(2)}) collective-permute-start(bf16[128,512]{1,0:T(8,128)(2,1)S(1)} %constant_dynamic-slice_fusion.6), channel_id=1, source_target_pairs={{0,2},{1,3},{2,0},{3,1},{4,6},{5,7},{6,4},{7,5},{8,10},{9,11},{10,... | collective-permute-start | bytes 393224 | tf_op jit(solution)/shard_map/ppermute | solution.py:459
  115.3 6.2 %collective-permute-start.9 = (bf16[64,1536]{1,0:T(8,128)(2,1)S(1)}, bf16[64,1536]{1,0:T(8,128)(2,1)S(1)}, u32[]{:S(2)}, u32[]{:S(2)}) collective-permute-start(bf16[64,1536]{1,0:T(8,128)(2,1)S(1)} %constant_dynamic-slice_fusion.5), channel_id=1, source_target_pairs={{0,2},{1,3},{2,0},{3,1},{4,6},{5,7},{6,4},{7,5},{8,10},{9,11},{10,... | collective-permute-start | bytes 589832 | tf_op jit(solution)/shard_map/ppermute | solution.py:459
  118.1 6.4 %collective-permute-start.14 = (bf16[32,2560]{1,0:T(8,128)(2,1)S(1)}, bf16[32,2560]{1,0:T(8,128)(2,1)S(1)}, u32[]{:S(2)}, u32[]{:S(2)}) collective-permute-start(bf16[32,2560]{1,0:T(8,128)(2,1)S(1)} %constant_dynamic-slice_fusion.4), channel_id=1, source_target_pairs={{0,4},{1,5},{2,6},{3,7},{4,0},{5,1},{6,2},{7,3},{8,12},{9,13},{10,... | collective-permute-start | bytes 491528 | tf_op jit(solution)/shard_map/ppermute | solution.py:459
  119.5 7.3 %collective-permute-start.13 = (bf16[64,512]{1,0:T(8,128)(2,1)S(1)}, bf16[64,512]{1,0:T(8,128)(2,1)S(1)}, u32[]{:S(2)}, u32[]{:S(2)}) collective-permute-start(bf16[64,512]{1,0:T(8,128)(2,1)S(1)} %constant_dynamic-slice_fusion.3), channel_id=1, source_target_pairs={{0,8},{1,9},{2,10},{3,11},{4,12},{5,13},{6,14},{7,15},{8,0},{9,1},... | collective-permute-start | bytes 196616 | tf_op jit(solution)/shard_map/ppermute | solution.py:459
  121.6 6.7 %collective-permute-start.12 = (bf16[32,1536]{1,0:T(8,128)(2,1)S(1)}, bf16[32,1536]{1,0:T(8,128)(2,1)S(1)}, u32[]{:S(2)}, u32[]{:S(2)}) collective-permute-start(bf16[32,1536]{1,0:T(8,128)(2,1)S(1)} %constant_dynamic-slice_fusion.2), channel_id=1, source_target_pairs={{0,4},{1,5},{2,6},{3,7},{4,0},{5,1},{6,2},{7,3},{8,12},{9,13},{10,... | collective-permute-start | bytes 294920 | tf_op jit(solution)/shard_map/ppermute | solution.py:459
  124.6 8.5 %collective-permute-start.17 = (bf16[16,2560]{1,0:T(8,128)(2,1)S(1)}, bf16[16,2560]{1,0:T(8,128)(2,1)S(1)}, u32[]{:S(2)}, u32[]{:S(2)}) collective-permute-start(bf16[16,2560]{1,0:T(8,128)(2,1)S(1)} %constant_dynamic-slice_fusion.1), channel_id=1, source_target_pairs={{0,8},{1,9},{2,10},{3,11},{4,12},{5,13},{6,14},{7,15},{8,0},{9,1},... | collective-permute-start | bytes 245768 | tf_op jit(solution)/shard_map/ppermute | solution.py:459
  127.4 7.1 %collective-permute-start.16 = (bf16[64,512]{1,0:T(8,128)(2,1)S(1)}, bf16[64,512]{1,0:T(8,128)(2,1)S(1)}, u32[]{:S(2)}, u32[]{:S(2)}) collective-permute-start(bf16[64,512]{1,0:T(8,128)(2,1)S(1)} %get-tuple-element.159), channel_id=1, source_target_pairs={{0,8},{1,9},{2,10},{3,11},{4,12},{5,13},{6,14},{7,15},{8,0},{9,1},... | collective-permute-start | bytes 196616 | tf_op jit(solution)/shard_map/ppermute | solution.py:459
  128.3 7.5 %collective-permute-start.15 = (bf16[16,1536]{1,0:T(8,128)(2,1)S(1)}, bf16[16,1536]{1,0:T(8,128)(2,1)S(1)}, u32[]{:S(2)}, u32[]{:S(2)}) collective-permute-start(bf16[16,1536]{1,0:T(8,128)(2,1)S(1)} %constant_dynamic-slice_fusion), channel_id=1, source_target_pairs={{0,8},{1,9},{2,10},{3,11},{4,12},{5,13},{6,14},{7,15},{8,0},{9,1},... | collective-permute-start | bytes 147464 | tf_op jit(solution)/shard_map/ppermute | solution.py:459
  133.7 6.9 %collective-permute-start.20 = (bf16[16,2560]{1,0:T(8,128)(2,1)S(1)}, bf16[16,2560]{1,0:T(8,128)(2,1)S(1)}, u32[]{:S(2)}, u32[]{:S(2)}) collective-permute-start(bf16[16,2560]{1,0:T(8,128)(2,1)S(1)} %get-tuple-element.163), channel_id=1, source_target_pairs={{0,8},{1,9},{2,10},{3,11},{4,12},{5,13},{6,14},{7,15},{8,0},{9,1},... | collective-permute-start | bytes 245768 | tf_op jit(solution)/shard_map/ppermute | solution.py:459
  134.5 6.9 %collective-permute-start.19 = (bf16[128,512]{1,0:T(8,128)(2,1)S(1)}, bf16[128,512]{1,0:T(8,128)(2,1)S(1)}, u32[]{:S(2)}, u32[]{:S(2)}) collective-permute-start(bf16[128,512]{1,0:T(8,128)(2,1)S(1)} %pad_maximum_fusion.6), channel_id=1, source_target_pairs={{0,2},{1,3},{2,0},{3,1},{4,6},{5,7},{6,4},{7,5},{8,10},{9,11},{10,... | collective-permute-start | bytes 393224 | tf_op jit(solution)/shard_map/ppermute | solution.py:459
  136.5 6.4 %collective-permute-start.18 = (bf16[24,1536]{1,0:T(8,128)(2,1)S(1)}, bf16[24,1536]{1,0:T(8,128)(2,1)S(1)}, u32[]{:S(2)}, u32[]{:S(2)}) collective-permute-start(bf16[24,1536]{1,0:T(8,128)(2,1)S(1)} %pad_maximum_fusion.7), channel_id=1, source_target_pairs={{0,8},{1,9},{2,10},{3,11},{4,12},{5,13},{6,14},{7,15},{8,0},{9,1},... | collective-permute-start | bytes 221192 | tf_op jit(solution)/shard_map/ppermute | solution.py:459
  140.6 5.5 %collective-permute-start.23 = (bf16[32,2560]{1,0:T(8,128)(2,1)S(1)}, bf16[32,2560]{1,0:T(8,128)(2,1)S(1)}, u32[]{:S(2)}, u32[]{:S(2)}) collective-permute-start(bf16[32,2560]{1,0:T(8,128)(2,1)S(1)} %pad_maximum_fusion.5), channel_id=1, source_target_pairs={{0,4},{1,5},{2,6},{3,7},{4,0},{5,1},{6,2},{7,3},{8,12},{9,13},{10,... | collective-permute-start | bytes 491528 | tf_op jit(solution)/shard_map/ppermute | solution.py:459
  141.4 6.8 %collective-permute-start.22 = (bf16[256,512]{1,0:T(8,128)(2,1)S(1)}, bf16[256,512]{1,0:T(8,128)(2,1)S(1)}, u32[]{:S(2)}, u32[]{:S(2)}) collective-permute-start(bf16[256,512]{1,0:T(8,128)(2,1)S(1)} %pad_maximum_fusion.3), channel_id=1, source_target_pairs={{0,1},{1,0},{2,3},{3,2},{4,5},{5,4},{6,7},{7,6},{8,9},{9,8},{10,11... | collective-permute-start | bytes 786440 | tf_op jit(solution)/shard_map/ppermute | solution.py:459
  143.6 7.7 %collective-permute-start.21 = (bf16[40,1536]{1,0:T(8,128)(2,1)S(1)}, bf16[40,1536]{1,0:T(8,128)(2,1)S(1)}, u32[]{:S(2)}, u32[]{:S(2)}) collective-permute-start(bf16[40,1536]{1,0:T(8,128)(2,1)S(1)} %concatenate.98), channel_id=1, source_target_pairs={{0,4},{1,5},{2,6},{3,7},{4,0},{5,1},{6,2},{7,3},{8,12},{9,13},{10,... | collective-permute-start | bytes 368648 | tf_op jit(solution)/shard_map/ppermute | solution.py:459
  146.2 7.6 %collective-permute-start.26 = (bf16[64,2560]{1,0:T(8,128)(2,1)S(1)}, bf16[64,2560]{1,0:T(8,128)(2,1)S(1)}, u32[]{:S(2)}, u32[]{:S(2)}) collective-permute-start(bf16[64,2560]{1,0:T(8,128)(2,1)S(1)} %pad_maximum_fusion.2), channel_id=1, source_target_pairs={{0,2},{1,3},{2,0},{3,1},{4,6},{5,7},{6,4},{7,5},{8,10},{9,11},{10,... | collective-permute-start | bytes 983048 | tf_op jit(solution)/shard_map/ppermute | solution.py:459
  148.2 10.7 %collective-permute-start.25 = (bf16[512,512]{1,0:T(8,128)(2,1)S(1)}, bf16[512,512]{1,0:T(8,128)(2,1)}, u32[]{:S(2)}, u32[]{:S(2)}) collective-permute-start(bf16[512,512]{1,0:T(8,128)(2,1)S(1)} %pad_maximum_fusion.1), channel_id=1, source_target_pairs={{0,4},{1,5},{2,6},{3,7},{4,0},{5,1},{6,2},{7,3},{8,12},{9,13},{10,... | collective-permute-start | bytes 1572872 | tf_op jit(solution)/shard_map/ppermute | solution.py:459
  152.1 8.7 %collective-permute-start.24 = (bf16[72,1536]{1,0:T(8,128)(2,1)S(1)}, bf16[72,1536]{1,0:T(8,128)(2,1)S(1)}, u32[]{:S(2)}, u32[]{:S(2)}) collective-permute-start(bf16[72,1536]{1,0:T(8,128)(2,1)S(1)} %concatenate.101), channel_id=1, source_target_pairs={{0,2},{1,3},{2,0},{3,1},{4,6},{5,7},{6,4},{7,5},{8,10},{9,11},{10,... | collective-permute-start | bytes 663560 | tf_op jit(solution)/shard_map/ppermute | solution.py:459
  154.6 10.6 %collective-permute-start.28 = (bf16[128,2560]{1,0:T(8,128)(2,1)S(1)}, bf16[128,2560]{1,0:T(8,128)(2,1)S(1)}, u32[]{:S(2)}, u32[]{:S(2)}) collective-permute-start(bf16[128,2560]{1,0:T(8,128)(2,1)S(1)} %pad_maximum_fusion), channel_id=1, source_target_pairs={{0,1},{1,0},{2,3},{3,2},{4,5},{5,4},{6,7},{7,6},{8,9},{9,8},{10,11... | collective-permute-start | bytes 1966088 | tf_op jit(solution)/shard_map/ppermute | solution.py:459
  160.8 5.2 %collective-permute-start.29 = (bf16[1024,512]{1,0:T(8,128)(2,1)}, bf16[1024,512]{1,0:T(8,128)(2,1)}, u32[]{:S(2)}, u32[]{:S(2)}) collective-permute-start(bf16[1024,512]{1,0:T(8,128)(2,1)} %constant_dynamic-update-slice_fusion.3.own_ref), channel_id=1, source_target_pairs={{0,16},{16,0},{1,17},{17,1},{2,18},{18,2},{3,19},{19,3},{4,20},{20... | collective-permute-start | bytes 3145736 | tf_op jit(solution)/shard_map/ppermute | solution.py:456
  161.7 8.5 %collective-permute-start.27 = (bf16[136,1536]{1,0:T(8,128)(2,1)S(1)}, bf16[136,1536]{1,0:T(8,128)(2,1)S(1)}, u32[]{:S(2)}, u32[]{:S(2)}) collective-permute-start(bf16[136,1536]{1,0:T(8,128)(2,1)S(1)} %concatenate.104), channel_id=1, source_target_pairs={{0,1},{1,0},{2,3},{3,2},{4,5},{5,4},{6,7},{7,6},{8,9},{9,8},{10,11... | collective-permute-start | bytes 1253384 | tf_op jit(solution)/shard_map/ppermute | solution.py:459
  166.0 5.0 %collective-permute-start.31 = (bf16[256,2560]{1,0:T(8,128)(2,1)}, bf16[256,2560]{1,0:T(8,128)(2,1)}, u32[]{:S(2)}, u32[]{:S(2)}) collective-permute-start(bf16[256,2560]{1,0:T(8,128)(2,1)} %constant_dynamic-update-slice_fusion.8.own_ref), channel_id=1, source_target_pairs={{0,16},{16,0},{1,17},{17,1},{2,18},{18,2},{3,19},{19,3},{4,20},{20... | collective-permute-start | bytes 3932168 | tf_op jit(solution)/shard_map/ppermute | solution.py:456
  170.6 5.0 %collective-permute-start.30 = (bf16[264,1536]{1,0:T(8,128)(2,1)S(1)}, bf16[264,1536]{1,0:T(8,128)(2,1)S(1)}, u32[]{:S(2)}, u32[]{:S(2)}) collective-permute-start(bf16[264,1536]{1,0:T(8,128)(2,1)S(1)} %concatenate.107), channel_id=1, source_target_pairs={{0,16},{16,0},{1,17},{17,1},{2,18},{18,2},{3,19},{19,3},{4,20},{20... | collective-permute-start | bytes 2433032 | tf_op jit(solution)/shard_map/ppermute | solution.py:456
  (9 other events, 74.8 us)

commit v5 on v4

--- a/solution.py
+++ b/solution.py
@@ -225,7 +225,7 @@
         memory_rows.append(branch[at + PART_FRAMES : at + PART_FRAMES + PART])
     memory_out[...] = jnp.concatenate(memory_rows, axis=0).astype(BF)
     residual = jnp.concatenate(residual, axis=0)
-    residual_out[...] = residual
+    residual_out[...] = residual.astype(BF)
     unit, _ = row_stats(residual)
     middle = (unit * middle_gain[...]).astype(BF)
     span = pl.ds(pl.multiple_of(step * ROWS, ROWS), ROWS)
@@ -271,7 +271,7 @@
     width = out_w.shape[0]
     ff = up_w.shape[1]
     span = pl.ds(pl.multiple_of(step * ROWS, ROWS), ROWS)
-    unit, scale = row_stats(residual[...])
+    unit, scale = row_stats(residual[...].astype(F32))
     middle_rows[span] = (unit * middle_gain[...]).astype(BF)
     grad_ff = grad_combined[...]
     for c in range(ff // width):
@@ -673,7 +673,7 @@
         [
             (BF, (parts * PART_ROWS, width), (FULL, width)),
             (BF, (tiles * PAIRS * TILE, 2 * TILE), (TILES * PAIRS, 2 * TILE)),
-            (F32, (total, width), (ROWS, width)),
+            (BF, (total, width), (ROWS, width)),
             (BF, (total, ff), (ROWS, ff)),
             (BF, (total, width), (ROWS, width)),
             (BF, (FRAMES, slots, width), slab),
@@ -686,7 +686,7 @@
         24,
     )
 
-    down = Sum(keep, send, 2)
+    down = Sum(keep, send, 0)
     down.start()
 
     grad_residual, grad_attended, keep, send, middle_part = call(
@@ -709,7 +709,7 @@
 
     down.land()
     down.values, grad_attended = lax.optimization_barrier((down.values, grad_attended))
-    up = Sum(keep, send, 0)
+    up = Sum(keep, send, 1)
     up.start()
     down.start()
 
@@ -737,7 +737,7 @@
         12,
     )
 
-    projections = Sum(keep, send, 0)
+    projections = Sum(keep, send, 2)
     sent = projections.start()
     carry_next = shift(first_carry, "seg", -1)
     down.land()

time: 181 us -> 181 us (level)
  waiting for transfers between devices: 22.8 us -> 16.7 us
  starting transfers between devices: 31.7 us -> 37.8 us
    ppermute x24, waiting for transfers between devices: 22.7 us -> 16.7 us  [swap(): return lax.ppermute(values, ('grp', 'seg'), pairs)]
    ppermute x24, starting transfers between devices: 23.2 us -> 29.2 us  [swap(): return lax.ppermute(values, ('grp', 'seg'), pairs)]
  transfers between devices with their start and end apart: 32 -> 32, of which waited for: 14 -> 12; matrix products, arithmetic and copies ran while one was open for 12% -> 12% of each run, Pallas kernels for 35% -> 35%
where the time goes in v5:
time: 181 us
  Pallas kernels  98.6 us (54%)
  starting transfers between devices  37.8 us (21%)
  local copies, waits for them, and re-layouts  17.3 us (10%)
  waiting for transfers between devices  16.7 us (9%)
  other arithmetic  9.04 us (5%)
    pallas_call x6, Pallas kernels, call(): pl.pallas_call(kernel, grid=(steps,), in_specs=[spec(array.shape, block)...  86.3 us
    ppermute x24, starting transfers between devices, swap(): return lax.ppermute(values, ('grp', 'seg'), pairs)  29.2 us
    ppermute x24, waiting for transfers between devices, swap(): return lax.ppermute(values, ('grp', 'seg'), pairs)  16.7 us
    pallas_call x3, Pallas kernels, finish(): pl.pallas_call(kernel, grid=(2 * halves,), in_specs=[pl.BlockSpec(memory_...  12.3 us
    ppermute x2, starting transfers between devices, shift(): lax.ppermute(values, axis, [(i, (i + by) % size) for i in range(size)])  7.56 us
    unnamed x26, local copies, waits for them, and re-layouts  6.11 us
    convert_element_type x12, other arithmetic, land(): (self.values.astype(F32) + other.astype(F32)).astype(self.values.dtype)  4.82 us
  transfers between devices with their start and end apart: 32, of which 12 were waited for; matrix products, arithmetic and copies ran while one was open for 12% of the time, Pallas kernels for 35%

profile of v5, /device:TPU:0, one launch (start us, length us, event | category | flops | bytes accessed | tf_op | source)
XLA Modules:
  0.0 180.6 jit_solution(3622540038514903411)
XLA Ops:
  2.3 3.0 %collective-permute-start = (bf16[21,8,512]{2,1,0:T(8,128)(2,1)S(1)}, bf16[21,8,512]{2,1,0:T(8,128)(2,1)S(1)}, u32[]{:S(2)}, u32[]{:S(2)}) collective-permute-start(bf16[21,8,512]{2,1,0:T(8,128)(2,1)S(1)} %pad_maximum_fusion.4), channel_id=1, source_target_pairs={{0,1},{1,2},{2,3},{3,4},{4,5},{5,6},{6,7},{7,8},{8,9},{9,10},{10,1... | collective-permute-start | bytes 516104 | tf_op jit(solution)/shard_map/ppermute | solution.py:429
  6.9 9.3 %project_kernel.1 = (bf16[1408,512]{1,0:T(8,128)(2,1)}, bf16[1792,512]{1,0:T(8,128)(2,1)}, bf16[2048,512]{1,0:T(8,128)(2,1)}, bf16[2048,1024]{1,0:T(8,128)(2,1)}) custom-call(bf16[20,64,512]{2,1,0:T(8,128)(2,1)} %bitcast.16, bf16[64,512]{1,0:T(8,128)(2,1)} %memory.1, f32[1,512]{1,0:T(1,128)} %bitcast.26, bf16[512,512]{1,0:T(8,128)(2,1)} %query_w.3, ...), custom_call_target="tpu_custom_call" | custom-call | flops 10000000000 | bytes 1000000 | tf_op jit(solution)/shard_map/project_kernel/pallas_call | solution.py:591
  17.3 3.1 %halo_kernel.1 = (bf16[1792,512]{1,0:T(8,128)(2,1)}, bf16[2048,1024]{1,0:T(8,128)(2,1)}) custom-call(bf16[21,8,512]{2,1,0:T(8,128)(2,1)} %copy-done.7, f32[1,512]{1,0:T(1,128)} %bitcast.27, bf16[512,512]{1,0:T(8,128)(2,1)} %key_w.5, bf16[512,512]{1,0:T(8,128)(2,1)} %value_w.5, ...), custom_call_target="tpu_custom_call", output_to_operand_aliasing={{0}: (6, {}), {1}: (7, {})} | custom-call | flops 2000000000 | bytes 200000 | tf_op jit(solution)/shard_map/halo_kernel/pallas_call | solution.py:591
  20.5 28.2 %forward_kernel.1 = (bf16[1408,512]{1,0:T(8,128)(2,1)}, bf16[8192,256]{1,0:T(8,128)(2,1)}, bf16[1280,512]{1,0:T(8,128)(2,1)}, bf16[1280,2048]{1,0:T(8,128)(2,1)}...) custom-call(s32[2]{0:T(128)} %pad_add_fusion.core.device_ref, ...), custom_call_target="tpu_custom_call" | custom-call | flops 24000000000 | bytes 2400000 | tf_op jit(solution)/shard_map/forward_kernel/pallas_call | solution.py:591
  48.7 17.9 %backward_kernel.1 = (bf16[1280,512]{1,0:T(8,128)(2,1)}, bf16[1408,512]{1,0:T(8,128)(2,1)}, bf16[256,2560]{1,0:T(8,128)(2,1)}, bf16[256,2560]{1,0:T(8,128)(2,1)}, f32[1,512]{1,0:T(1,128)}) custom-call(s32[2]{0:T(128)} %pad_add_fusion.core.device_ref, bf16[1280,2048]{1,0:T(8,128)(2,1)} %get-tuple-element.115.slope, ...), custom_call_target="tpu_custom_call" | custom-call | flops 16000000000 | bytes 1600000 | tf_op jit(solution)/shard_map/backward_kernel/pallas_call | solution.py:591
  68.3 1.5 collective-permute-start.2
  69.8 19.1 %attention_back_kernel.1 = (bf16[1408,512]{1,0:T(8,128)(2,1)}, bf16[1408,1024]{1,0:T(8,128)(2,1)}, bf16[384,1024]{1,0:T(8,128)(2,1)}, bf16[48,1024]{1,0:T(8,128)...) custom-call(s32[2]{0:T(128)} %pad_add_fusion.core.device_ref, bf16[256,176]{1,0:T(8,128)(2,1)} %constant.195.clone.pick_query, ...), custom_call_target="tpu_custom_call" | custom-call | flops 12000000000 | bytes 1200000 | tf_op jit(solution)/shard_map/attention_back_kernel/pallas_call | solution.py:591
  89.0 4.6 %collective-permute-start.5 = (bf16[48,1024]{1,0:T(8,128)(2,1)}, bf16[48,1024]{1,0:T(8,128)(2,1)S(1)}, u32[]{:S(2)}, u32[]{:S(2)}) collective-permute-start(bf16[48,1024]{1,0:T(8,128)(2,1)} %get-tuple-element.139), channel_id=1, source_target_pairs={{0,15},{1,0},{2,1},{3,2},{4,3},{5,4},{6,5},{7,6},{8,7},{9,8},{10,9... | collective-permute-start | bytes 294920 | tf_op jit(solution)/shard_map/ppermute | solution.py:429
  93.6 1.6 add_convert_fusion
  95.2 1.2 add_convert_fusion.4
  97.3 2.1 %collective-permute-start.7 = (bf16[256,512]{1,0:T(8,128)(2,1)S(1)}, bf16[256,512]{1,0:T(8,128)(2,1)}, u32[]{:S(2)}, u32[]{:S(2)}) collective-permute-start(bf16[256,512]{1,0:T(8,128)(2,1)S(1)} %constant_dynamic-slice_fusion.10), channel_id=1, source_target_pairs={{0,2},{1,3},{2,0},{3,1},{4,6},{5,7},{6,4},{7,5},{8,10},{9,11},{10,... | collective-permute-start | bytes 786440 | tf_op jit(solution)/shard_map/ppermute | solution.py:459
  101.1 8.7 %projection_back_kernel.1 = (f32[20,64,512]{2,1,0:T(8,128)}, bf16[64,512]{1,0:T(8,128)(2,1)}, f32[1,512]{1,0:T(1,128)}) custom-call(bf16[176,48]{1,0:T(8,128)(2,1)} %constant.193.clone.unpick_carry, bf16[1408,1024]{1,0:T(8,128)(2,1)} %get-tuple-element.137.grad_pair, bf16[384,1024]{1,0:T(8,128)(2,1)} %get-tuple-element.138.grad_carry, ...), custom_call_target="tpu_custom_call" | custom-call | flops 8000000000 | bytes 800000 | tf_op jit(solution)/shard_map/projection_back_kernel/pallas_call | solution.py:591
  110.8 2.1 %collective-permute-start.11 = (bf16[64,2560]{1,0:T(8,128)(2,1)S(1)}, bf16[64,2560]{1,0:T(8,128)(2,1)S(1)}, u32[]{:S(2)}, u32[]{:S(2)}) collective-permute-start(bf16[64,2560]{1,0:T(8,128)(2,1)S(1)} %constant_dynamic-slice_fusion.7), channel_id=1, source_target_pairs={{0,4},{1,5},{2,6},{3,7},{4,0},{5,1},{6,2},{7,3},{8,12},{9,13},{10,... | collective-permute-start | bytes 983048 | tf_op jit(solution)/shard_map/ppermute | solution.py:459
  114.2 3.7 %collective-permute-done.11 = bf16[64,2560]{1,0:T(8,128)(2,1)S(1)} collective-permute-done((bf16[64,2560]{1,0:T(8,128)(2,1)S(1)}, bf16[64,2560]{1,0:T(8,128)(2,1)S(1)}, u32[]{:S(2)}, u32[]{:S(2)}) %collective-permute-start.11) | collective-permute-done | bytes 327712 | tf_op jit(solution)/shard_map/ppermute | solution.py:459
  118.1 1.2 collective-permute-done.10
  121.4 2.0 %collective-permute-done.14 = bf16[32,2560]{1,0:T(8,128)(2,1)S(1)} collective-permute-done((bf16[32,2560]{1,0:T(8,128)(2,1)S(1)}, bf16[32,2560]{1,0:T(8,128)(2,1)S(1)}, u32[]{:S(2)}, u32[]{:S(2)}) %collective-permute-start.14) | collective-permute-done | bytes 163872 | tf_op jit(solution)/shard_map/ppermute | solution.py:459
  125.5 1.6 collective-permute-start.16
  127.2 1.4 collective-permute-start.15
  129.5 1.3 collective-permute-start.20
  130.8 2.4 %collective-permute-done.16 = bf16[64,512]{1,0:T(8,128)(2,1)S(1)} collective-permute-done((bf16[64,512]{1,0:T(8,128)(2,1)S(1)}, bf16[64,512]{1,0:T(8,128)(2,1)S(1)}, u32[]{:S(2)}, u32[]{:S(2)}) %collective-permute-start.16) | collective-permute-done | bytes 65568 | tf_op jit(solution)/shard_map/ppermute | solution.py:459
  133.3 2.6 %collective-permute-start.19 = (bf16[128,512]{1,0:T(8,128)(2,1)S(1)}, bf16[128,512]{1,0:T(8,128)(2,1)S(1)}, u32[]{:S(2)}, u32[]{:S(2)}) collective-permute-start(bf16[128,512]{1,0:T(8,128)(2,1)S(1)} %pad_maximum_fusion.6), channel_id=1, source_target_pairs={{0,4},{1,5},{2,6},{3,7},{4,0},{5,1},{6,2},{7,3},{8,12},{9,13},{10,... | collective-permute-start | bytes 393224 | tf_op jit(solution)/shard_map/ppermute | solution.py:459
  136.5 2.6 %collective-permute-start.18 = (bf16[24,1536]{1,0:T(8,128)(2,1)S(1)}, bf16[24,1536]{1,0:T(8,128)(2,1)S(1)}, u32[]{:S(2)}, u32[]{:S(2)}) collective-permute-start(bf16[24,1536]{1,0:T(8,128)(2,1)S(1)} %pad_maximum_fusion.7), channel_id=1, source_target_pairs={{0,8},{1,9},{2,10},{3,11},{4,12},{5,13},{6,14},{7,15},{8,0},{9,1},... | collective-permute-start | bytes 221192 | tf_op jit(solution)/shard_map/ppermute | solution.py:459
  140.5 1.7 collective-permute-start.22
  147.0 2.2 %collective-permute-start.25 = (bf16[512,512]{1,0:T(8,128)(2,1)S(1)}, bf16[512,512]{1,0:T(8,128)(2,1)}, u32[]{:S(2)}, u32[]{:S(2)}) collective-permute-start(bf16[512,512]{1,0:T(8,128)(2,1)S(1)} %pad_maximum_fusion.1), channel_id=1, source_target_pairs={{0,1},{1,0},{2,3},{3,2},{4,5},{5,4},{6,7},{7,6},{8,9},{9,8},{10,11... | collective-permute-start | bytes 1572872 | tf_op jit(solution)/shard_map/ppermute | solution.py:459
  150.4 2.1 %collective-permute-start.24 = (bf16[72,1536]{1,0:T(8,128)(2,1)S(1)}, bf16[72,1536]{1,0:T(8,128)(2,1)S(1)}, u32[]{:S(2)}, u32[]{:S(2)}) collective-permute-start(bf16[72,1536]{1,0:T(8,128)(2,1)S(1)} %concatenate.101), channel_id=1, source_target_pairs={{0,1},{1,0},{2,3},{3,2},{4,5},{5,4},{6,7},{7,6},{8,9},{9,8},{10,11... | collective-permute-start | bytes 663560 | tf_op jit(solution)/shard_map/ppermute | solution.py:459
  154.0 2.5 %collective-permute-start.28 = (bf16[128,2560]{1,0:T(8,128)(2,1)S(1)}, bf16[128,2560]{1,0:T(8,128)(2,1)S(1)}, u32[]{:S(2)}, u32[]{:S(2)}) collective-permute-start(bf16[128,2560]{1,0:T(8,128)(2,1)S(1)} %pad_maximum_fusion), channel_id=1, source_target_pairs={{0,2},{1,3},{2,0},{3,1},{4,6},{5,7},{6,4},{7,5},{8,10},{9,11},{10,... | collective-permute-start | bytes 1966088 | tf_op jit(solution)/shard_map/ppermute | solution.py:459
  156.5 1.9 %constant_dynamic-update-slice_fusion.3.own_ref = bf16[1024,512]{1,0:T(8,128)(2,1)} fusion(bf16[1024,512]{1,0:T(8,128)(2,1)} %constant_dynamic-update-slice_fusion.4, bf16[512,512]{1,0:T(8,128)(2,1)} %collective-permute-done.25), kind=kLoop, calls=%fused_computation.26 | loop fusion | bytes 1048576 | tf_op jit(solution)/shard_map/concatenate | solution.py:512
  159.5 1.5 collective-permute-start.27
  161.0 4.0 %collective-permute-done.28 = bf16[128,2560]{1,0:T(8,128)(2,1)S(1)} collective-permute-done((bf16[128,2560]{1,0:T(8,128)(2,1)S(1)}, bf16[128,2560]{1,0:T(8,128)(2,1)S(1)}, u32[]{:S(2)}, u32[]{:S(2)}) %collective-permute-start.28) | collective-permute-done | bytes 655392 | tf_op jit(solution)/shard_map/ppermute | solution.py:459
  165.9 4.2 %finish.3 = f32[2048,512]{1,0:T(8,128)} custom-call(s32[2]{0:T(128)} %pad_add_fusion.core.device_ref, bf16[1024,512]{1,0:T(8,128)(2,1)} %constant_dynamic-update-slice_fusion.3.own_ref, bf16[1024,512]{1,0:T(8,128)(2,1)} %collective-permute-done.29.other_ref), custom_call_target="tpu_custom_call" | custom-call | flops 3000000000 | bytes 300000 | tf_op jit(solution)/shard_map/finish/pallas_call | solution.py:569
  170.9 4.5 %finish.4 = (f32[512,2048]{1,0:T(8,128)}, f32[512,512]{1,0:T(8,128)}) custom-call(s32[2]{0:T(128)} %pad_add_fusion.core.device_ref, bf16[256,2560]{1,0:T(8,128)(2,1)} %constant_dynamic-update-slice_fusion.8.own_ref, bf16[256,2560]{1,0:T(8,128)(2,1)} %collective-permute-done.31.other_ref), custom_call_target="tpu_custom_call" | custom-call | flops 3000000000 | bytes 300000 | tf_op jit(solution)/shard_map/finish/pallas_call | solution.py:569
  177.0 3.6 %finish.5 = (f32[512,512]{1,0:T(8,128)}, f32[512,512]{1,0:T(8,128)}, f32[512,512]{1,0:T(8,128)}) custom-call(s32[2]{0:T(128)} %pad_add_fusion.core.device_ref, bf16[256,1536]{1,0:T(8,128)(2,1)} %copy-done.4, bf16[256,1536]{1,0:T(8,128)(2,1)} %slice.77.other_ref), custom_call_target="tpu_custom_call" | custom-call | flops 3000000000 | bytes 300000 | tf_op jit(solution)/shard_map/finish/pallas_call | solution.py:569
  (133 shorter events, 30.2 us)
Async XLA Ops:
  2.3 14.4 %collective-permute-start = (bf16[21,8,512]{2,1,0:T(8,128)(2,1)S(1)}, bf16[21,8,512]{2,1,0:T(8,128)(2,1)S(1)}, u32[]{:S(2)}, u32[]{:S(2)}) collective-permute-start(bf16[21,8,512]{2,1,0:T(8,128)(2,1)S(1)} %pad_maximum_fusion.4), channel_id=1, source_target_pairs={{0,1},{1,2},{2,3},{3,4},{4,5},{5,6},{6,7},{7,8},{8,9},{9,10},{10,1... | collective-permute-start | bytes 516104 | tf_op jit(solution)/shard_map/ppermute | solution.py:429
  48.6 18.6 %collective-permute-start.1 = (bf16[1024,512]{1,0:T(8,128)(2,1)}, bf16[1024,512]{1,0:T(8,128)(2,1)S(1)}, u32[]{:S(2)}, u32[]{:S(2)}) collective-permute-start(bf16[1024,512]{1,0:T(8,128)(2,1)} %get-tuple-element.114), channel_id=1, source_target_pairs={{0,16},{16,0},{1,17},{17,1},{2,18},{18,2},{3,19},{19,3},{4,20},{20... | collective-permute-start | bytes 3145736 | tf_op jit(solution)/shard_map/ppermute | solution.py:456
  66.7 26.9 %collective-permute-start.3 = (bf16[256,2560]{1,0:T(8,128)(2,1)}, bf16[256,2560]{1,0:T(8,128)(2,1)}, u32[]{:S(2)}, u32[]{:S(2)}) collective-permute-start(bf16[256,2560]{1,0:T(8,128)(2,1)} %get-tuple-element.122), channel_id=1, source_target_pairs={{0,16},{16,0},{1,17},{17,1},{2,18},{18,2},{3,19},{19,3},{4,20},{20... | collective-permute-start | bytes 3932168 | tf_op jit(solution)/shard_map/ppermute | solution.py:456
  68.3 26.9 %collective-permute-start.2 = (bf16[512,512]{1,0:T(8,128)(2,1)}, bf16[512,512]{1,0:T(8,128)(2,1)}, u32[]{:S(2)}, u32[]{:S(2)}) collective-permute-start(bf16[512,512]{1,0:T(8,128)(2,1)} %constant_dynamic-slice_fusion.11), channel_id=1, source_target_pairs={{0,1},{1,0},{2,3},{3,2},{4,5},{5,4},{6,7},{7,6},{8,9},{9,8},{10,11... | collective-permute-start | bytes 1572872 | tf_op jit(solution)/shard_map/ppermute | solution.py:459
  88.9 10.5 %collective-permute-start.4 = (bf16[256,1536]{1,0:T(8,128)(2,1)}, bf16[256,1536]{1,0:T(8,128)(2,1)S(1)}, u32[]{:S(2)}, u32[]{:S(2)}) collective-permute-start(bf16[256,1536]{1,0:T(8,128)(2,1)} %get-tuple-element.130), channel_id=1, source_target_pairs={{0,16},{16,0},{1,17},{17,1},{2,18},{18,2},{3,19},{19,3},{4,20},{20... | collective-permute-start | bytes 2359304 | tf_op jit(solution)/shard_map/ppermute | solution.py:456
  89.0 11.4 %collective-permute-start.5 = (bf16[48,1024]{1,0:T(8,128)(2,1)}, bf16[48,1024]{1,0:T(8,128)(2,1)S(1)}, u32[]{:S(2)}, u32[]{:S(2)}) collective-permute-start(bf16[48,1024]{1,0:T(8,128)(2,1)} %get-tuple-element.139), channel_id=1, source_target_pairs={{0,15},{1,0},{2,1},{3,2},{4,3},{5,4},{6,5},{7,6},{8,7},{9,8},{10,9... | collective-permute-start | bytes 294920 | tf_op jit(solution)/shard_map/ppermute | solution.py:429
  97.3 13.2 %collective-permute-start.8 = (bf16[128,2560]{1,0:T(8,128)(2,1)}, bf16[128,2560]{1,0:T(8,128)(2,1)S(1)}, u32[]{:S(2)}, u32[]{:S(2)}) collective-permute-start(bf16[128,2560]{1,0:T(8,128)(2,1)} %constant_dynamic-slice_fusion.9), channel_id=1, source_target_pairs={{0,2},{1,3},{2,0},{3,1},{4,6},{5,7},{6,4},{7,5},{8,10},{9,11},{10,... | collective-permute-start | bytes 1966088 | tf_op jit(solution)/shard_map/ppermute | solution.py:459
  97.3 15.5 %collective-permute-start.7 = (bf16[256,512]{1,0:T(8,128)(2,1)S(1)}, bf16[256,512]{1,0:T(8,128)(2,1)}, u32[]{:S(2)}, u32[]{:S(2)}) collective-permute-start(bf16[256,512]{1,0:T(8,128)(2,1)S(1)} %constant_dynamic-slice_fusion.10), channel_id=1, source_target_pairs={{0,2},{1,3},{2,0},{3,1},{4,6},{5,7},{6,4},{7,5},{8,10},{9,11},{10,... | collective-permute-start | bytes 786440 | tf_op jit(solution)/shard_map/ppermute | solution.py:459
  100.4 13.6 %collective-permute-start.6 = (bf16[128,1536]{1,0:T(8,128)(2,1)}, bf16[128,1536]{1,0:T(8,128)(2,1)S(1)}, u32[]{:S(2)}, u32[]{:S(2)}) collective-permute-start(bf16[128,1536]{1,0:T(8,128)(2,1)} %constant_dynamic-slice_fusion.8), channel_id=1, source_target_pairs={{0,4},{1,5},{2,6},{3,7},{4,0},{5,1},{6,2},{7,3},{8,12},{9,13},{10,... | collective-permute-start | bytes 1179656 | tf_op jit(solution)/shard_map/ppermute | solution.py:459
  110.8 7.1 %collective-permute-start.11 = (bf16[64,2560]{1,0:T(8,128)(2,1)S(1)}, bf16[64,2560]{1,0:T(8,128)(2,1)S(1)}, u32[]{:S(2)}, u32[]{:S(2)}) collective-permute-start(bf16[64,2560]{1,0:T(8,128)(2,1)S(1)} %constant_dynamic-slice_fusion.7), channel_id=1, source_target_pairs={{0,4},{1,5},{2,6},{3,7},{4,0},{5,1},{6,2},{7,3},{8,12},{9,13},{10,... | collective-permute-start | bytes 983048 | tf_op jit(solution)/shard_map/ppermute | solution.py:459
  113.9 5.4 %collective-permute-start.10 = (bf16[128,512]{1,0:T(8,128)(2,1)S(1)}, bf16[128,512]{1,0:T(8,128)(2,1)S(1)}, u32[]{:S(2)}, u32[]{:S(2)}) collective-permute-start(bf16[128,512]{1,0:T(8,128)(2,1)S(1)} %constant_dynamic-slice_fusion.6), channel_id=1, source_target_pairs={{0,4},{1,5},{2,6},{3,7},{4,0},{5,1},{6,2},{7,3},{8,12},{9,13},{10,... | collective-permute-start | bytes 393224 | tf_op jit(solution)/shard_map/ppermute | solution.py:459
  114.1 7.1 %collective-permute-start.9 = (bf16[64,1536]{1,0:T(8,128)(2,1)S(1)}, bf16[64,1536]{1,0:T(8,128)(2,1)S(1)}, u32[]{:S(2)}, u32[]{:S(2)}) collective-permute-start(bf16[64,1536]{1,0:T(8,128)(2,1)S(1)} %constant_dynamic-slice_fusion.5), channel_id=1, source_target_pairs={{0,1},{1,0},{2,3},{3,2},{4,5},{5,4},{6,7},{7,6},{8,9},{9,8},{10,11... | collective-permute-start | bytes 589832 | tf_op jit(solution)/shard_map/ppermute | solution.py:459
  118.0 5.4 %collective-permute-start.14 = (bf16[32,2560]{1,0:T(8,128)(2,1)S(1)}, bf16[32,2560]{1,0:T(8,128)(2,1)S(1)}, u32[]{:S(2)}, u32[]{:S(2)}) collective-permute-start(bf16[32,2560]{1,0:T(8,128)(2,1)S(1)} %constant_dynamic-slice_fusion.4), channel_id=1, source_target_pairs={{0,1},{1,0},{2,3},{3,2},{4,5},{5,4},{6,7},{7,6},{8,9},{9,8},{10,11... | collective-permute-start | bytes 491528 | tf_op jit(solution)/shard_map/ppermute | solution.py:459
  119.4 5.5 %collective-permute-start.13 = (bf16[64,512]{1,0:T(8,128)(2,1)S(1)}, bf16[64,512]{1,0:T(8,128)(2,1)S(1)}, u32[]{:S(2)}, u32[]{:S(2)}) collective-permute-start(bf16[64,512]{1,0:T(8,128)(2,1)S(1)} %constant_dynamic-slice_fusion.3), channel_id=1, source_target_pairs={{0,8},{1,9},{2,10},{3,11},{4,12},{5,13},{6,14},{7,15},{8,0},{9,1},... | collective-permute-start | bytes 196616 | tf_op jit(solution)/shard_map/ppermute | solution.py:459
  121.3 5.8 %collective-permute-start.12 = (bf16[32,1536]{1,0:T(8,128)(2,1)S(1)}, bf16[32,1536]{1,0:T(8,128)(2,1)S(1)}, u32[]{:S(2)}, u32[]{:S(2)}) collective-permute-start(bf16[32,1536]{1,0:T(8,128)(2,1)S(1)} %constant_dynamic-slice_fusion.2), channel_id=1, source_target_pairs={{0,2},{1,3},{2,0},{3,1},{4,6},{5,7},{6,4},{7,5},{8,10},{9,11},{10,... | collective-permute-start | bytes 294920 | tf_op jit(solution)/shard_map/ppermute | solution.py:459
  123.5 5.4 %collective-permute-start.17 = (bf16[16,2560]{1,0:T(8,128)(2,1)S(1)}, bf16[16,2560]{1,0:T(8,128)(2,1)S(1)}, u32[]{:S(2)}, u32[]{:S(2)}) collective-permute-start(bf16[16,2560]{1,0:T(8,128)(2,1)S(1)} %constant_dynamic-slice_fusion.1), channel_id=1, source_target_pairs={{0,8},{1,9},{2,10},{3,11},{4,12},{5,13},{6,14},{7,15},{8,0},{9,1},... | collective-permute-start | bytes 245768 | tf_op jit(solution)/shard_map/ppermute | solution.py:459
  125.5 7.7 %collective-permute-start.16 = (bf16[64,512]{1,0:T(8,128)(2,1)S(1)}, bf16[64,512]{1,0:T(8,128)(2,1)S(1)}, u32[]{:S(2)}, u32[]{:S(2)}) collective-permute-start(bf16[64,512]{1,0:T(8,128)(2,1)S(1)} %get-tuple-element.159), channel_id=1, source_target_pairs={{0,8},{1,9},{2,10},{3,11},{4,12},{5,13},{6,14},{7,15},{8,0},{9,1},... | collective-permute-start | bytes 196616 | tf_op jit(solution)/shard_map/ppermute | solution.py:459
  127.2 8.7 %collective-permute-start.15 = (bf16[16,1536]{1,0:T(8,128)(2,1)S(1)}, bf16[16,1536]{1,0:T(8,128)(2,1)S(1)}, u32[]{:S(2)}, u32[]{:S(2)}) collective-permute-start(bf16[16,1536]{1,0:T(8,128)(2,1)S(1)} %constant_dynamic-slice_fusion), channel_id=1, source_target_pairs={{0,8},{1,9},{2,10},{3,11},{4,12},{5,13},{6,14},{7,15},{8,0},{9,1},... | collective-permute-start | bytes 147464 | tf_op jit(solution)/shard_map/ppermute | solution.py:459
  129.5 10.2 %collective-permute-start.20 = (bf16[16,2560]{1,0:T(8,128)(2,1)S(1)}, bf16[16,2560]{1,0:T(8,128)(2,1)S(1)}, u32[]{:S(2)}, u32[]{:S(2)}) collective-permute-start(bf16[16,2560]{1,0:T(8,128)(2,1)S(1)} %get-tuple-element.163), channel_id=1, source_target_pairs={{0,8},{1,9},{2,10},{3,11},{4,12},{5,13},{6,14},{7,15},{8,0},{9,1},... | collective-permute-start | bytes 245768 | tf_op jit(solution)/shard_map/ppermute | solution.py:459
  133.3 7.2 %collective-permute-start.19 = (bf16[128,512]{1,0:T(8,128)(2,1)S(1)}, bf16[128,512]{1,0:T(8,128)(2,1)S(1)}, u32[]{:S(2)}, u32[]{:S(2)}) collective-permute-start(bf16[128,512]{1,0:T(8,128)(2,1)S(1)} %pad_maximum_fusion.6), channel_id=1, source_target_pairs={{0,4},{1,5},{2,6},{3,7},{4,0},{5,1},{6,2},{7,3},{8,12},{9,13},{10,... | collective-permute-start | bytes 393224 | tf_op jit(solution)/shard_map/ppermute | solution.py:459
  136.5 6.7 %collective-permute-start.18 = (bf16[24,1536]{1,0:T(8,128)(2,1)S(1)}, bf16[24,1536]{1,0:T(8,128)(2,1)S(1)}, u32[]{:S(2)}, u32[]{:S(2)}) collective-permute-start(bf16[24,1536]{1,0:T(8,128)(2,1)S(1)} %pad_maximum_fusion.7), channel_id=1, source_target_pairs={{0,8},{1,9},{2,10},{3,11},{4,12},{5,13},{6,14},{7,15},{8,0},{9,1},... | collective-permute-start | bytes 221192 | tf_op jit(solution)/shard_map/ppermute | solution.py:459
  139.7 5.6 %collective-permute-start.23 = (bf16[32,2560]{1,0:T(8,128)(2,1)S(1)}, bf16[32,2560]{1,0:T(8,128)(2,1)S(1)}, u32[]{:S(2)}, u32[]{:S(2)}) collective-permute-start(bf16[32,2560]{1,0:T(8,128)(2,1)S(1)} %pad_maximum_fusion.5), channel_id=1, source_target_pairs={{0,1},{1,0},{2,3},{3,2},{4,5},{5,4},{6,7},{7,6},{8,9},{9,8},{10,11... | collective-permute-start | bytes 491528 | tf_op jit(solution)/shard_map/ppermute | solution.py:459
  140.5 6.4 %collective-permute-start.22 = (bf16[256,512]{1,0:T(8,128)(2,1)S(1)}, bf16[256,512]{1,0:T(8,128)(2,1)S(1)}, u32[]{:S(2)}, u32[]{:S(2)}) collective-permute-start(bf16[256,512]{1,0:T(8,128)(2,1)S(1)} %pad_maximum_fusion.3), channel_id=1, source_target_pairs={{0,2},{1,3},{2,0},{3,1},{4,6},{5,7},{6,4},{7,5},{8,10},{9,11},{10,... | collective-permute-start | bytes 786440 | tf_op jit(solution)/shard_map/ppermute | solution.py:459
  143.9 5.7 %collective-permute-start.21 = (bf16[40,1536]{1,0:T(8,128)(2,1)S(1)}, bf16[40,1536]{1,0:T(8,128)(2,1)S(1)}, u32[]{:S(2)}, u32[]{:S(2)}) collective-permute-start(bf16[40,1536]{1,0:T(8,128)(2,1)S(1)} %concatenate.98), channel_id=1, source_target_pairs={{0,2},{1,3},{2,0},{3,1},{4,6},{5,7},{6,4},{7,5},{8,10},{9,11},{10,... | collective-permute-start | bytes 368648 | tf_op jit(solution)/shard_map/ppermute | solution.py:459
  145.4 7.8 %collective-permute-start.26 = (bf16[64,2560]{1,0:T(8,128)(2,1)S(1)}, bf16[64,2560]{1,0:T(8,128)(2,1)S(1)}, u32[]{:S(2)}, u32[]{:S(2)}) collective-permute-start(bf16[64,2560]{1,0:T(8,128)(2,1)S(1)} %pad_maximum_fusion.2), channel_id=1, source_target_pairs={{0,4},{1,5},{2,6},{3,7},{4,0},{5,1},{6,2},{7,3},{8,12},{9,13},{10,... | collective-permute-start | bytes 983048 | tf_op jit(solution)/shard_map/ppermute | solution.py:459
  147.0 9.5 %collective-permute-start.25 = (bf16[512,512]{1,0:T(8,128)(2,1)S(1)}, bf16[512,512]{1,0:T(8,128)(2,1)}, u32[]{:S(2)}, u32[]{:S(2)}) collective-permute-start(bf16[512,512]{1,0:T(8,128)(2,1)S(1)} %pad_maximum_fusion.1), channel_id=1, source_target_pairs={{0,1},{1,0},{2,3},{3,2},{4,5},{5,4},{6,7},{7,6},{8,9},{9,8},{10,11... | collective-permute-start | bytes 1572872 | tf_op jit(solution)/shard_map/ppermute | solution.py:459
  150.4 8.3 %collective-permute-start.24 = (bf16[72,1536]{1,0:T(8,128)(2,1)S(1)}, bf16[72,1536]{1,0:T(8,128)(2,1)S(1)}, u32[]{:S(2)}, u32[]{:S(2)}) collective-permute-start(bf16[72,1536]{1,0:T(8,128)(2,1)S(1)} %concatenate.101), channel_id=1, source_target_pairs={{0,1},{1,0},{2,3},{3,2},{4,5},{5,4},{6,7},{7,6},{8,9},{9,8},{10,11... | collective-permute-start | bytes 663560 | tf_op jit(solution)/shard_map/ppermute | solution.py:459
  154.0 11.0 %collective-permute-start.28 = (bf16[128,2560]{1,0:T(8,128)(2,1)S(1)}, bf16[128,2560]{1,0:T(8,128)(2,1)S(1)}, u32[]{:S(2)}, u32[]{:S(2)}) collective-permute-start(bf16[128,2560]{1,0:T(8,128)(2,1)S(1)} %pad_maximum_fusion), channel_id=1, source_target_pairs={{0,2},{1,3},{2,0},{3,1},{4,6},{5,7},{6,4},{7,5},{8,10},{9,11},{10,... | collective-permute-start | bytes 1966088 | tf_op jit(solution)/shard_map/ppermute | solution.py:459
  158.3 7.6 %collective-permute-start.29 = (bf16[1024,512]{1,0:T(8,128)(2,1)}, bf16[1024,512]{1,0:T(8,128)(2,1)}, u32[]{:S(2)}, u32[]{:S(2)}) collective-permute-start(bf16[1024,512]{1,0:T(8,128)(2,1)} %constant_dynamic-update-slice_fusion.3.own_ref), channel_id=1, source_target_pairs={{0,16},{16,0},{1,17},{17,1},{2,18},{18,2},{3,19},{19,3},{4,20},{20... | collective-permute-start | bytes 3145736 | tf_op jit(solution)/shard_map/ppermute | solution.py:456
  159.5 10.6 %collective-permute-start.27 = (bf16[136,1536]{1,0:T(8,128)(2,1)S(1)}, bf16[136,1536]{1,0:T(8,128)(2,1)S(1)}, u32[]{:S(2)}, u32[]{:S(2)}) collective-permute-start(bf16[136,1536]{1,0:T(8,128)(2,1)S(1)} %concatenate.104), channel_id=1, source_target_pairs={{0,4},{1,5},{2,6},{3,7},{4,0},{5,1},{6,2},{7,3},{8,12},{9,13},{10,... | collective-permute-start | bytes 1253384 | tf_op jit(solution)/shard_map/ppermute | solution.py:459
  165.9 5.0 %collective-permute-start.31 = (bf16[256,2560]{1,0:T(8,128)(2,1)}, bf16[256,2560]{1,0:T(8,128)(2,1)}, u32[]{:S(2)}, u32[]{:S(2)}) collective-permute-start(bf16[256,2560]{1,0:T(8,128)(2,1)} %constant_dynamic-update-slice_fusion.8.own_ref), channel_id=1, source_target_pairs={{0,16},{16,0},{1,17},{17,1},{2,18},{18,2},{3,19},{19,3},{4,20},{20... | collective-permute-start | bytes 3932168 | tf_op jit(solution)/shard_map/ppermute | solution.py:456
  170.5 5.0 %collective-permute-start.30 = (bf16[264,1536]{1,0:T(8,128)(2,1)S(1)}, bf16[264,1536]{1,0:T(8,128)(2,1)S(1)}, u32[]{:S(2)}, u32[]{:S(2)}) collective-permute-start(bf16[264,1536]{1,0:T(8,128)(2,1)S(1)} %concatenate.107), channel_id=1, source_target_pairs={{0,16},{16,0},{1,17},{17,1},{2,18},{18,2},{3,19},{19,3},{4,20},{20... | collective-permute-start | bytes 2433032 | tf_op jit(solution)/shard_map/ppermute | solution.py:456
  (9 other events, 74.9 us)
